TPU v7x, 128 devices: a whole 4x4x4 slice. The times are simulated.
128 devices in a mesh: pp: 2 (over core), ep: 16 (over y, x), dp: 4 (over z).
Axes of the slice: x: 4, y: 4, z: 4, core: 2. Of those that a mesh axis runs over, the one named last changes fastest.
Arguments:
- tokens: bfloat16 [4096, 3072], P('ep'), may hold values from -6 to 6
- norm_gain: float32 [3072], replicated, may hold values from 0.25 to 1.75
- router_weight: bfloat16 [3072, 16], replicated, may hold values from -0.109375 to 0.109375
- expert_ids: int32 [4096, 4], P('ep'), may hold values from 0 to 15, all different within a row; in each aligned block of 256 rows (0 to 255, 256 to 511, ...) at most 72 rows name the same one
- up_weight: bfloat16 [16, 3072, 6144], P('ep', None, ('pp', 'dp')), may hold values from -0.109375 to 0.109375
- down_weight: bfloat16 [16, 6144, 3072], P('ep', ('pp', 'dp')), may hold values from -0.078125 to 0.078125
Outputs:
- mixed: bfloat16 [4096, 3072], P('ep')
Inputs may be any that keep to these rules, and one draw needn't show every extreme that they name: `expert_ids`: each row names 4 different experts. In each aligned block of 256 rows (the rows of one index of ep) no expert is named by more than 72 rows, a bound that some block reaches.
All inputs are finite; a program needn't handle non-finite values.
Results may differ from a plain program's by a relative error of at most 0.0085.
Values may be sent and summed in bfloat16 or wider, within the bound.
No kernel may reach another device: no remote copies, remote signals or barrier semaphores. Data moves between devices by JAX's collectives and lax.ppermute only.
A program may use at most 576 MiB of HBM per device.

v0:
```python
import jax
import jax.numpy as jnp
from jax import lax
from jax.sharding import PartitionSpec as P

D = 3072
EXPERTS = 16
TOP = 4
TOK_DEV = 256
CAP = 72


EPSILON = 1e-05


def layer_norm(values_in, gain_row):
    values = values_in.astype(jnp.float32)
    center = jnp.mean(values, axis=-1, keepdims=True)
    shifted = values - center
    spread = jnp.mean(shifted * shifted, axis=-1, keepdims=True)
    return (shifted / jnp.sqrt(spread + EPSILON) * gain_row).astype(jnp.bfloat16)


def slot_plan(chosen_ids):
    flat_ids = chosen_ids.reshape(-1)
    onehot = (flat_ids[:, None] == jnp.arange(EXPERTS, dtype=jnp.int32)[None, :]).astype(jnp.int32)
    before = jnp.cumsum(onehot, axis=0) - onehot
    return flat_ids * CAP + jnp.sum(before * onehot, axis=1)


def gate_rows(normed, route_matrix, chosen_ids):
    logits = jnp.dot(normed, route_matrix, preferred_element_type=jnp.float32)
    weights = jnp.exp(jnp.take_along_axis(logits, chosen_ids, axis=1))
    return weights / jnp.sum(weights, axis=1, keepdims=True)


def expert_rows(received, up_matrix, down_matrix):
    groups, local_count, slot_cap, width = received.shape
    up_proj = jnp.einsum("gscd,sdf->sgcf", received, up_matrix, preferred_element_type=jnp.float32)
    total_rows = local_count * groups * slot_cap
    hidden = jax.nn.silu(up_proj).astype(jnp.bfloat16).reshape(total_rows, up_matrix.shape[2])
    owner = jnp.arange(total_rows, dtype=jnp.int32) // (groups * slot_cap)
    term = jnp.dot(hidden, down_matrix[0], preferred_element_type=jnp.float32)
    total = jnp.where((owner == 0)[:, None], term, 0.0)
    whole = lax.psum(total, ("pp", "dp")).astype(jnp.bfloat16)
    return jnp.transpose(whole.reshape(local_count, groups, slot_cap, width), (1, 0, 2, 3))


def on_device(tokens, norm_gain, router_weight, expert_ids, up_weight, down_weight):
    normed = layer_norm(tokens, norm_gain)
    groups = lax.axis_size("ep")
    local_count = up_weight.shape[0]
    token_of = jnp.arange(TOK_DEV * TOP, dtype=jnp.int32) // TOP
    gate_values = gate_rows(normed, router_weight, expert_ids)
    slot_index = slot_plan(expert_ids)
    buffer = jnp.zeros((EXPERTS * CAP, D), jnp.bfloat16).at[slot_index].set(normed[token_of])
    outgoing = buffer.reshape(groups, local_count, CAP, D)
    received = lax.all_to_all(outgoing, "ep", split_axis=0, concat_axis=0, tiled=True)
    answered = expert_rows(received, up_weight, down_weight)
    returned = lax.all_to_all(answered, "ep", split_axis=0, concat_axis=0, tiled=True)
    picked = returned.reshape(EXPERTS * CAP, D)[slot_index].reshape(TOK_DEV, TOP, D)
    mixed_out = jnp.sum(gate_values[:, :, None] * picked.astype(jnp.float32), axis=1)
    return (tokens.astype(jnp.float32) + mixed_out).astype(jnp.bfloat16)


def solution(mesh):
    in_specs = (
        P("ep", None),
        P(),
        P(),
        P("ep", None),
        P("ep", None, ("pp", "dp")),
        P("ep", ("pp", "dp"), None),
    )
    out_specs = P("ep", None)
    return jax.shard_map(
        on_device, mesh=mesh, in_specs=in_specs, out_specs=out_specs, check_vma=False
    )
```

profile of v0, /device:TPU:1, one launch (start us, length us, event | category | flops | bytes accessed | tf_op | source)
XLA Modules:
  0.0 632.8 jit_solution(198469074752060265)
XLA Ops:
  0.0 0.8 broadcast_multiply_fusion
  0.8 0.8 copy.35
  1.9 1.7 convert_reduce_fusion
  3.6 2.0 fusion.9
  5.6 0.1 copy.34
  5.9 4.5 reduce-window.6
  10.9 0.7 fusion.11
  11.6 32.6 %scatter_custom_fusion = bf16[1152,3072]{1,0:T(8,128)(2,1)} fusion(s32[1024]{0:T(1024)S(1)} %bitcast.54, bf16[256,3072]{1,0:T(8,128)(2,1)S(1)} %fusion.11, s32[1024]{0:T(1024)S(1)} %broadcast_clamp_fusion.1, bf16[]{:T(256)} %constant.60.clone.1), kind=kCustom, calls=%fused_computation.8 | custom fusion | bytes 7077890 | tf_op jit(solution)/shard_map/scatter | solution.py:56
  44.2 7.6 %all-to-all-start = ((bf16[16,1,72,3072]{3,2,1,0:T(8,128)(2,1)}), bf16[16,1,72,3072]{3,2,1,0:T(8,128)(2,1)}, u32[]{:S(2)}, u32[]{:S(2)}) async-start(bf16[16,1,72,3072]{3,2,1,0:T(8,128)(2,1)} %bitcast.49), calls=%async_computation | async-start | bytes 14155776 | tf_op jit(solution)/shard_map/all_to_all | solution.py:58
  51.8 103.9 %all-to-all-done = bf16[16,1,72,3072]{3,2,1,0:T(8,128)(2,1)} async-done(((bf16[16,1,72,3072]{3,2,1,0:T(8,128)(2,1)}), bf16[16,1,72,3072]{3,2,1,0:T(8,128)(2,1)}, u32[]{:S(2)}, u32[]{:S(2)}) %all-to-all-start) | async-done | bytes 7077920 | tf_op jit(solution)/shard_map/all_to_all | solution.py:58
  155.7 9.6 %multiply_convert_fusion = bf16[16,72,768]{2,1,0:T(8,128)(2,1)S(1)} fusion(bf16[1,3072,768]{2,1,0:T(8,128)(2,1)} %param.10, bf16[16,1,72,3072]{3,2,1,0:T(8,128)(2,1)} %all-to-all-done), kind=kOutput, calls=%fused_computation.17 | convolution fusion | flops 5440241664 | bytes 13565952 | tf_op jit(solution)/shard_map/gscd,sdf->sgcf/dot_general | solution.py:39
  165.3 11.3 %convolution_select_fusion = f32[1152,3072]{1,0:T(8,128)} fusion(bf16[1152,768]{1,0:T(8,128)(2,1)S(1)} %bitcast.57, pred[1152]{0:T(1024)(128)(4,1)S(1)} %fusion.21, bf16[1,768,3072]{2,1,0:T(8,128)(2,1)} %param.11), kind=kOutput, calls=%fused_computation.4 | convolution fusion | flops 5439356928 | bytes 20644992 | tf_op jit(solution)/shard_map/dot_general | solution.py:43
  176.6 281.8 %all-reduce.1 = bf16[1152,3072]{1,0:T(8,128)(2,1)} all-reduce(f32[1152,3072]{1,0:T(8,128)} %convolution_select_fusion), channel_id=1, replica_groups=mesh['pp'=2,'ep'=16,'dp'=4] {'pp','dp'}, use_global_device_ids=true, to_apply=%region_7.8 | all-reduce | flops 3538944 | bytes 21233664 | tf_op jit(solution)/shard_map/psum | solution.py:45
  458.4 5.6 all-to-all-start.1
  464.0 0.1 copy.31
  464.3 0.5 fusion.25
  464.8 8.7 %gather_fusion.1 = f32[1024]{0:T(1024)S(1)} fusion(f32[256,16]{0,1:T(8,128)S(1)} %fusion.25, s32[1024]{0:T(1024)S(1)} %reshape.186), kind=kCustom, calls=%fused_computation.2 | custom fusion | bytes 16384 | tf_op jit(solution)/shard_map/jit(take_along_axis)/gather | solution.py:33
  473.5 0.1 reshape.189
  473.7 0.1 copy.33
  473.9 98.2 %all-to-all-done.1 = bf16[16,1,72,3072]{3,2,1,0:T(8,128)(2,1)} async-done(((bf16[16,1,72,3072]{3,2,1,0:T(8,128)(2,1)}), bf16[16,1,72,3072]{3,2,1,0:T(8,128)(2,1)}, u32[]{:S(2)}, u32[]{:S(2)}) %all-to-all-start.1) | async-done | bytes 7077920 | tf_op jit(solution)/shard_map/all_to_all | solution.py:60
  572.1 16.1 %gather_fusion = bf16[1024,3072]{1,0:T(8,128)(2,1)} fusion(bf16[1152,3072]{1,0:T(8,128)(2,1)} %bitcast.14, s32[1024]{0:T(1024)S(1)} %broadcast_clamp_fusion), kind=kCustom, calls=%fused_computation.1 | custom fusion | bytes 12587008 | tf_op jit(solution)/shard_map/gather | solution.py:61
  588.2 12.2 %reshape.169 = f32[256,4,3072]{2,1,0:T(4,128)} reshape(bf16[1024,3072]{1,0:T(8,128)(2,1)} %gather_fusion) | data formatting | bytes 18874368 | tf_op jit(solution)/shard_map/convert_element_type | solution.py:62
  600.5 30.8 %multiply_reduce_fusion = f32[256,3072]{1,0:T(8,128)S(1)} fusion(f32[256,4,3072]{2,1,0:T(4,128)} %reshape.169, f32[256,4]{1,0:T(8,128)S(1)} %copy.33), kind=kLoop, calls=%fused_computation.5 | loop fusion | flops 5505024 | bytes 15732736 | tf_op jit(solution)/shard_map/reduce_sum | solution.py:62
  631.2 1.6 fusion.12
  (33 shorter events, 1.1 us)
Async XLA Ops:
  0.0 464.3 %copy-start = (bf16[3072,16]{0,1:T(8,128)(2,1)S(1)}, bf16[3072,16]{0,1:T(8,128)(2,1)}, u32[]{:S(2)}) copy-start(bf16[3072,16]{0,1:T(8,128)(2,1)} %param.8) | copy-start | bytes 294916
  0.0 10.9 %copy-start.2 = (bf16[256,3072]{1,0:T(8,128)(2,1)S(1)}, bf16[256,3072]{1,0:T(8,128)(2,1)}, u32[]{:S(2)}) copy-start(bf16[256,3072]{1,0:T(8,128)(2,1)} %param.6) | copy-start | bytes 4718596
  0.0 10.9 %copy-start.4 = (f32[3072]{0:T(1024)S(1)}, f32[3072]{0:T(1024)}, u32[]{:S(2)}) copy-start(f32[3072]{0:T(1024)} %param.7) | copy-start | bytes 36868
  44.2 111.5 %all-to-all-start = ((bf16[16,1,72,3072]{3,2,1,0:T(8,128)(2,1)}), bf16[16,1,72,3072]{3,2,1,0:T(8,128)(2,1)}, u32[]{:S(2)}, u32[]{:S(2)}) async-start(bf16[16,1,72,3072]{3,2,1,0:T(8,128)(2,1)} %bitcast.49), calls=%async_computation | async-start | bytes 14155776 | tf_op jit(solution)/shard_map/all_to_all | solution.py:58
  458.4 5.6 copy-start.3
  458.4 113.7 %all-to-all-start.1 = ((bf16[16,1,72,3072]{3,2,1,0:T(8,128)(2,1)}), bf16[16,1,72,3072]{3,2,1,0:T(8,128)(2,1)}, u32[]{:S(2)}, u32[]{:S(2)}) async-start(bf16[16,1,72,3072]{3,2,1,0:T(8,128)(2,1)} %bitcast.50), calls=%async_computation.1 | async-start | bytes 14155776 | tf_op jit(solution)/shard_map/all_to_all | solution.py:60
  600.5 32.4 %copy-start.1 = (bf16[3072,16]{0,1:T(8,128)(2,1)S(1)}, bf16[3072,16]{0,1:T(8,128)(2,1)}, u32[]{:S(2)}) copy-start(bf16[3072,16]{0,1:T(8,128)(2,1)} %param.8) | copy-start | bytes 294916
where the time goes:
time: 634 us; the launch traced here: 633 us
  blocking collectives  282 us (44%)
  waiting for transfers between devices  202 us (32%)
  local copies, waits for them, and re-layouts  71.8 us (11%)
  other arithmetic  42.4 us (7%)
  matrix products  21.4 us (3%)
  starting transfers between devices  13.2 us (2%)
    psum x1, blocking collectives, expert_rows(): whole = lax.psum(total, ('pp', 'dp')).astype(jnp.bfloat16)  282 us
    all_to_all x1, waiting for transfers between devices, on_device(): lax.all_to_all(outgoing, 'ep', split_axis=0, concat_axis=0, tiled=True)  104 us
    all_to_all x1, waiting for transfers between devices, on_device(): lax.all_to_all(answered, 'ep', split_axis=0, concat_axis=0, tiled=True)  98.2 us
    scatter x1, local copies, waits for them, and re-layouts, on_device(): jnp.zeros((EXPERTS * CAP, D), jnp.bfloat16).at[slot_index]  32.6 us
    reduce_sum x1, other arithmetic, on_device(): jnp.sum(gate_values[:, :, None] * picked.astype(jnp.float32), axis=1)  30.8 us
    gather x1, local copies, waits for them, and re-layouts, on_device(): returned.reshape(EXPERTS * CAP, D)[slot_index].reshape(TOK_DEV, TOP, D)  16.1 us
  transfers between devices with their start and end apart: 2, of which 2 were waited for; matrix products, arithmetic and copies ran while one was open for 2% of the time, Pallas kernels for 0%

commit v1 on v0

v1 whole, which is shorter than its diff:
```python
import jax
import jax.numpy as jnp
from jax import lax
from jax.experimental import pallas as pl
from jax.experimental.pallas import tpu as pltpu
from jax.sharding import PartitionSpec as P

D = 3072
EXPERTS = 16
TOP = 4
TOK_DEV = 256
CAP = 72
ROWS = EXPERTS * CAP
HALF = D // 2
SHARE = D // 8
EPSILON = 1e-05
F32 = jnp.float32
BF16 = jnp.bfloat16
VMEM_LIMIT = 60 * 1024 * 1024
NT = (((1,), (1,)), ((), ()))


def route_kernel(tok_ref, gain_ref, router_ref, ids_ref, buf_ref, mix_ref, normed_ref, key_ref):
    step = pl.program_id(0)
    experts_a_step = EXPERTS // pl.num_programs(0)

    @pl.when(step == 0)
    def _():
        def norm_rows(part, carry):
            rows = pl.ds(pl.multiple_of(part * 32, 32), 32)
            values = tok_ref[rows, :].astype(F32)
            shifted = values - jnp.mean(values, axis=-1, keepdims=True)
            spread = jnp.mean(shifted * shifted, axis=-1, keepdims=True)
            normed = (shifted * lax.rsqrt(spread + EPSILON) * gain_ref[...]).astype(BF16)
            normed_ref[0, rows, :] = normed[:, :HALF]
            normed_ref[1, rows, :] = normed[:, HALF:]
            return carry

        lax.fori_loop(0, TOK_DEV // 32, norm_rows, 0)
        logits = lax.dot_general(normed_ref[0], router_ref[:, :HALF], NT, preferred_element_type=F32)
        logits += lax.dot_general(normed_ref[1], router_ref[:, HALF:], NT, preferred_element_type=F32)

        named = jnp.zeros((EXPERTS, TOK_DEV), jnp.int32)
        expert = lax.broadcasted_iota(jnp.int32, (EXPERTS, TOK_DEV), 0)
        for k in range(TOP):
            named += (ids_ref[k : k + 1, :] == expert).astype(jnp.int32)
        named = named.astype(F32)
        row = lax.broadcasted_iota(jnp.int32, (TOK_DEV, TOK_DEV), 0)
        col = lax.broadcasted_iota(jnp.int32, (TOK_DEV, TOK_DEV), 1)
        earlier = (row > col).astype(F32).astype(BF16)
        same = (row == col).astype(F32).astype(BF16)
        named_bf = named.astype(BF16)
        place_t = lax.dot_general(named_bf, earlier, NT, preferred_element_type=F32)
        key_ref[...] = jnp.where(named > 0.5, place_t, -1.0)
        place = lax.dot_general(earlier, named_bf, NT, preferred_element_type=F32)
        chosen = lax.dot_general(same, named_bf, NT, preferred_element_type=F32) > 0.5
        key = jnp.where(chosen, place, -1.0)
        weight = jnp.where(chosen, jnp.exp(logits), 0.0)
        gate = weight / jnp.sum(weight, axis=1, keepdims=True)

        slot = lax.broadcasted_iota(jnp.int32, (EXPERTS, ROWS), 1)
        first = lax.broadcasted_iota(jnp.int32, (EXPERTS, ROWS), 0) * CAP
        inside = (slot >= first) & (slot < first + CAP)
        spread_out = inside.astype(F32).astype(BF16)
        slot_in = jnp.sum(jnp.where(inside, slot - first, 0).astype(F32), axis=0, keepdims=True)
        key_wide = jnp.dot(key.astype(BF16), spread_out, preferred_element_type=F32)
        gate_wide = jnp.dot(gate.astype(BF16), spread_out, preferred_element_type=F32)
        mix_ref[...] = jnp.where(key_wide == slot_in, gate_wide, 0.0).astype(BF16)

    keys = key_ref[pl.ds(pl.multiple_of(step * experts_a_step, experts_a_step), experts_a_step), :]
    slot_row = lax.broadcasted_iota(jnp.int32, (CAP, TOK_DEV), 0).astype(F32)
    picks = [(slot_row == keys[e : e + 1, :]).astype(F32) for e in range(experts_a_step)]
    pick = jnp.concatenate(picks, axis=0).astype(BF16)
    buf_ref[...] = jnp.dot(pick, normed_ref[lax.axis_index("pp")], preferred_element_type=F32).astype(BF16)


def route(tokens, norm_gain, router_weight, expert_ids):
    steps = 2
    whole = lambda i: (0, 0)
    return pl.pallas_call(
        route_kernel,
        grid=(steps,),
        in_specs=[
            pl.BlockSpec((TOK_DEV, D), whole),
            pl.BlockSpec((1, D), whole),
            pl.BlockSpec((EXPERTS, D), whole),
            pl.BlockSpec((TOP, TOK_DEV), whole),
        ],
        out_specs=[
            pl.BlockSpec((ROWS // steps, HALF), lambda i: (i, 0)),
            pl.BlockSpec((TOK_DEV, ROWS), whole),
        ],
        out_shape=[
            jax.ShapeDtypeStruct((ROWS, HALF), BF16),
            jax.ShapeDtypeStruct((TOK_DEV, ROWS), BF16),
        ],
        scratch_shapes=[
            pltpu.VMEM((2, TOK_DEV, HALF), BF16),
            pltpu.VMEM((EXPERTS, TOK_DEV), F32),
        ],
        compiler_params=pltpu.CompilerParams(vmem_limit_bytes=VMEM_LIMIT),
        cost_estimate=pl.CostEstimate(flops=2 * ROWS * TOK_DEV * HALF, bytes_accessed=6_000_000, transcendentals=0),
    )(tokens, norm_gain.reshape(1, D), router_weight.T, expert_ids.T)


def up_first_kernel(at_ref, x_ref, w_ref, out_ref):
    out_ref[...] = jnp.dot(x_ref[...], w_ref[0], preferred_element_type=F32)


def up_second_kernel(at_ref, x_ref, w_ref, part_ref, out_ref):
    value = part_ref[...] + jnp.dot(x_ref[...], w_ref[0], preferred_element_type=F32)
    out_ref[...] = (value / (1.0 + jnp.exp(-value))).astype(BF16)


def up_half(at, rows_in, weight, part=None):
    count, inner = rows_in.shape
    units = weight.shape[2]
    block = count // 4
    row_block = lambda i, at: (i, 0)
    specs = [pl.BlockSpec((block, inner), row_block), pl.BlockSpec((1, inner, units), lambda i, at: (at[0], 0, 0))]
    args = [rows_in, weight]
    if part is not None:
        specs.append(pl.BlockSpec((block, units), row_block))
        args.append(part)
    return pl.pallas_call(
        up_first_kernel if part is None else up_second_kernel,
        grid_spec=pltpu.PrefetchScalarGridSpec(
            num_scalar_prefetch=1,
            grid=(4,),
            in_specs=specs,
            out_specs=pl.BlockSpec((block, units), row_block),
        ),
        out_shape=jax.ShapeDtypeStruct((count, units), F32 if part is None else BF16),
        compiler_params=pltpu.CompilerParams(vmem_limit_bytes=VMEM_LIMIT),
        cost_estimate=pl.CostEstimate(flops=2 * count * inner * units, bytes_accessed=9_000_000, transcendentals=0),
    )(at, *args)


def down_first_kernel(at_ref, h_ref, w_ref, out_ref):
    out_ref[0] = jnp.dot(h_ref[...], w_ref[...], preferred_element_type=F32).astype(BF16)


def down_second_kernel(at_ref, h_ref, w_ref, got_ref, out_ref):
    value = jnp.dot(h_ref[...], w_ref[...], preferred_element_type=F32)
    out_ref[0] = (value + got_ref[0].astype(F32)).astype(BF16)


def down_half(at, hidden, weight, got=None):
    count, units = hidden.shape
    piece = lambda i, at: (i, 0, 0)
    specs = [
        pl.BlockSpec((count, units), lambda i, at: (0, 0)),
        pl.BlockSpec((units, SHARE), lambda i, at: (0, at[0] * 4 + i)),
    ]
    args = [hidden, weight]
    if got is not None:
        specs.append(pl.BlockSpec((1, count, SHARE), piece))
        args.append(got)
    return pl.pallas_call(
        down_first_kernel if got is None else down_second_kernel,
        grid_spec=pltpu.PrefetchScalarGridSpec(
            num_scalar_prefetch=1,
            grid=(4,),
            in_specs=specs,
            out_specs=pl.BlockSpec((1, count, SHARE), piece),
        ),
        out_shape=jax.ShapeDtypeStruct((4, count, SHARE), BF16),
        compiler_params=pltpu.CompilerParams(vmem_limit_bytes=VMEM_LIMIT),
        cost_estimate=pl.CostEstimate(flops=2 * count * units * HALF, bytes_accessed=9_000_000, transcendentals=0),
    )(at, *args)


def mix_kernel(at_ref, tok_ref, mix_ref, rows_ref, out_ref):
    total = tok_ref[...].astype(F32)
    for source in range(rows_ref.shape[0]):
        total += jnp.dot(mix_ref[...], rows_ref[source], preferred_element_type=F32)
    out_ref[...] = total.astype(BF16)


def mix(at, tokens, mix_matrix, rows):
    whole = lambda i, at: (0, 0)
    return pl.pallas_call(
        mix_kernel,
        grid_spec=pltpu.PrefetchScalarGridSpec(
            num_scalar_prefetch=1,
            grid=(1,),
            in_specs=[
                pl.BlockSpec((TOK_DEV, SHARE), lambda i, at: (0, at[0])),
                pl.BlockSpec((TOK_DEV, ROWS), whole),
                pl.BlockSpec(rows.shape, lambda i, at: (0, 0, 0)),
            ],
            out_specs=pl.BlockSpec((TOK_DEV, SHARE), whole),
        ),
        out_shape=jax.ShapeDtypeStruct((TOK_DEV, SHARE), BF16),
        compiler_params=pltpu.CompilerParams(vmem_limit_bytes=VMEM_LIMIT),
        cost_estimate=pl.CostEstimate(flops=8 * TOK_DEV * ROWS * SHARE, bytes_accessed=4_000_000, transcendentals=0),
    )(at, tokens, mix_matrix, rows)


def swap(values):
    return lax.ppermute(values, "pp", [(0, 1), (1, 0)])


def spread_copies(values, axis):
    count = lax.axis_size(axis)
    copies = jnp.broadcast_to(values[None], (count,) + values.shape)
    return lax.all_to_all(copies, axis, split_axis=0, concat_axis=0, tiled=True)


def on_device(tokens, norm_gain, router_weight, expert_ids, up_weight, down_weight):
    core = lax.axis_index("pp").astype(jnp.int32)
    own, other = core.reshape(1), (1 - core).reshape(1)
    share = (core * 4 + lax.axis_index("dp").astype(jnp.int32)).reshape(1)
    up = up_weight.reshape(2, HALF, up_weight.shape[2])
    down = down_weight[0]

    outgoing, mix_matrix = route(tokens, norm_gain, router_weight, expert_ids)
    mine = lax.all_to_all(outgoing.reshape(EXPERTS, CAP, HALF), "ep", split_axis=0, concat_axis=0, tiled=True).reshape(ROWS, HALF)
    theirs = swap(mine)
    part = up_half(own, mine, up)
    hidden = up_half(other, theirs, up, part)
    got = swap(down_half(other, hidden, down))
    total = down_half(own, hidden, down, got)
    returned = lax.all_to_all(
        total.reshape(4 * EXPERTS, CAP, SHARE), ("dp", "ep"), split_axis=0, concat_axis=0, tiled=True
    ).reshape(4, ROWS, SHARE)
    piece = mix(share, tokens, mix_matrix, returned)
    pieces = spread_copies(spread_copies(piece, "dp"), "pp")
    return jnp.transpose(pieces, (2, 0, 1, 3)).reshape(TOK_DEV, D)


def solution(mesh):
    in_specs = (
        P("ep", None),
        P(),
        P(),
        P("ep", None),
        P("ep", None, ("pp", "dp")),
        P("ep", ("pp", "dp"), None),
    )
    return jax.shard_map(on_device, mesh=mesh, in_specs=in_specs, out_specs=P("ep", None), check_vma=False)
```

time: 634 us -> 185 us (0.29)
  blocking collectives: 282 us -> 71.2 us
  waiting for transfers between devices: 202 us -> 51.5 us
  local copies, waits for them, and re-layouts: 71.8 us -> 8.57 us
  other arithmetic: 42.4 us -> 0 us
  Pallas kernels: 0 us -> 41.9 us
  matrix products: 21.4 us -> 0 us
    psum x1 -> x0, blocking collectives: 282 us -> none  [expert_rows(): whole = lax.psum(total, ('pp', 'dp')).astype(jnp.bfloat16)]
    all_to_all x2 -> x1, waiting for transfers between devices: 202 us -> 45.5 us  [on_device(): lax.all_to_all(total.reshape(4 * EXPERTS, CAP, SHARE), ('dp', 'ep'), spli...]
    all_to_all x0 -> x3, blocking collectives: none -> 71.2 us  [the longest x1 50.5 us: on_device(): lax.all_to_all(outgoing.reshape(EXPERTS, CAP, HALF), 'ep', split_axis=0,...]
    pallas_call x0 -> x6, Pallas kernels: none -> 41.9 us  [the longest x2 15.3 us: down_half(): pl.pallas_call(down_first_kernel if got is None else down_second_kernel,...]
    reduce_sum x5 -> x0, other arithmetic: 34.5 us -> none  [the longest x1 30.8 us: on_device(): jnp.sum(gate_values[:, :, None] * picked.astype(jnp.float32), axis=1)]
    scatter x1 -> x0, local copies, waits for them, and re-layouts: 32.6 us -> none  [on_device(): jnp.zeros((EXPERTS * CAP, D), jnp.bfloat16).at[slot_index]]
    gather x6 -> x0, local copies, waits for them, and re-layouts: 25.3 us -> none  [the longest x1 16.1 us: on_device(): returned.reshape(EXPERTS * CAP, D)[slot_index].reshape(TOK_DEV, TOP, D)]
    dot_general x3 -> x0, matrix products: 21.4 us -> none  [the longest x1 11.3 us: expert_rows(): term = jnp.dot(hidden, down_matrix[0], preferred_element_type=jnp.float32)]
  transfers between devices with their start and end apart: 2 -> 3, of which waited for: 2 -> 2; matrix products, arithmetic and copies ran while one was open for 2% -> 0% of each run, Pallas kernels for 0% -> 4%
where the time goes in v1:
time: 185 us; the launch traced here: 184 us
  blocking collectives  71.2 us (38%)
  waiting for transfers between devices  51.5 us (28%)
  Pallas kernels  41.9 us (23%)
  starting transfers between devices  10.8 us (6%)
  local copies, waits for them, and re-layouts  8.57 us (5%)
    all_to_all x1, blocking collectives, on_device(): lax.all_to_all(outgoing.reshape(EXPERTS, CAP, HALF), 'ep', split_axis=0,...  50.5 us
    all_to_all x1, waiting for transfers between devices, on_device(): lax.all_to_all(total.reshape(4 * EXPERTS, CAP, SHARE), ('dp', 'ep'), spli...  45.5 us
    all_to_all x2, blocking collectives, spread_copies(): return lax.all_to_all(copies, axis, split_axis=0, concat_axis=0, tiled=True)  20.7 us
    pallas_call x2, Pallas kernels, down_half(): pl.pallas_call(down_first_kernel if got is None else down_second_kernel,...  15.3 us
    pallas_call x2, Pallas kernels, up_half(): pl.pallas_call(up_first_kernel if part is None else up_second_kernel, gri...  14.6 us
    pallas_call x1, Pallas kernels, route(): pl.pallas_call(route_kernel, grid=(steps,), in_specs=[pl.BlockSpec((TOK_D...  7.56 us
    all_to_all x1, starting transfers between devices, on_device(): lax.all_to_all(total.reshape(4 * EXPERTS, CAP, SHARE), ('dp', 'ep'), spli...  7.16 us
    ppermute x2, waiting for transfers between devices, swap(): return lax.ppermute(values, 'pp', [(0, 1), (1, 0)])  6.06 us
  transfers between devices with their start and end apart: 3, of which 2 were waited for; matrix products, arithmetic and copies ran while one was open for 0% of the time, Pallas kernels for 4%

profile of v1, /device:TPU:1, one launch (start us, length us, event | category | flops | bytes accessed | tf_op | source)
XLA Modules:
  0.0 184.0 jit_solution(8088771385941657415)
XLA Ops:
  0.0 7.6 %shard_map.64 = (bf16[1152,1536]{1,0:T(8,128)(2,1)}, bf16[256,1152]{1,0:T(8,128)(2,1)}) custom-call(bf16[256,3072]{1,0:T(8,128)(2,1)} %tok_ref.3, f32[1,3072]{1,0:T(1,128)} %bitcast.26, bf16[16,3072]{1,0:T(8,128)(2,1)} %bitcast.25, s32[4,256]{1,0:T(4,128)} %bitcast.27), custom_call_target="tpu_custom_call" | custom-call | flops 905969664 | bytes 6000000 | tf_op jit(solution)/shard_map/pallas_call | solution.py:80
  7.6 50.5 %all_to_all.20 = bf16[16,72,1536]{2,1,0:T(8,128)(2,1)S(1)} all-to-all(bf16[16,72,1536]{2,1,0:T(8,128)(2,1)} %bitcast.24), channel_id=1, replica_groups=mesh['pp'=2,'ep'=16,'dp'=4] {'ep'}, dimensions={0} | all-to-all | bytes 7077888 | tf_op jit(solution)/shard_map/all_to_all | solution.py:218
  58.1 0.0 copy-start
  58.1 1.8 collective-permute-start
  59.9 0.0 copy-done
  59.9 7.0 %shard_map.65.part_ref = f32[1152,768]{1,0:T(8,128)} custom-call(s32[1]{0:T(128)} %bitcast.4.at_ref, bf16[1152,1536]{1,0:T(8,128)(2,1)} %bitcast.18, bf16[2,1536,768]{2,1,0:T(8,128)(2,1)} %bitcast.15), custom_call_target="tpu_custom_call" | custom-call | flops 2717908992 | bytes 9000000 | tf_op jit(solution)/shard_map/pallas_call | solution.py:125
  67.0 0.0 collective-permute-done.x_ref
  67.0 7.6 %shard_map.66.h_ref = bf16[1152,768]{1,0:T(8,128)(2,1)} custom-call(s32[1]{0:T(128)} %bitcast.5.at_ref, bf16[1152,1536]{1,0:T(8,128)(2,1)} %collective-permute-done.x_ref, bf16[2,1536,768]{2,1,0:T(8,128)(2,1)} %bitcast.16, f32[1152,768]{1,0:T(8,128)} %shard_map.65.part_ref), custom_call_target="tpu_custom_call" | custom-call | flops 2717908992 | bytes 9000000 | tf_op jit(solution)/shard_map/pallas_call | solution.py:125
  74.6 7.3 %shard_map.67 = bf16[4,1152,384]{2,1,0:T(8,128)(2,1)} custom-call(s32[1]{0:T(128)} %bitcast.5.at_ref, bf16[1152,768]{1,0:T(8,128)(2,1)} %shard_map.66.h_ref, bf16[768,3072]{1,0:T(8,128)(2,1)} %bitcast.22), custom_call_target="tpu_custom_call" | custom-call | flops 2717908992 | bytes 9000000 | tf_op jit(solution)/shard_map/pallas_call | solution.py:159
  81.9 1.8 collective-permute-start.1
  83.7 6.1 %collective-permute-done.1.got_ref = bf16[4,1152,384]{2,1,0:T(8,128)(2,1)S(1)} collective-permute-done((bf16[4,1152,384]{2,1,0:T(8,128)(2,1)}, bf16[4,1152,384]{2,1,0:T(8,128)(2,1)S(1)}, u32[]{:S(2)}, u32[]{:S(2)}) %collective-permute-start.1) | collective-permute-done | bytes 3538976 | tf_op jit(solution)/shard_map/ppermute | solution.py:201
  89.7 1.8 copy-done.2
  91.5 8.0 %shard_map.68 = bf16[4,1152,384]{2,1,0:T(8,128)(2,1)} custom-call(s32[1]{0:T(128)} %bitcast.4.at_ref, bf16[1152,768]{1,0:T(8,128)(2,1)} %shard_map.66.h_ref, bf16[768,3072]{1,0:T(8,128)(2,1)} %bitcast.23, bf16[4,1152,384]{2,1,0:T(8,128)(2,1)} %copy-done.2), custom_call_target="tpu_custom_call" | custom-call | flops 2717908992 | bytes 9000000 | tf_op jit(solution)/shard_map/pallas_call | solution.py:159
  99.5 7.2 %all-to-all-start.1 = ((bf16[64,72,384]{2,1,0:T(8,128)(2,1)}), bf16[64,72,384]{2,1,0:T(8,128)(2,1)S(1)}, u32[]{:S(2)}, u32[]{:S(2)}) async-start(bf16[64,72,384]{2,1,0:T(8,128)(2,1)} %bitcast.20), calls=%async_computation.1 | async-start | bytes 7077888 | tf_op jit(solution)/shard_map/all_to_all | solution.py:224
  106.7 45.5 %all-to-all-done.1 = bf16[64,72,384]{2,1,0:T(8,128)(2,1)S(1)} async-done(((bf16[64,72,384]{2,1,0:T(8,128)(2,1)}), bf16[64,72,384]{2,1,0:T(8,128)(2,1)S(1)}, u32[]{:S(2)}, u32[]{:S(2)}) %all-to-all-start.1) | async-done | bytes 3538976 | tf_op jit(solution)/shard_map/all_to_all | solution.py:224
  152.1 1.8 copy-done.1
  153.9 4.4 %shard_map.69 = bf16[256,384]{1,0:T(8,128)(2,1)} custom-call(s32[1]{0:T(128)} %bitcast.at_ref, bf16[256,3072]{1,0:T(8,128)(2,1)} %tok_ref.3, bf16[256,1152]{1,0:T(8,128)(2,1)} %get-tuple-element.7.mix_ref, bf16[4,1152,384]{2,1,0:T(8,128)(2,1)} %bitcast.19), custom_call_target="tpu_custom_call" | custom-call | flops 905969664 | bytes 4000000 | tf_op jit(solution)/shard_map/pallas_call | solution.py:182
  158.3 1.0 broadcast_in_dim.4
  159.3 12.8 %all_to_all.21 = bf16[4,256,384]{2,1,0:T(8,128)(2,1)S(1)} all-to-all(bf16[4,256,384]{2,1,0:T(8,128)(2,1)S(1)} %broadcast_in_dim.4), channel_id=1, replica_groups=mesh['pp'=2,'ep'=16,'dp'=4] {'dp'}, dimensions={0} | all-to-all | bytes 1572864 | tf_op jit(solution)/shard_map/all_to_all | solution.py:207
  172.1 0.6 copy.8
  172.7 0.4 broadcast_in_dim.5
  173.2 7.8 %all_to_all.22 = bf16[2,4,256,384]{3,1,2,0:T(4,128)(2,1)S(1)} all-to-all(bf16[2,4,256,384]{3,1,2,0:T(4,128)(2,1)S(1)} %broadcast_in_dim.5), channel_id=1, replica_groups=mesh['pp'=2,'ep'=16,'dp'=4] {'pp'}, dimensions={0} | all-to-all | bytes 3145728 | tf_op jit(solution)/shard_map/all_to_all | solution.py:207
  181.0 1.3 copy.9
  182.3 1.7 copy.10
  (2 shorter events, 0.0 us)
Async XLA Ops:
  58.1 1.8 copy-start
  58.1 8.8 %collective-permute-start = (bf16[1152,1536]{1,0:T(8,128)(2,1)S(1)}, bf16[1152,1536]{1,0:T(8,128)(2,1)}, u32[]{:S(2)}, u32[]{:S(2)}) collective-permute-start(bf16[1152,1536]{1,0:T(8,128)(2,1)S(1)} %bitcast.17), channel_id=1, source_target_pairs={{0,64},{64,0},{1,65},{65,1},{2,66},{66,2},{3,67},{67,3},{4,68},{68... | collective-permute-start | bytes 10616840 | tf_op jit(solution)/shard_map/ppermute | solution.py:201
  81.9 7.8 %collective-permute-start.1 = (bf16[4,1152,384]{2,1,0:T(8,128)(2,1)}, bf16[4,1152,384]{2,1,0:T(8,128)(2,1)S(1)}, u32[]{:S(2)}, u32[]{:S(2)}) collective-permute-start(bf16[4,1152,384]{2,1,0:T(8,128)(2,1)} %shard_map.67), channel_id=1, source_target_pairs={{0,64},{64,0},{1,65},{65,1},{2,66},{66,2},{3,67},{67,3},{4,68},{68... | collective-permute-start | bytes 10616840 | tf_op jit(solution)/shard_map/ppermute | solution.py:201
  89.7 1.8 copy-start.2
  99.5 52.7 %all-to-all-start.1 = ((bf16[64,72,384]{2,1,0:T(8,128)(2,1)}), bf16[64,72,384]{2,1,0:T(8,128)(2,1)S(1)}, u32[]{:S(2)}, u32[]{:S(2)}) async-start(bf16[64,72,384]{2,1,0:T(8,128)(2,1)} %bitcast.20), calls=%async_computation.1 | async-start | bytes 7077888 | tf_op jit(solution)/shard_map/all_to_all | solution.py:224
  152.1 1.8 copy-start.1

commit v2 on v1

--- a/solution.py
+++ b/solution.py
@@ -12,11 +12,14 @@
 CAP = 72
 ROWS = EXPERTS * CAP
 HALF = D // 2
-SHARE = D // 8
+WIDE = 512
+THIN = 256
+Z_STEPS = (0, 2, 1, 3)
 EPSILON = 1e-05
 F32 = jnp.float32
 BF16 = jnp.bfloat16
-VMEM_LIMIT = 60 * 1024 * 1024
+ROUTE_VMEM = 60 * 1024 * 1024
+MATMUL_VMEM = 16 * 1024 * 1024
 NT = (((1,), (1,)), ((), ()))
 
 
@@ -98,7 +101,7 @@
             pltpu.VMEM((2, TOK_DEV, HALF), BF16),
             pltpu.VMEM((EXPERTS, TOK_DEV), F32),
         ],
-        compiler_params=pltpu.CompilerParams(vmem_limit_bytes=VMEM_LIMIT),
+        compiler_params=pltpu.CompilerParams(vmem_limit_bytes=ROUTE_VMEM),
         cost_estimate=pl.CostEstimate(flops=2 * ROWS * TOK_DEV * HALF, bytes_accessed=6_000_000, transcendentals=0),
     )(tokens, norm_gain.reshape(1, D), router_weight.T, expert_ids.T)
 
@@ -131,7 +134,7 @@
             out_specs=pl.BlockSpec((block, units), row_block),
         ),
         out_shape=jax.ShapeDtypeStruct((count, units), F32 if part is None else BF16),
-        compiler_params=pltpu.CompilerParams(vmem_limit_bytes=VMEM_LIMIT),
+        compiler_params=pltpu.CompilerParams(vmem_limit_bytes=MATMUL_VMEM),
         cost_estimate=pl.CostEstimate(flops=2 * count * inner * units, bytes_accessed=9_000_000, transcendentals=0),
     )(at, *args)
 
@@ -140,93 +143,152 @@
     out_ref[0] = jnp.dot(h_ref[...], w_ref[...], preferred_element_type=F32).astype(BF16)
 
 
-def down_second_kernel(at_ref, h_ref, w_ref, got_ref, out_ref):
+def down_second_kernel(at_ref, h_ref, w_ref, got_ref, *out_refs):
     value = jnp.dot(h_ref[...], w_ref[...], preferred_element_type=F32)
-    out_ref[0] = (value + got_ref[0].astype(F32)).astype(BF16)
-
-
-def down_half(at, hidden, weight, got=None):
+    value = (value + got_ref[0].astype(F32)).astype(BF16)
+    for piece, out_ref in enumerate(out_refs):
+
+        @pl.when(pl.program_id(0) == piece)
+        def _(out_ref=out_ref):
+            out_ref[...] = value
+
+
+def down_part(blocks, hidden, weight, width, got=None):
     count, units = hidden.shape
-    piece = lambda i, at: (i, 0, 0)
+    parts = blocks.shape[0]
+    piece = pl.BlockSpec((1, count, width), lambda i, at: (i, 0, 0))
     specs = [
         pl.BlockSpec((count, units), lambda i, at: (0, 0)),
-        pl.BlockSpec((units, SHARE), lambda i, at: (0, at[0] * 4 + i)),
+        pl.BlockSpec((units, width), lambda i, at: (0, at[i])),
     ]
     args = [hidden, weight]
-    if got is not None:
-        specs.append(pl.BlockSpec((1, count, SHARE), piece))
+    if got is None:
+        out_specs, out_shape = piece, jax.ShapeDtypeStruct((parts, count, width), BF16)
+    else:
+        specs.append(piece)
         args.append(got)
+        out_specs = [pl.BlockSpec((count, width), lambda i, at: (0, 0))] * parts
+        out_shape = [jax.ShapeDtypeStruct((count, width), BF16)] * parts
     return pl.pallas_call(
         down_first_kernel if got is None else down_second_kernel,
-        grid_spec=pltpu.PrefetchScalarGridSpec(
-            num_scalar_prefetch=1,
-            grid=(4,),
-            in_specs=specs,
-            out_specs=pl.BlockSpec((1, count, SHARE), piece),
-        ),
-        out_shape=jax.ShapeDtypeStruct((4, count, SHARE), BF16),
-        compiler_params=pltpu.CompilerParams(vmem_limit_bytes=VMEM_LIMIT),
-        cost_estimate=pl.CostEstimate(flops=2 * count * units * HALF, bytes_accessed=9_000_000, transcendentals=0),
-    )(at, *args)
-
-
-def mix_kernel(at_ref, tok_ref, mix_ref, rows_ref, out_ref):
-    total = tok_ref[...].astype(F32)
-    for source in range(rows_ref.shape[0]):
-        total += jnp.dot(mix_ref[...], rows_ref[source], preferred_element_type=F32)
-    out_ref[...] = total.astype(BF16)
-
-
-def mix(at, tokens, mix_matrix, rows):
+        grid_spec=pltpu.PrefetchScalarGridSpec(num_scalar_prefetch=1, grid=(parts,), in_specs=specs, out_specs=out_specs),
+        out_shape=out_shape,
+        compiler_params=pltpu.CompilerParams(vmem_limit_bytes=MATMUL_VMEM),
+        cost_estimate=pl.CostEstimate(flops=2 * count * units * width * parts, bytes_accessed=6_000_000, transcendentals=0),
+    )(blocks, *args)
+
+
+def mix_kernel(mix_ref, rows_ref, out_ref):
+    out_ref[...] = jnp.dot(mix_ref[...], rows_ref[...], preferred_element_type=F32).astype(BF16)
+
+
+def mix_add_kernel(at_ref, tok_ref, mix_ref, rows_ref, out_ref):
+    total = jnp.dot(mix_ref[...], rows_ref[...], preferred_element_type=F32)
+    out_ref[...] = (tok_ref[...].astype(F32) + total).astype(BF16)
+
+
+def mix(mix_matrix, rows):
+    return pl.pallas_call(
+        mix_kernel,
+        out_shape=jax.ShapeDtypeStruct((TOK_DEV, rows.shape[1]), BF16),
+        compiler_params=pltpu.CompilerParams(vmem_limit_bytes=MATMUL_VMEM),
+        cost_estimate=pl.CostEstimate(flops=2 * TOK_DEV * rows.size, bytes_accessed=2_000_000, transcendentals=0),
+    )(mix_matrix, rows)
+
+
+def mix_add(at, tokens, mix_matrix, rows):
     whole = lambda i, at: (0, 0)
-    return pl.pallas_call(
-        mix_kernel,
+    width = rows.shape[1]
+    return pl.pallas_call(
+        mix_add_kernel,
         grid_spec=pltpu.PrefetchScalarGridSpec(
             num_scalar_prefetch=1,
             grid=(1,),
             in_specs=[
-                pl.BlockSpec((TOK_DEV, SHARE), lambda i, at: (0, at[0])),
+                pl.BlockSpec((TOK_DEV, width), lambda i, at: (0, at[0])),
                 pl.BlockSpec((TOK_DEV, ROWS), whole),
-                pl.BlockSpec(rows.shape, lambda i, at: (0, 0, 0)),
+                pl.BlockSpec(rows.shape, whole),
             ],
-            out_specs=pl.BlockSpec((TOK_DEV, SHARE), whole),
+            out_specs=pl.BlockSpec((TOK_DEV, width), whole),
         ),
-        out_shape=jax.ShapeDtypeStruct((TOK_DEV, SHARE), BF16),
-        compiler_params=pltpu.CompilerParams(vmem_limit_bytes=VMEM_LIMIT),
-        cost_estimate=pl.CostEstimate(flops=8 * TOK_DEV * ROWS * SHARE, bytes_accessed=4_000_000, transcendentals=0),
+        out_shape=jax.ShapeDtypeStruct((TOK_DEV, width), BF16),
+        compiler_params=pltpu.CompilerParams(vmem_limit_bytes=MATMUL_VMEM),
+        cost_estimate=pl.CostEstimate(flops=2 * TOK_DEV * rows.size, bytes_accessed=2_000_000, transcendentals=0),
     )(at, tokens, mix_matrix, rows)
+
+
+def assemble_kernel(at_ref, *refs):
+    pieces, out_ref, sems = refs[:-2], refs[-2], refs[-1]
+    copies = []
+    for i, piece in enumerate(pieces):
+        start = pl.multiple_of(at_ref[i] * 256, 256)
+        copies.append(pltpu.make_async_copy(piece, out_ref.at[:, pl.ds(start, piece.shape[1])], sems.at[i]))
+    for copy in copies:
+        copy.start()
+    for copy in copies:
+        copy.wait()
+
+
+def assemble(at, pieces):
+    return pl.pallas_call(
+        assemble_kernel,
+        in_specs=[pl.BlockSpec(memory_space=pltpu.SMEM)] + [pl.BlockSpec(memory_space=pl.ANY)] * len(pieces),
+        out_specs=pl.BlockSpec(memory_space=pl.ANY),
+        out_shape=jax.ShapeDtypeStruct((TOK_DEV, D), BF16),
+        scratch_shapes=[pltpu.SemaphoreType.DMA((len(pieces),))],
+        compiler_params=pltpu.CompilerParams(vmem_limit_bytes=MATMUL_VMEM),
+        cost_estimate=pl.CostEstimate(flops=0, bytes_accessed=3_000_000, transcendentals=0),
+    )(at, *pieces)
 
 
 def swap(values):
     return lax.ppermute(values, "pp", [(0, 1), (1, 0)])
 
 
-def spread_copies(values, axis):
-    count = lax.axis_size(axis)
-    copies = jnp.broadcast_to(values[None], (count,) + values.shape)
-    return lax.all_to_all(copies, axis, split_axis=0, concat_axis=0, tiled=True)
+def along_z(values, step):
+    count = lax.axis_size("dp")
+    return lax.ppermute(values, "dp", [(i, (i + step) % count) for i in range(count)])
+
+
+def to_experts(rows):
+    width = rows.shape[1]
+    return lax.all_to_all(rows.reshape(EXPERTS, CAP, width), "ep", split_axis=0, concat_axis=0, tiled=True).reshape(ROWS, width)
 
 
 def on_device(tokens, norm_gain, router_weight, expert_ids, up_weight, down_weight):
     core = lax.axis_index("pp").astype(jnp.int32)
-    own, other = core.reshape(1), (1 - core).reshape(1)
-    share = (core * 4 + lax.axis_index("dp").astype(jnp.int32)).reshape(1)
+    z = lax.axis_index("dp").astype(jnp.int32)
+    other = 1 - core
+    steps = jnp.array(Z_STEPS, jnp.int32)
+    ranks = (z + steps) % 4
     up = up_weight.reshape(2, HALF, up_weight.shape[2])
     down = down_weight[0]
 
     outgoing, mix_matrix = route(tokens, norm_gain, router_weight, expert_ids)
-    mine = lax.all_to_all(outgoing.reshape(EXPERTS, CAP, HALF), "ep", split_axis=0, concat_axis=0, tiled=True).reshape(ROWS, HALF)
+    mine = to_experts(outgoing)
     theirs = swap(mine)
-    part = up_half(own, mine, up)
-    hidden = up_half(other, theirs, up, part)
-    got = swap(down_half(other, hidden, down))
-    total = down_half(own, hidden, down, got)
-    returned = lax.all_to_all(
-        total.reshape(4 * EXPERTS, CAP, SHARE), ("dp", "ep"), split_axis=0, concat_axis=0, tiled=True
-    ).reshape(4, ROWS, SHARE)
-    piece = mix(share, tokens, mix_matrix, returned)
-    pieces = spread_copies(spread_copies(piece, "dp"), "pp")
-    return jnp.transpose(pieces, (2, 0, 1, 3)).reshape(TOK_DEV, D)
+    part = up_half(core.reshape(1), mine, up)
+    hidden = up_half(other.reshape(1), theirs, up, part)
+
+    got_wide = swap(down_part((other * 3).reshape(1), hidden, down, WIDE))
+    got_thin = swap(down_part(other * 6 + 2 + ranks, hidden, down, THIN))
+    (wide,) = down_part((core * 3).reshape(1), hidden, down, WIDE, got_wide)
+    thin = down_part(core * 6 + 2 + ranks, hidden, down, THIN, got_thin)
+    thin_sum = thin[0].astype(F32)
+    for piece, step in zip(thin[1:], Z_STEPS[1:]):
+        thin_sum = thin_sum + along_z(piece, step).astype(F32)
+    wide_part = mix(mix_matrix, to_experts(wide))
+    thin_own = mix_add((core * 6 + 2 + z).reshape(1), tokens, mix_matrix, to_experts(thin_sum.astype(BF16)))
+
+    wide_own = lax.dynamic_slice(tokens, (0, core * HALF), (TOK_DEV, WIDE)).astype(F32) + wide_part.astype(F32)
+    for step in Z_STEPS[1:]:
+        wide_own = wide_own + along_z(wide_part, step).astype(F32)
+    wide_own = wide_own.astype(BF16)
+    thin_all = [thin_own] + [along_z(thin_own, step) for step in Z_STEPS[1:]]
+    pieces = [wide_own, swap(wide_own)] + thin_all + [swap(piece) for piece in thin_all]
+    sources = (z - steps) % 4
+    places = jnp.concatenate([jnp.stack([core * 6, other * 6]), core * 6 + 2 + sources, other * 6 + 2 + sources])
+    return assemble(places.astype(jnp.int32), pieces)
 
 
 def solution(mesh):

time: 185 us -> 157 us (0.85)
  waiting for transfers between devices: 51.5 us -> 30.8 us
  blocking collectives: 71.2 us -> 50.7 us
  starting transfers between devices: 10.8 us -> 27.1 us
  Pallas kernels: 41.9 us -> 33.8 us
  other arithmetic: 0 us -> 2.9 us
  local copies, waits for them, and re-layouts: 8.57 us -> 10.9 us
    all_to_all x1 -> x2, waiting for transfers between devices: 45.5 us -> 8.06 us  [to_experts(): lax.all_to_all(rows.reshape(EXPERTS, CAP, width), 'ep', split_axis=0, con...]
    ppermute x0 -> x9, waiting for transfers between devices: none -> 21.3 us  [along_z(): lax.ppermute(values, 'dp', [(i, (i + step) % count) for i in range(count)])]
    all_to_all x3 -> x1, blocking collectives: 71.2 us -> 50.7 us  [to_experts(): lax.all_to_all(rows.reshape(EXPERTS, CAP, width), 'ep', split_axis=0, con...]
    ppermute x0 -> x9, starting transfers between devices: none -> 10.9 us  [along_z(): lax.ppermute(values, 'dp', [(i, (i + step) % count) for i in range(count)])]
    unnamed x6 -> x20, local copies, waits for them, and re-layouts: 3.55 us -> 10.9 us
    pallas_call x2, Pallas kernels: 14.6 us -> 8.94 us  [up_half(): pl.pallas_call(up_first_kernel if part is None else up_second_kernel, gri...]
    ppermute x2 -> x8, starting transfers between devices: 3.61 us -> 8.8 us  [swap(): return lax.ppermute(values, 'pp', [(0, 1), (1, 0)])]
    ppermute x2 -> x8, waiting for transfers between devices: 6.06 us -> 1.44 us  [swap(): return lax.ppermute(values, 'pp', [(0, 1), (1, 0)])]
  transfers between devices with their start and end apart: 3 -> 19, of which waited for: 2 -> 6; matrix products, arithmetic and copies ran while one was open for 0% -> 2% of each run, Pallas kernels for 4% -> 9%
where the time goes in v2:
time: 157 us; the launch traced here: 156 us
  blocking collectives  50.7 us (32%)
  Pallas kernels  33.8 us (22%)
  waiting for transfers between devices  30.8 us (20%)
  starting transfers between devices  27.1 us (17%)
  local copies, waits for them, and re-layouts  10.9 us (7%)
  other arithmetic  2.9 us (2%)
    all_to_all x1, blocking collectives, to_experts(): lax.all_to_all(rows.reshape(EXPERTS, CAP, width), 'ep', split_axis=0, con...  50.7 us
    ppermute x9, waiting for transfers between devices, along_z(): lax.ppermute(values, 'dp', [(i, (i + step) % count) for i in range(count)])  21.3 us
    pallas_call x4, Pallas kernels, down_part(): pl.pallas_call(down_first_kernel if got is None else down_second_kernel,...  14.7 us
    unnamed x20, local copies, waits for them, and re-layouts  10.9 us
    ppermute x9, starting transfers between devices, along_z(): lax.ppermute(values, 'dp', [(i, (i + step) % count) for i in range(count)])  10.9 us
    pallas_call x2, Pallas kernels, up_half(): pl.pallas_call(up_first_kernel if part is None else up_second_kernel, gri...  8.94 us
    ppermute x8, starting transfers between devices, swap(): return lax.ppermute(values, 'pp', [(0, 1), (1, 0)])  8.8 us
    all_to_all x2, waiting for transfers between devices, to_experts(): lax.all_to_all(rows.reshape(EXPERTS, CAP, width), 'ep', split_axis=0, con...  8.06 us
  transfers between devices with their start and end apart: 19, of which 6 were waited for; matrix products, arithmetic and copies ran while one was open for 2% of the time, Pallas kernels for 9%

profile of v2, /device:TPU:1, one launch (start us, length us, event | category | flops | bytes accessed | tf_op | source)
XLA Modules:
  0.0 156.3 jit_solution(7618763849933522221)
XLA Ops:
  0.0 7.5 %shard_map.73 = (bf16[1152,1536]{1,0:T(8,128)(2,1)}, bf16[256,1152]{1,0:T(8,128)(2,1)}) custom-call(bf16[256,3072]{1,0:T(8,128)(2,1)} %tok_ref.3, f32[1,3072]{1,0:T(1,128)} %bitcast.32, bf16[16,3072]{1,0:T(8,128)(2,1)} %bitcast.31, s32[4,256]{1,0:T(4,128)} %bitcast.33), custom_call_target="tpu_custom_call" | custom-call | flops 905969664 | bytes 6000000 | tf_op jit(solution)/shard_map/pallas_call | solution.py:83
  7.5 50.7 %all_to_all.15 = bf16[16,72,1536]{2,1,0:T(8,128)(2,1)S(1)} all-to-all(bf16[16,72,1536]{2,1,0:T(8,128)(2,1)} %bitcast.30), channel_id=1, replica_groups=mesh['pp'=2,'ep'=16,'dp'=4] {'ep'}, dimensions={0} | all-to-all | bytes 7077888 | tf_op jit(solution)/shard_map/all_to_all | solution.py:255
  58.2 1.8 %collective-permute-start = (bf16[1152,1536]{1,0:T(8,128)(2,1)S(1)}, bf16[1152,1536]{1,0:T(8,128)(2,1)}, u32[]{:S(2)}, u32[]{:S(2)}) collective-permute-start(bf16[1152,1536]{1,0:T(8,128)(2,1)S(1)} %bitcast.26), channel_id=1, source_target_pairs={{0,64},{64,0},{1,65},{65,1},{2,66},{66,2},{3,67},{67,3},{4,68},{68... | collective-permute-start | bytes 10616840 | tf_op jit(solution)/shard_map/ppermute | solution.py:245
  60.1 2.3 %copy-done.2 = bf16[1,3072,768]{2,1,0:T(8,128)(2,1)S(1)} copy-done((bf16[1,3072,768]{2,1,0:T(8,128)(2,1)S(1)}, bf16[1,3072,768]{2,1,0:T(8,128)(2,1)}, u32[]{:S(2)}) %copy-start.2) | copy-done | bytes 4718616
  62.4 3.4 %shard_map.74.part_ref = f32[1152,768]{1,0:T(8,128)S(1)} custom-call(s32[1]{0:T(128)} %bitcast.10.at_ref, bf16[1152,1536]{1,0:T(8,128)(2,1)S(1)} %bitcast.27, bf16[2,1536,768]{2,1,0:T(8,128)(2,1)S(1)} %bitcast.24), custom_call_target="tpu_custom_call" | custom-call | flops 2717908992 | bytes 9000000 | tf_op jit(solution)/shard_map/pallas_call | solution.py:128
  66.0 2.5 %copy-done.3 = bf16[1,3072,768]{2,1,0:T(8,128)(2,1)S(1)} copy-done((bf16[1,3072,768]{2,1,0:T(8,128)(2,1)S(1)}, bf16[1,3072,768]{2,1,0:T(8,128)(2,1)}, u32[]{:S(2)}) %copy-start.3) | copy-done | bytes 4718616
  68.5 5.5 %shard_map.75.h_ref = bf16[1152,768]{1,0:T(8,128)(2,1)S(1)} custom-call(s32[1]{0:T(128)} %bitcast.6.at_ref, bf16[1152,1536]{1,0:T(8,128)(2,1)} %collective-permute-done.x_ref, bf16[2,1536,768]{2,1,0:T(8,128)(2,1)S(1)} %bitcast.25, f32[1152,768]{1,0:T(8,128)S(1)} %shard_map.74.part_ref), custom_call_target="tpu_custom_call" | custom-call | flops 2717908992 | bytes 9000000 | tf_op jit(solution)/shard_map/pallas_call | solution.py:128
  74.0 4.3 %shard_map.79 = bf16[4,1152,256]{2,1,0:T(8,128)(2,1)} custom-call(s32[4]{0:T(128)S(1)} %get-tuple-element.17.at_ref, bf16[1152,768]{1,0:T(8,128)(2,1)S(1)} %shard_map.75.h_ref, bf16[768,3072]{1,0:T(8,128)(2,1)S(1)} %bitcast.20), custom_call_target="tpu_custom_call" | custom-call | flops 1811939328 | bytes 6000000 | tf_op jit(solution)/shard_map/pallas_call | solution.py:172
  78.7 2.3 %copy-done = bf16[1,768,3072]{2,1,0:T(8,128)(2,1)S(1)} copy-done((bf16[1,768,3072]{2,1,0:T(8,128)(2,1)S(1)}, bf16[1,768,3072]{2,1,0:T(8,128)(2,1)}, u32[]{:S(2)}) %copy-start) | copy-done | bytes 4718616
  81.1 2.1 %shard_map.76 = bf16[1,1152,512]{2,1,0:T(8,128)(2,1)} custom-call(s32[1]{0:T(128)} %bitcast.12.at_ref, bf16[1152,768]{1,0:T(8,128)(2,1)S(1)} %shard_map.75.h_ref, bf16[768,3072]{1,0:T(8,128)(2,1)S(1)} %bitcast.21), custom_call_target="tpu_custom_call" | custom-call | flops 905969664 | bytes 6000000 | tf_op jit(solution)/shard_map/pallas_call | solution.py:172
  83.3 2.3 %copy-done.1 = bf16[1,768,3072]{2,1,0:T(8,128)(2,1)S(1)} copy-done((bf16[1,768,3072]{2,1,0:T(8,128)(2,1)S(1)}, bf16[1,768,3072]{2,1,0:T(8,128)(2,1)}, u32[]{:S(2)}) %copy-start.1) | copy-done | bytes 4718616
  85.6 6.2 %shard_map.80 = (bf16[1152,256]{1,0:T(8,128)(2,1)S(1)}, bf16[1152,256]{1,0:T(8,128)(2,1)}, bf16[1152,256]{1,0:T(8,128)(2,1)}, bf16[1152,256]{1,0:T(8,128)(2,1)}) custom-call(s32[4]{0:T(128)S(1)} %broadcast_add_fusion.2.at_ref, bf16[1152,768]{1,0:T(8,128)(2,1)S(1)} %shard_map.75.h_ref, bf16[768,3072]{1,0:T(8,128)(2,1)S(1)} %bitcast.22, ...), custom_call_target="tpu_custom_call" | custom-call | flops 1811939328 | bytes 6000000 | tf_op jit(solution)/shard_map/pallas_call | solution.py:172
  91.9 3.8 %collective-permute-start.9 = (bf16[1152,256]{1,0:T(8,128)(2,1)}, bf16[1152,256]{1,0:T(8,128)(2,1)}, u32[]{:S(2)}, u32[]{:S(2)}) collective-permute-start(bf16[1152,256]{1,0:T(8,128)(2,1)} %get-tuple-element.16), channel_id=1, source_target_pairs={{0,3},{1,0},{2,1},{3,2},{4,7},{5,4},{6,5},{7,6},{8,11},{9,8},{10,9... | collective-permute-start | bytes 1769480 | tf_op jit(solution)/shard_map/ppermute | solution.py:250
  96.9 2.1 %shard_map.77 = bf16[1152,512]{1,0:T(8,128)(2,1)} custom-call(s32[1]{0:T(128)} %bitcast.5.at_ref, bf16[1152,768]{1,0:T(8,128)(2,1)S(1)} %shard_map.75.h_ref, bf16[768,3072]{1,0:T(8,128)(2,1)S(1)} %bitcast.23, bf16[1,1152,512]{2,1,0:T(8,128)(2,1)S(1)} %collective-permute-done.1.got_ref), custom_call_target="tpu_custom_call" | custom-call | flops 905969664 | bytes 6000000 | tf_op jit(solution)/shard_map/pallas_call | solution.py:172
  99.0 3.7 %all-to-all-start.1 = ((bf16[16,72,512]{2,1,0:T(8,128)(2,1)}), bf16[16,72,512]{2,1,0:T(8,128)(2,1)S(1)}, u32[]{:S(2)}, u32[]{:S(2)}) async-start(bf16[16,72,512]{2,1,0:T(8,128)(2,1)} %bitcast.13), calls=%async_computation.1 | async-start | bytes 2359296 | tf_op jit(solution)/shard_map/all_to_all | solution.py:255
  102.7 18.2 %collective-permute-done.9 = bf16[1152,256]{1,0:T(8,128)(2,1)} collective-permute-done((bf16[1152,256]{1,0:T(8,128)(2,1)}, bf16[1152,256]{1,0:T(8,128)(2,1)}, u32[]{:S(2)}, u32[]{:S(2)}) %collective-permute-start.9) | collective-permute-done | bytes 589856 | tf_op jit(solution)/shard_map/ppermute | solution.py:250
  120.9 3.1 %collective-permute-done.8 = bf16[1152,256]{1,0:T(8,128)(2,1)} collective-permute-done((bf16[1152,256]{1,0:T(8,128)(2,1)}, bf16[1152,256]{1,0:T(8,128)(2,1)}, u32[]{:S(2)}, u32[]{:S(2)}) %collective-permute-start.8) | collective-permute-done | bytes 589856 | tf_op jit(solution)/shard_map/ppermute | solution.py:250
  124.0 2.6 %add_convert_fusion = bf16[1152,256]{1,0:T(8,128)(2,1)} fusion(bf16[1152,256]{1,0:T(8,128)(2,1)} %collective-permute-done.9, bf16[1152,256]{1,0:T(8,128)(2,1)} %collective-permute-done.8, bf16[1152,256]{1,0:T(8,128)(2,1)} %collective-permute-done.7, bf16[1152,256]{1,0:T(8,128)(2,1)S(1)} %get-tuple-element.13), kind=kLoop, calls=%fused_computation | loop fusion | flops 2359296 | bytes 2949120 | tf_op jit(solution)/shard_map/convert_element_type | solution.py:281
  126.6 3.7 %all-to-all-start.2 = ((bf16[16,72,256]{2,1,0:T(8,128)(2,1)}), bf16[16,72,256]{2,1,0:T(8,128)(2,1)S(1)}, u32[]{:S(2)}, u32[]{:S(2)}) async-start(bf16[16,72,256]{2,1,0:T(8,128)(2,1)} %bitcast.16), calls=%async_computation.2 | async-start | bytes 1179648 | tf_op jit(solution)/shard_map/all_to_all | solution.py:255
  133.0 8.1 %all-to-all-done.2 = bf16[16,72,256]{2,1,0:T(8,128)(2,1)S(1)} async-done(((bf16[16,72,256]{2,1,0:T(8,128)(2,1)}), bf16[16,72,256]{2,1,0:T(8,128)(2,1)S(1)}, u32[]{:S(2)}, u32[]{:S(2)}) %all-to-all-start.2) | async-done | bytes 589856 | tf_op jit(solution)/shard_map/all_to_all | solution.py:255
  144.2 2.4 %collective-permute-start.12 = (bf16[256,256]{1,0:T(8,128)(2,1)S(1)}, bf16[256,256]{1,0:T(8,128)(2,1)S(1)}, u32[]{:S(2)}, u32[]{:S(2)}) collective-permute-start(bf16[256,256]{1,0:T(8,128)(2,1)S(1)} %shard_map.81.refs_2_), channel_id=1, source_target_pairs={{0,3},{1,0},{2,1},{3,2},{4,7},{5,4},{6,5},{7,6},{8,11},{9,8},{10,9... | collective-permute-start | bytes 393224 | tf_op jit(solution)/shard_map/ppermute | solution.py:250
  146.7 3.0 %collective-permute-start.5 = (bf16[256,512]{1,0:T(8,128)(2,1)S(1)}, bf16[256,512]{1,0:T(8,128)(2,1)S(1)}, u32[]{:S(2)}, u32[]{:S(2)}) collective-permute-start(bf16[256,512]{1,0:T(8,128)(2,1)S(1)} %add_convert_fusion.1.refs_0_), channel_id=1, source_target_pairs={{0,64},{64,0},{1,65},{65,1},{2,66},{66,2},{3,67},{67,3},{4,68},{68... | collective-permute-start | bytes 786440 | tf_op jit(solution)/shard_map/ppermute | solution.py:245
  149.8 2.1 %collective-permute-start.14 = (bf16[256,256]{1,0:T(8,128)(2,1)S(1)}, bf16[256,256]{1,0:T(8,128)(2,1)S(1)}, u32[]{:S(2)}, u32[]{:S(2)}) collective-permute-start(bf16[256,256]{1,0:T(8,128)(2,1)S(1)} %collective-permute-done.10.refs_3_), channel_id=1, source_target_pairs={{0,64},{64,0},{1,65},{65,1},{2,66},{66,2},{3,67},{67,3},{4,68},{68... | collective-permute-start | bytes 393224 | tf_op jit(solution)/shard_map/ppermute | solution.py:245
  154.6 1.8 %shard_map.82 = bf16[256,3072]{1,0:T(8,128)(2,1)} custom-call(s32[10]{0:T(128)S(1)} %pad_add_fusion.at_ref, bf16[256,512]{1,0:T(8,128)(2,1)S(1)} %add_convert_fusion.1.refs_0_, bf16[256,512]{1,0:T(8,128)(2,1)S(1)} %collective-permute-done.5.refs_1_, bf16[256,256]{1,0:T(8,128)(2,1)S(1)} %shard_map.81.refs_2_, ...), custom_call_target="tpu_custom_call" | custom-call | bytes 3000000 | tf_op jit(solution)/shard_map/pallas_call | solution.py:233
  (53 shorter events, 10.7 us)
Async XLA Ops:
  7.5 52.5 %copy-start.7 = (s32[4]{0:T(128)S(1)}, s32[4]{0:T(128)}, u32[]{:S(2)}) copy-start(s32[4]{0:T(128)} %constant.44.clone) | copy-start | bytes 52
  58.2 7.8 %collective-permute-start = (bf16[1152,1536]{1,0:T(8,128)(2,1)S(1)}, bf16[1152,1536]{1,0:T(8,128)(2,1)}, u32[]{:S(2)}, u32[]{:S(2)}) collective-permute-start(bf16[1152,1536]{1,0:T(8,128)(2,1)S(1)} %bitcast.26), channel_id=1, source_target_pairs={{0,64},{64,0},{1,65},{65,1},{2,66},{66,2},{3,67},{67,3},{4,68},{68... | collective-permute-start | bytes 10616840 | tf_op jit(solution)/shard_map/ppermute | solution.py:245
  66.0 8.0 %slice-start = ((s8[4718592]{0:T(1024)(128)(4,1)}), s8[4194304]{0:T(1024)(128)(4,1)S(1)}, s32[]{:S(2)}) async-start(s8[4718592]{0:T(1024)(128)(4,1)} %bitcast.18), calls=%async_computation.3 | async-start | bytes 8388608
  68.5 5.5 %slice-start.1 = ((s8[4718592]{0:T(1024)(128)(4,1)}), s8[524288]{0:T(1024)(128)(4,1)S(1)}, s32[]{:S(2)}) async-start(s8[4718592]{0:T(1024)(128)(4,1)} %bitcast.18), calls=%async_computation.4 | async-start | bytes 1048576
  78.3 5.0 %collective-permute-start.6 = (bf16[4,1152,256]{2,1,0:T(8,128)(2,1)}, bf16[4,1152,256]{2,1,0:T(8,128)(2,1)}, u32[]{:S(2)}, u32[]{:S(2)}) collective-permute-start(bf16[4,1152,256]{2,1,0:T(8,128)(2,1)} %shard_map.79), channel_id=1, source_target_pairs={{0,64},{64,0},{1,65},{65,1},{2,66},{66,2},{3,67},{67,3},{4,68},{68... | collective-permute-start | bytes 7077896 | tf_op jit(solution)/shard_map/ppermute | solution.py:245
  83.2 13.8 %collective-permute-start.1 = (bf16[1,1152,512]{2,1,0:T(8,128)(2,1)}, bf16[1,1152,512]{2,1,0:T(8,128)(2,1)S(1)}, u32[]{:S(2)}, u32[]{:S(2)}) collective-permute-start(bf16[1,1152,512]{2,1,0:T(8,128)(2,1)} %shard_map.76), channel_id=1, source_target_pairs={{0,64},{64,0},{1,65},{65,1},{2,66},{66,2},{3,67},{67,3},{4,68},{68... | collective-permute-start | bytes 3538952 | tf_op jit(solution)/shard_map/ppermute | solution.py:245
  91.9 29.1 %collective-permute-start.9 = (bf16[1152,256]{1,0:T(8,128)(2,1)}, bf16[1152,256]{1,0:T(8,128)(2,1)}, u32[]{:S(2)}, u32[]{:S(2)}) collective-permute-start(bf16[1152,256]{1,0:T(8,128)(2,1)} %get-tuple-element.16), channel_id=1, source_target_pairs={{0,3},{1,0},{2,1},{3,2},{4,7},{5,4},{6,5},{7,6},{8,11},{9,8},{10,9... | collective-permute-start | bytes 1769480 | tf_op jit(solution)/shard_map/ppermute | solution.py:250
  95.6 28.4 %collective-permute-start.8 = (bf16[1152,256]{1,0:T(8,128)(2,1)}, bf16[1152,256]{1,0:T(8,128)(2,1)}, u32[]{:S(2)}, u32[]{:S(2)}) collective-permute-start(bf16[1152,256]{1,0:T(8,128)(2,1)} %get-tuple-element.15), channel_id=1, source_target_pairs={{0,1},{1,2},{2,3},{3,0},{4,5},{5,6},{6,7},{7,4},{8,9},{9,10},{10,1... | collective-permute-start | bytes 1769480 | tf_op jit(solution)/shard_map/ppermute | solution.py:250
  95.6 28.4 %collective-permute-start.7 = (bf16[1152,256]{1,0:T(8,128)(2,1)}, bf16[1152,256]{1,0:T(8,128)(2,1)}, u32[]{:S(2)}, u32[]{:S(2)}) collective-permute-start(bf16[1152,256]{1,0:T(8,128)(2,1)} %get-tuple-element.14), channel_id=1, source_target_pairs={{0,2},{1,3},{2,0},{3,1},{4,6},{5,7},{6,4},{7,5},{8,10},{9,11},{10,... | collective-permute-start | bytes 1769480 | tf_op jit(solution)/shard_map/ppermute | solution.py:250
  99.0 27.6 %all-to-all-start.1 = ((bf16[16,72,512]{2,1,0:T(8,128)(2,1)}), bf16[16,72,512]{2,1,0:T(8,128)(2,1)S(1)}, u32[]{:S(2)}, u32[]{:S(2)}) async-start(bf16[16,72,512]{2,1,0:T(8,128)(2,1)} %bitcast.13), calls=%async_computation.1 | async-start | bytes 2359296 | tf_op jit(solution)/shard_map/all_to_all | solution.py:255
  124.0 6.3 %copy-start.4 = (bf16[256,1152]{1,0:T(8,128)(2,1)S(1)}, bf16[256,1152]{1,0:T(8,128)(2,1)}, u32[]{:S(2)}) copy-start(bf16[256,1152]{1,0:T(8,128)(2,1)} %get-tuple-element.11.mix_ref) | copy-start | bytes 1769476
  126.6 6.4 %copy-start.6 = (s32[4]{0:T(128)S(1)}, s32[4]{0:T(128)}, u32[]{:S(2)}) copy-start(s32[4]{0:T(128)} %constant.47) | copy-start | bytes 52
  126.6 14.5 %all-to-all-start.2 = ((bf16[16,72,256]{2,1,0:T(8,128)(2,1)}), bf16[16,72,256]{2,1,0:T(8,128)(2,1)S(1)}, u32[]{:S(2)}, u32[]{:S(2)}) async-start(bf16[16,72,256]{2,1,0:T(8,128)(2,1)} %bitcast.16), calls=%async_computation.2 | async-start | bytes 1179648 | tf_op jit(solution)/shard_map/all_to_all | solution.py:255
  130.9 13.3 %collective-permute-start.4 = (bf16[256,512]{1,0:T(8,128)(2,1)S(1)}, bf16[256,512]{1,0:T(8,128)(2,1)S(1)}, u32[]{:S(2)}, u32[]{:S(2)}) collective-permute-start(bf16[256,512]{1,0:T(8,128)(2,1)S(1)} %shard_map.78), channel_id=1, source_target_pairs={{0,3},{1,0},{2,1},{3,2},{4,7},{5,4},{6,5},{7,6},{8,11},{9,8},{10,9... | collective-permute-start | bytes 786440 | tf_op jit(solution)/shard_map/ppermute | solution.py:250
  131.3 15.3 %collective-permute-start.3 = (bf16[256,512]{1,0:T(8,128)(2,1)S(1)}, bf16[256,512]{1,0:T(8,128)(2,1)S(1)}, u32[]{:S(2)}, u32[]{:S(2)}) collective-permute-start(bf16[256,512]{1,0:T(8,128)(2,1)S(1)} %shard_map.78), channel_id=1, source_target_pairs={{0,1},{1,2},{2,3},{3,0},{4,5},{5,6},{6,7},{7,4},{8,9},{9,10},{10,1... | collective-permute-start | bytes 786440 | tf_op jit(solution)/shard_map/ppermute | solution.py:250
  132.4 14.2 %collective-permute-start.2 = (bf16[256,512]{1,0:T(8,128)(2,1)S(1)}, bf16[256,512]{1,0:T(8,128)(2,1)S(1)}, u32[]{:S(2)}, u32[]{:S(2)}) collective-permute-start(bf16[256,512]{1,0:T(8,128)(2,1)S(1)} %shard_map.78), channel_id=1, source_target_pairs={{0,2},{1,3},{2,0},{3,1},{4,6},{5,7},{6,4},{7,5},{8,10},{9,11},{10,... | collective-permute-start | bytes 786440 | tf_op jit(solution)/shard_map/ppermute | solution.py:250
  142.8 7.0 %collective-permute-start.10 = (bf16[256,256]{1,0:T(8,128)(2,1)S(1)}, bf16[256,256]{1,0:T(8,128)(2,1)S(1)}, u32[]{:S(2)}, u32[]{:S(2)}) collective-permute-start(bf16[256,256]{1,0:T(8,128)(2,1)S(1)} %shard_map.81.refs_2_), channel_id=1, source_target_pairs={{0,2},{1,3},{2,0},{3,1},{4,6},{5,7},{6,4},{7,5},{8,10},{9,11},{10,... | collective-permute-start | bytes 393224 | tf_op jit(solution)/shard_map/ppermute | solution.py:250
  143.9 8.0 %collective-permute-start.11 = (bf16[256,256]{1,0:T(8,128)(2,1)S(1)}, bf16[256,256]{1,0:T(8,128)(2,1)S(1)}, u32[]{:S(2)}, u32[]{:S(2)}) collective-permute-start(bf16[256,256]{1,0:T(8,128)(2,1)S(1)} %shard_map.81.refs_2_), channel_id=1, source_target_pairs={{0,1},{1,2},{2,3},{3,0},{4,5},{5,6},{6,7},{7,4},{8,9},{9,10},{10,1... | collective-permute-start | bytes 393224 | tf_op jit(solution)/shard_map/ppermute | solution.py:250
  144.2 9.1 %collective-permute-start.12 = (bf16[256,256]{1,0:T(8,128)(2,1)S(1)}, bf16[256,256]{1,0:T(8,128)(2,1)S(1)}, u32[]{:S(2)}, u32[]{:S(2)}) collective-permute-start(bf16[256,256]{1,0:T(8,128)(2,1)S(1)} %shard_map.81.refs_2_), channel_id=1, source_target_pairs={{0,3},{1,0},{2,1},{3,2},{4,7},{5,4},{6,5},{7,6},{8,11},{9,8},{10,9... | collective-permute-start | bytes 393224 | tf_op jit(solution)/shard_map/ppermute | solution.py:250
  146.7 6.6 %collective-permute-start.5 = (bf16[256,512]{1,0:T(8,128)(2,1)S(1)}, bf16[256,512]{1,0:T(8,128)(2,1)S(1)}, u32[]{:S(2)}, u32[]{:S(2)}) collective-permute-start(bf16[256,512]{1,0:T(8,128)(2,1)S(1)} %add_convert_fusion.1.refs_0_), channel_id=1, source_target_pairs={{0,64},{64,0},{1,65},{65,1},{2,66},{66,2},{3,67},{67,3},{4,68},{68... | collective-permute-start | bytes 786440 | tf_op jit(solution)/shard_map/ppermute | solution.py:245
  149.7 3.6 %collective-permute-start.13 = (bf16[256,256]{1,0:T(8,128)(2,1)S(1)}, bf16[256,256]{1,0:T(8,128)(2,1)S(1)}, u32[]{:S(2)}, u32[]{:S(2)}) collective-permute-start(bf16[256,256]{1,0:T(8,128)(2,1)S(1)} %shard_map.81.refs_2_), channel_id=1, source_target_pairs={{0,64},{64,0},{1,65},{65,1},{2,66},{66,2},{3,67},{67,3},{4,68},{68... | collective-permute-start | bytes 393224 | tf_op jit(solution)/shard_map/ppermute | solution.py:245
  149.8 3.5 %collective-permute-start.14 = (bf16[256,256]{1,0:T(8,128)(2,1)S(1)}, bf16[256,256]{1,0:T(8,128)(2,1)S(1)}, u32[]{:S(2)}, u32[]{:S(2)}) collective-permute-start(bf16[256,256]{1,0:T(8,128)(2,1)S(1)} %collective-permute-done.10.refs_3_), channel_id=1, source_target_pairs={{0,64},{64,0},{1,65},{65,1},{2,66},{66,2},{3,67},{67,3},{4,68},{68... | collective-permute-start | bytes 393224 | tf_op jit(solution)/shard_map/ppermute | solution.py:245
  151.9 2.3 %collective-permute-start.15 = (bf16[256,256]{1,0:T(8,128)(2,1)S(1)}, bf16[256,256]{1,0:T(8,128)(2,1)S(1)}, u32[]{:S(2)}, u32[]{:S(2)}) collective-permute-start(bf16[256,256]{1,0:T(8,128)(2,1)S(1)} %collective-permute-done.11.refs_4_), channel_id=1, source_target_pairs={{0,64},{64,0},{1,65},{65,1},{2,66},{66,2},{3,67},{67,3},{4,68},{68... | collective-permute-start | bytes 393224 | tf_op jit(solution)/shard_map/ppermute | solution.py:245
  153.2 1.3 collective-permute-start.16
  (5 other events, 10.9 us)

commit v3 on v2

--- a/solution.py
+++ b/solution.py
@@ -14,7 +14,7 @@
 HALF = D // 2
 WIDE = 512
 THIN = 256
-Z_STEPS = (0, 2, 1, 3)
+Z_STEPS = (2, 1, 3, 0)
 EPSILON = 1e-05
 F32 = jnp.float32
 BF16 = jnp.bfloat16
@@ -106,83 +106,19 @@
     )(tokens, norm_gain.reshape(1, D), router_weight.T, expert_ids.T)
 
 
-def up_first_kernel(at_ref, x_ref, w_ref, out_ref):
-    out_ref[...] = jnp.dot(x_ref[...], w_ref[0], preferred_element_type=F32)
-
-
-def up_second_kernel(at_ref, x_ref, w_ref, part_ref, out_ref):
-    value = part_ref[...] + jnp.dot(x_ref[...], w_ref[0], preferred_element_type=F32)
-    out_ref[...] = (value / (1.0 + jnp.exp(-value))).astype(BF16)
-
-
-def up_half(at, rows_in, weight, part=None):
-    count, inner = rows_in.shape
-    units = weight.shape[2]
-    block = count // 4
-    row_block = lambda i, at: (i, 0)
-    specs = [pl.BlockSpec((block, inner), row_block), pl.BlockSpec((1, inner, units), lambda i, at: (at[0], 0, 0))]
-    args = [rows_in, weight]
-    if part is not None:
-        specs.append(pl.BlockSpec((block, units), row_block))
-        args.append(part)
-    return pl.pallas_call(
-        up_first_kernel if part is None else up_second_kernel,
-        grid_spec=pltpu.PrefetchScalarGridSpec(
-            num_scalar_prefetch=1,
-            grid=(4,),
-            in_specs=specs,
-            out_specs=pl.BlockSpec((block, units), row_block),
-        ),
-        out_shape=jax.ShapeDtypeStruct((count, units), F32 if part is None else BF16),
-        compiler_params=pltpu.CompilerParams(vmem_limit_bytes=MATMUL_VMEM),
-        cost_estimate=pl.CostEstimate(flops=2 * count * inner * units, bytes_accessed=9_000_000, transcendentals=0),
-    )(at, *args)
-
-
-def down_first_kernel(at_ref, h_ref, w_ref, out_ref):
-    out_ref[0] = jnp.dot(h_ref[...], w_ref[...], preferred_element_type=F32).astype(BF16)
-
-
-def down_second_kernel(at_ref, h_ref, w_ref, got_ref, *out_refs):
-    value = jnp.dot(h_ref[...], w_ref[...], preferred_element_type=F32)
-    value = (value + got_ref[0].astype(F32)).astype(BF16)
-    for piece, out_ref in enumerate(out_refs):
-
-        @pl.when(pl.program_id(0) == piece)
-        def _(out_ref=out_ref):
-            out_ref[...] = value
-
-
-def down_part(blocks, hidden, weight, width, got=None):
-    count, units = hidden.shape
-    parts = blocks.shape[0]
-    piece = pl.BlockSpec((1, count, width), lambda i, at: (i, 0, 0))
-    specs = [
-        pl.BlockSpec((count, units), lambda i, at: (0, 0)),
-        pl.BlockSpec((units, width), lambda i, at: (0, at[i])),
-    ]
-    args = [hidden, weight]
-    if got is None:
-        out_specs, out_shape = piece, jax.ShapeDtypeStruct((parts, count, width), BF16)
-    else:
-        specs.append(piece)
-        args.append(got)
-        out_specs = [pl.BlockSpec((count, width), lambda i, at: (0, 0))] * parts
-        out_shape = [jax.ShapeDtypeStruct((count, width), BF16)] * parts
-    return pl.pallas_call(
-        down_first_kernel if got is None else down_second_kernel,
-        grid_spec=pltpu.PrefetchScalarGridSpec(num_scalar_prefetch=1, grid=(parts,), in_specs=specs, out_specs=out_specs),
-        out_shape=out_shape,
-        compiler_params=pltpu.CompilerParams(vmem_limit_bytes=MATMUL_VMEM),
-        cost_estimate=pl.CostEstimate(flops=2 * count * units * width * parts, bytes_accessed=6_000_000, transcendentals=0),
-    )(blocks, *args)
+def product(rows, weight):
+    return jnp.dot(rows, weight, preferred_element_type=F32)
+
+
+def columns(weight, start, width):
+    return lax.dynamic_slice_in_dim(weight, start, width, axis=1)
 
 
 def mix_kernel(mix_ref, rows_ref, out_ref):
     out_ref[...] = jnp.dot(mix_ref[...], rows_ref[...], preferred_element_type=F32).astype(BF16)
 
 
-def mix_add_kernel(at_ref, tok_ref, mix_ref, rows_ref, out_ref):
+def mix_add_kernel(tok_ref, mix_ref, rows_ref, out_ref):
     total = jnp.dot(mix_ref[...], rows_ref[...], preferred_element_type=F32)
     out_ref[...] = (tok_ref[...].astype(F32) + total).astype(BF16)
 
@@ -196,25 +132,13 @@
     )(mix_matrix, rows)
 
 
-def mix_add(at, tokens, mix_matrix, rows):
-    whole = lambda i, at: (0, 0)
-    width = rows.shape[1]
+def mix_add(tokens, mix_matrix, rows):
     return pl.pallas_call(
         mix_add_kernel,
-        grid_spec=pltpu.PrefetchScalarGridSpec(
-            num_scalar_prefetch=1,
-            grid=(1,),
-            in_specs=[
-                pl.BlockSpec((TOK_DEV, width), lambda i, at: (0, at[0])),
-                pl.BlockSpec((TOK_DEV, ROWS), whole),
-                pl.BlockSpec(rows.shape, whole),
-            ],
-            out_specs=pl.BlockSpec((TOK_DEV, width), whole),
-        ),
-        out_shape=jax.ShapeDtypeStruct((TOK_DEV, width), BF16),
+        out_shape=jax.ShapeDtypeStruct((TOK_DEV, rows.shape[1]), BF16),
         compiler_params=pltpu.CompilerParams(vmem_limit_bytes=MATMUL_VMEM),
         cost_estimate=pl.CostEstimate(flops=2 * TOK_DEV * rows.size, bytes_accessed=2_000_000, transcendentals=0),
-    )(at, tokens, mix_matrix, rows)
+    )(tokens, mix_matrix, rows)
 
 
 def assemble_kernel(at_ref, *refs):
@@ -259,34 +183,37 @@
     core = lax.axis_index("pp").astype(jnp.int32)
     z = lax.axis_index("dp").astype(jnp.int32)
     other = 1 - core
-    steps = jnp.array(Z_STEPS, jnp.int32)
-    ranks = (z + steps) % 4
     up = up_weight.reshape(2, HALF, up_weight.shape[2])
     down = down_weight[0]
 
     outgoing, mix_matrix = route(tokens, norm_gain, router_weight, expert_ids)
+    token_wide = lax.dynamic_slice(tokens, (0, core * HALF), (TOK_DEV, WIDE))
+    token_thin = lax.dynamic_slice(tokens, (0, core * HALF + WIDE + z * THIN), (TOK_DEV, THIN))
+    token_wide, token_thin = lax.optimization_barrier((token_wide, token_thin))
     mine = to_experts(outgoing)
     theirs = swap(mine)
-    part = up_half(core.reshape(1), mine, up)
-    hidden = up_half(other.reshape(1), theirs, up, part)
-
-    got_wide = swap(down_part((other * 3).reshape(1), hidden, down, WIDE))
-    got_thin = swap(down_part(other * 6 + 2 + ranks, hidden, down, THIN))
-    (wide,) = down_part((core * 3).reshape(1), hidden, down, WIDE, got_wide)
-    thin = down_part(core * 6 + 2 + ranks, hidden, down, THIN, got_thin)
-    thin_sum = thin[0].astype(F32)
-    for piece, step in zip(thin[1:], Z_STEPS[1:]):
+    hidden = jax.nn.silu(product(mine, up[core]) + product(theirs, up[other])).astype(BF16)
+
+    def partial_sums(start, width):
+        got = swap(product(hidden, columns(down, other * HALF + start, width)).astype(BF16))
+        return (product(hidden, columns(down, core * HALF + start, width)) + got.astype(F32)).astype(BF16)
+
+    thin = [partial_sums(WIDE + rank * THIN, THIN) for rank in [(z + step) % 4 for step in Z_STEPS]]
+    wide = partial_sums(0, WIDE)
+    thin_sum = thin[-1].astype(F32)
+    for piece, step in zip(thin[:-1], Z_STEPS[:-1]):
         thin_sum = thin_sum + along_z(piece, step).astype(F32)
-    wide_part = mix(mix_matrix, to_experts(wide))
-    thin_own = mix_add((core * 6 + 2 + z).reshape(1), tokens, mix_matrix, to_experts(thin_sum.astype(BF16)))
-
-    wide_own = lax.dynamic_slice(tokens, (0, core * HALF), (TOK_DEV, WIDE)).astype(F32) + wide_part.astype(F32)
-    for step in Z_STEPS[1:]:
+    wide_rows, thin_sum = lax.optimization_barrier((to_experts(wide), thin_sum.astype(BF16)))
+    wide_part = mix(mix_matrix, wide_rows)
+    thin_own = mix_add(token_thin, mix_matrix, to_experts(thin_sum))
+
+    wide_own = token_wide.astype(F32) + wide_part.astype(F32)
+    for step in Z_STEPS[:-1]:
         wide_own = wide_own + along_z(wide_part, step).astype(F32)
     wide_own = wide_own.astype(BF16)
-    thin_all = [thin_own] + [along_z(thin_own, step) for step in Z_STEPS[1:]]
+    thin_all = [along_z(thin_own, step) for step in Z_STEPS[:-1]] + [thin_own]
     pieces = [wide_own, swap(wide_own)] + thin_all + [swap(piece) for piece in thin_all]
-    sources = (z - steps) % 4
+    sources = (z - jnp.array(Z_STEPS, jnp.int32)) % 4
     places = jnp.concatenate([jnp.stack([core * 6, other * 6]), core * 6 + 2 + sources, other * 6 + 2 + sources])
     return assemble(places.astype(jnp.int32), pieces)
 

time: 157 us -> 146 us (0.930)
  Pallas kernels: 33.8 us -> 10.1 us
  matrix products: 0 us -> 23.3 us
  local copies, waits for them, and re-layouts: 10.9 us -> 1.9 us
  waiting for transfers between devices: 30.8 us -> 28.3 us
    pallas_call x7 -> x1, Pallas kernels: 24 us -> 0.34 us  [mix_add(): pl.pallas_call(mix_add_kernel, out_shape=jax.ShapeDtypeStruct((TOK_DEV, r...]
    dot_general x0 -> x12, matrix products: none -> 23.3 us  [product(): return jnp.dot(rows, weight, preferred_element_type=F32)]
    unnamed x20 -> x8, local copies, waits for them, and re-layouts: 10.9 us -> 0.02 us
    dynamic_slice x0 -> x2, local copies, waits for them, and re-layouts: none -> 1.89 us  [the longest x1 0.97 us: on_device(): token_wide = lax.dynamic_slice(tokens, (0, core * HALF), (TOK_DEV, WIDE))]
    ppermute x9, waiting for transfers between devices: 21.3 us -> 19.4 us  [along_z(): lax.ppermute(values, 'dp', [(i, (i + step) % count) for i in range(count)])]
    all_to_all x2, waiting for transfers between devices: 8.06 us -> 6.4 us  [to_experts(): lax.all_to_all(rows.reshape(EXPERTS, CAP, width), 'ep', split_axis=0, con...]
    ppermute x8 -> x11, starting transfers between devices: 8.8 us -> 10.4 us  [swap(): return lax.ppermute(values, 'pp', [(0, 1), (1, 0)])]
  transfers between devices with their start and end apart: 19 -> 22, of which waited for: 6 -> 7; matrix products, arithmetic and copies ran while one was open for 2% -> 14% of each run, Pallas kernels for 9% -> 1%
where the time goes in v3:
time: 146 us
  blocking collectives  50.5 us (35%)
  starting transfers between devices  28.4 us (19%)
  waiting for transfers between devices  28.3 us (19%)
  matrix products  23.3 us (16%)
  Pallas kernels  10.1 us (7%)
  other arithmetic  2.9 us (2%)
  local copies, waits for them, and re-layouts  1.9 us (1%)
    all_to_all x1, blocking collectives, to_experts(): lax.all_to_all(rows.reshape(EXPERTS, CAP, width), 'ep', split_axis=0, con...  50.5 us
    dot_general x12, matrix products, product(): return jnp.dot(rows, weight, preferred_element_type=F32)  23.3 us
    ppermute x9, waiting for transfers between devices, along_z(): lax.ppermute(values, 'dp', [(i, (i + step) % count) for i in range(count)])  19.4 us
    ppermute x9, starting transfers between devices, along_z(): lax.ppermute(values, 'dp', [(i, (i + step) % count) for i in range(count)])  10.6 us
    ppermute x11, starting transfers between devices, swap(): return lax.ppermute(values, 'pp', [(0, 1), (1, 0)])  10.4 us
    pallas_call x1, Pallas kernels, route(): pl.pallas_call(route_kernel, grid=(steps,), in_specs=[pl.BlockSpec((TOK_D...  7.51 us
    all_to_all x2, starting transfers between devices, to_experts(): lax.all_to_all(rows.reshape(EXPERTS, CAP, width), 'ep', split_axis=0, con...  7.43 us
    all_to_all x2, waiting for transfers between devices, to_experts(): lax.all_to_all(rows.reshape(EXPERTS, CAP, width), 'ep', split_axis=0, con...  6.4 us
  transfers between devices with their start and end apart: 22, of which 7 were waited for; matrix products, arithmetic and copies ran while one was open for 14% of the time, Pallas kernels for 1%

profile of v3, /device:TPU:1, one launch (start us, length us, event | category | flops | bytes accessed | tf_op | source)
XLA Modules:
  0.0 145.9 jit_solution(15100650905973322610)
XLA Ops:
  0.0 7.5 %shard_map.73 = (bf16[1152,1536]{1,0:T(8,128)(2,1)}, bf16[256,1152]{1,0:T(8,128)(2,1)}) custom-call(bf16[256,3072]{1,0:T(8,128)(2,1)} %tok_ref.1, f32[1,3072]{1,0:T(1,128)} %bitcast.79, bf16[16,3072]{1,0:T(8,128)(2,1)} %bitcast.78, s32[4,256]{1,0:T(4,128)} %bitcast.80), custom_call_target="tpu_custom_call" | custom-call | flops 905969664 | bytes 6000000 | tf_op jit(solution)/shard_map/pallas_call | solution.py:83
  7.5 50.5 %all_to_all.15 = bf16[16,72,1536]{2,1,0:T(8,128)(2,1)S(1)} all-to-all(bf16[16,72,1536]{2,1,0:T(8,128)(2,1)} %bitcast.72), channel_id=1, replica_groups=mesh['pp'=2,'ep'=16,'dp'=4] {'ep'}, dimensions={0} | all-to-all | bytes 7077888 | tf_op jit(solution)/shard_map/all_to_all | solution.py:179
  58.1 1.8 %collective-permute-start = (bf16[1152,1536]{1,0:T(8,128)(2,1)S(1)}, bf16[1152,1536]{1,0:T(8,128)(2,1)}, u32[]{:S(2)}, u32[]{:S(2)}) collective-permute-start(bf16[1152,1536]{1,0:T(8,128)(2,1)S(1)} %bitcast.70), channel_id=1, source_target_pairs={{0,64},{64,0},{1,65},{65,1},{2,66},{66,2},{3,67},{67,3},{4,68},{68... | collective-permute-start | bytes 10616840 | tf_op jit(solution)/shard_map/ppermute | solution.py:169
  59.9 4.7 %fusion.1 = f32[1152,768]{1,0:T(8,128)S(1)} fusion(bf16[1152,1536]{1,0:T(8,128)(2,1)S(1)} %bitcast.71, bf16[2,1536,768]{2,1,0:T(8,128)(2,1)} %bitcast.76, s32[]{:T(128)S(6)} %select_n.68), kind=kOutput, calls=%fused_computation.8 | convolution fusion | flops 2717908992 | bytes 9437188 | tf_op jit(solution)/shard_map/dot_general | solution.py:110
  64.6 1.2 collective-permute-done
  65.9 6.0 %multiply_convert_fusion = bf16[1152,768]{1,0:T(8,128)(2,1)S(1)} fusion(f32[1152,768]{1,0:T(8,128)S(1)} %fusion.1, bf16[1152,1536]{1,0:T(8,128)(2,1)} %collective-permute-done, bf16[2,1536,768]{2,1,0:T(8,128)(2,1)} %bitcast.77, s32[]{:T(128)S(6)} %select_n.69), kind=kOutput, calls=%fused_computation.1 | convolution fusion | flops 2723217408 | bytes 11206660 | tf_op jit(solution)/shard_map/dot_general | solution.py:110
  76.2 1.5 convolution_convert_fusion.4
  78.1 1.5 %add_convert_fusion.2 = bf16[1152,256]{1,0:T(8,128)(2,1)} fusion(bf16[1152,256]{1,0:T(8,128)(2,1)S(1)} %collective-permute-done.7, bf16[1152,768]{1,0:T(8,128)(2,1)S(1)} %multiply_convert_fusion, bf16[1,768,3072]{2,1,0:T(8,128)(2,1)S(1)} %bitcast.75, s32[]{:T(128)S(6)} %select_n.81), kind=kOutput, calls=%fused_computation.14 | convolution fusion | flops 453869568 | bytes 3342340 | tf_op jit(solution)/shard_map/dot_general | solution.py:110
  79.6 3.7 %collective-permute-start.8 = (bf16[1152,256]{1,0:T(8,128)(2,1)}, bf16[1152,256]{1,0:T(8,128)(2,1)}, u32[]{:S(2)}, u32[]{:S(2)}) collective-permute-start(bf16[1152,256]{1,0:T(8,128)(2,1)} %add_convert_fusion.2), channel_id=1, source_target_pairs={{0,3},{1,0},{2,1},{3,2},{4,7},{5,4},{6,5},{7,6},{8,11},{9,8},{10,9... | collective-permute-start | bytes 1769480 | tf_op jit(solution)/shard_map/ppermute | solution.py:174
  83.3 1.5 add_convert_fusion.3
  84.8 1.5 %add_convert_fusion.4 = bf16[1152,256]{1,0:T(8,128)(2,1)} fusion(bf16[1152,256]{1,0:T(8,128)(2,1)S(1)} %collective-permute-done.3, bf16[1152,768]{1,0:T(8,128)(2,1)S(1)} %multiply_convert_fusion, bf16[1,768,3072]{2,1,0:T(8,128)(2,1)S(1)} %bitcast.75, s32[]{:T(128)S(6)} %select_n.75), kind=kOutput, calls=%fused_computation.16 | convolution fusion | flops 453869568 | bytes 3342340 | tf_op jit(solution)/shard_map/dot_general | solution.py:110
  86.2 1.3 collective-permute-start.4
  87.6 2.1 %add_convert_fusion = bf16[1152,512]{1,0:T(8,128)(2,1)} fusion(bf16[1152,512]{1,0:T(8,128)(2,1)S(1)} %collective-permute-done.1, bf16[1152,768]{1,0:T(8,128)(2,1)S(1)} %multiply_convert_fusion, bf16[1,768,3072]{2,1,0:T(8,128)(2,1)S(1)} %bitcast.75, s32[]{:T(128)S(6)} %select_n.66), kind=kOutput, calls=%fused_computation.10 | convolution fusion | flops 907739136 | bytes 4915204 | tf_op jit(solution)/shard_map/dot_general | solution.py:110
  89.7 3.7 %all-to-all-start.1 = ((bf16[16,72,512]{2,1,0:T(8,128)(2,1)}), bf16[16,72,512]{2,1,0:T(8,128)(2,1)S(1)}, u32[]{:S(2)}, u32[]{:S(2)}) async-start(bf16[16,72,512]{2,1,0:T(8,128)(2,1)} %bitcast.73), calls=%async_computation.1 | async-start | bytes 2359296 | tf_op jit(solution)/shard_map/all_to_all | solution.py:179
  93.4 1.6 %fusion.28 = f32[1152,256]{1,0:T(8,128)S(1)} fusion(bf16[1152,768]{1,0:T(8,128)(2,1)S(1)} %multiply_convert_fusion, bf16[1,768,3072]{2,1,0:T(8,128)(2,1)} %param.12, s32[]{:T(128)S(6)} %select_n.72), kind=kOutput, calls=%fused_computation.34 | convolution fusion | flops 452984832 | bytes 3342340 | tf_op jit(solution)/shard_map/dot_general | solution.py:110
  95.1 13.8 %collective-permute-done.8 = bf16[1152,256]{1,0:T(8,128)(2,1)} collective-permute-done((bf16[1152,256]{1,0:T(8,128)(2,1)}, bf16[1152,256]{1,0:T(8,128)(2,1)}, u32[]{:S(2)}, u32[]{:S(2)}) %collective-permute-start.8) | collective-permute-done | bytes 589856 | tf_op jit(solution)/shard_map/ppermute | solution.py:174
  108.8 4.5 %collective-permute-done.6 = bf16[1152,256]{1,0:T(8,128)(2,1)} collective-permute-done((bf16[1152,256]{1,0:T(8,128)(2,1)}, bf16[1152,256]{1,0:T(8,128)(2,1)}, u32[]{:S(2)}, u32[]{:S(2)}) %collective-permute-start.6) | collective-permute-done | bytes 589856 | tf_op jit(solution)/shard_map/ppermute | solution.py:174
  113.4 2.6 %add_convert_fusion.1 = bf16[1152,256]{1,0:T(8,128)(2,1)} fusion(bf16[1152,256]{1,0:T(8,128)(2,1)} %collective-permute-done.8, bf16[1152,256]{1,0:T(8,128)(2,1)} %collective-permute-done.6, bf16[1152,256]{1,0:T(8,128)(2,1)} %collective-permute-done.4, f32[1152,256]{1,0:T(8,128)S(1)} %fusion.28, bf16[1152,256]{1,0:T(8,128)(2,1)S(1)} %collective-permute-done.2), kind=kLoop, calls=%fused_computation.13 | loop fusion | flops 3244032 | bytes 4128768 | tf_op jit(solution)/shard_map/convert_element_type | solution.py:206
  116.0 3.7 %all-to-all-start.2 = ((bf16[16,72,256]{2,1,0:T(8,128)(2,1)}), bf16[16,72,256]{2,1,0:T(8,128)(2,1)S(1)}, u32[]{:S(2)}, u32[]{:S(2)}) async-start(bf16[16,72,256]{2,1,0:T(8,128)(2,1)} %bitcast.22), calls=%async_computation.2 | async-start | bytes 1179648 | tf_op jit(solution)/shard_map/all_to_all | solution.py:179
  121.4 1.5 collective-permute-start.10
  124.4 6.4 %all-to-all-done.2 = bf16[16,72,256]{2,1,0:T(8,128)(2,1)S(1)} async-done(((bf16[16,72,256]{2,1,0:T(8,128)(2,1)}), bf16[16,72,256]{2,1,0:T(8,128)(2,1)S(1)}, u32[]{:S(2)}, u32[]{:S(2)}) %all-to-all-start.2) | async-done | bytes 589856 | tf_op jit(solution)/shard_map/all_to_all | solution.py:179
  131.8 2.7 %collective-permute-start.15 = (bf16[256,256]{1,0:T(8,128)(2,1)S(1)}, bf16[256,256]{1,0:T(8,128)(2,1)S(1)}, u32[]{:S(2)}, u32[]{:S(2)}) collective-permute-start(bf16[256,256]{1,0:T(8,128)(2,1)S(1)} %shard_map.75.refs_5_), channel_id=1, source_target_pairs={{0,3},{1,0},{2,1},{3,2},{4,7},{5,4},{6,5},{7,6},{8,11},{9,8},{10,9... | collective-permute-start | bytes 393224 | tf_op jit(solution)/shard_map/ppermute | solution.py:174
  134.7 4.8 %collective-permute-start.12 = (bf16[256,512]{1,0:T(8,128)(2,1)S(1)}, bf16[256,512]{1,0:T(8,128)(2,1)S(1)}, u32[]{:S(2)}, u32[]{:S(2)}) collective-permute-start(bf16[256,512]{1,0:T(8,128)(2,1)S(1)} %add_convert_fusion.6.refs_0_), channel_id=1, source_target_pairs={{0,64},{64,0},{1,65},{65,1},{2,66},{66,2},{3,67},{67,3},{4,68},{68... | collective-permute-start | bytes 786440 | tf_op jit(solution)/shard_map/ppermute | solution.py:169
  143.9 1.8 %shard_map.76 = bf16[256,3072]{1,0:T(8,128)(2,1)} custom-call(s32[10]{0:T(128)S(1)} %pad_add_fusion.at_ref, bf16[256,512]{1,0:T(8,128)(2,1)S(1)} %add_convert_fusion.6.refs_0_, bf16[256,512]{1,0:T(8,128)(2,1)S(1)} %collective-permute-done.12.refs_1_, bf16[256,256]{1,0:T(8,128)(2,1)S(1)} %collective-permute-done.13.refs_2_, ...), custom_call_target="tpu_custom_call" | custom-call | bytes 3000000 | tf_op jit(solution)/shard_map/pallas_call | solution.py:157
  (53 shorter events, 13.5 us)
Async XLA Ops:
  58.1 7.8 %collective-permute-start = (bf16[1152,1536]{1,0:T(8,128)(2,1)S(1)}, bf16[1152,1536]{1,0:T(8,128)(2,1)}, u32[]{:S(2)}, u32[]{:S(2)}) collective-permute-start(bf16[1152,1536]{1,0:T(8,128)(2,1)S(1)} %bitcast.70), channel_id=1, source_target_pairs={{0,64},{64,0},{1,65},{65,1},{2,66},{66,2},{3,67},{67,3},{4,68},{68... | collective-permute-start | bytes 10616840 | tf_op jit(solution)/shard_map/ppermute | solution.py:169
  59.9 12.0 %slice-start = ((s8[4718592]{0:T(1024)(128)(4,1)}), s8[4194304]{0:T(1024)(128)(4,1)S(1)}, s32[]{:S(2)}) async-start(s8[4718592]{0:T(1024)(128)(4,1)} %bitcast.74), calls=%async_computation.3 | async-start | bytes 8388608
  73.0 14.6 %collective-permute-start.1 = (bf16[1152,512]{1,0:T(8,128)(2,1)S(1)}, bf16[1152,512]{1,0:T(8,128)(2,1)S(1)}, u32[]{:S(2)}, u32[]{:S(2)}) collective-permute-start(bf16[1152,512]{1,0:T(8,128)(2,1)S(1)} %convolution_convert_fusion), channel_id=1, source_target_pairs={{0,64},{64,0},{1,65},{65,1},{2,66},{66,2},{3,67},{67,3},{4,68},{68... | collective-permute-start | bytes 3538952 | tf_op jit(solution)/shard_map/ppermute | solution.py:169
  74.1 4.0 %collective-permute-start.7 = (bf16[1152,256]{1,0:T(8,128)(2,1)S(1)}, bf16[1152,256]{1,0:T(8,128)(2,1)S(1)}, u32[]{:S(2)}, u32[]{:S(2)}) collective-permute-start(bf16[1152,256]{1,0:T(8,128)(2,1)S(1)} %convolution_convert_fusion.1), channel_id=1, source_target_pairs={{0,64},{64,0},{1,65},{65,1},{2,66},{66,2},{3,67},{67,3},{4,68},{68... | collective-permute-start | bytes 1769480 | tf_op jit(solution)/shard_map/ppermute | solution.py:169
  74.9 8.4 %collective-permute-start.5 = (bf16[1152,256]{1,0:T(8,128)(2,1)S(1)}, bf16[1152,256]{1,0:T(8,128)(2,1)S(1)}, u32[]{:S(2)}, u32[]{:S(2)}) collective-permute-start(bf16[1152,256]{1,0:T(8,128)(2,1)S(1)} %convolution_convert_fusion.2), channel_id=1, source_target_pairs={{0,64},{64,0},{1,65},{65,1},{2,66},{66,2},{3,67},{67,3},{4,68},{68... | collective-permute-start | bytes 1769480 | tf_op jit(solution)/shard_map/ppermute | solution.py:169
  76.0 8.7 %collective-permute-start.3 = (bf16[1152,256]{1,0:T(8,128)(2,1)S(1)}, bf16[1152,256]{1,0:T(8,128)(2,1)S(1)}, u32[]{:S(2)}, u32[]{:S(2)}) collective-permute-start(bf16[1152,256]{1,0:T(8,128)(2,1)S(1)} %convolution_convert_fusion.3), channel_id=1, source_target_pairs={{0,64},{64,0},{1,65},{65,1},{2,66},{66,2},{3,67},{67,3},{4,68},{68... | collective-permute-start | bytes 1769480 | tf_op jit(solution)/shard_map/ppermute | solution.py:169
  77.7 17.4 %collective-permute-start.2 = (bf16[1152,256]{1,0:T(8,128)(2,1)}, bf16[1152,256]{1,0:T(8,128)(2,1)S(1)}, u32[]{:S(2)}, u32[]{:S(2)}) collective-permute-start(bf16[1152,256]{1,0:T(8,128)(2,1)} %convolution_convert_fusion.4), channel_id=1, source_target_pairs={{0,64},{64,0},{1,65},{65,1},{2,66},{66,2},{3,67},{67,3},{4,68},{68... | collective-permute-start | bytes 1769480 | tf_op jit(solution)/shard_map/ppermute | solution.py:169
  79.6 29.3 %collective-permute-start.8 = (bf16[1152,256]{1,0:T(8,128)(2,1)}, bf16[1152,256]{1,0:T(8,128)(2,1)}, u32[]{:S(2)}, u32[]{:S(2)}) collective-permute-start(bf16[1152,256]{1,0:T(8,128)(2,1)} %add_convert_fusion.2), channel_id=1, source_target_pairs={{0,3},{1,0},{2,1},{3,2},{4,7},{5,4},{6,5},{7,6},{8,11},{9,8},{10,9... | collective-permute-start | bytes 1769480 | tf_op jit(solution)/shard_map/ppermute | solution.py:174
  84.8 28.6 %collective-permute-start.6 = (bf16[1152,256]{1,0:T(8,128)(2,1)}, bf16[1152,256]{1,0:T(8,128)(2,1)}, u32[]{:S(2)}, u32[]{:S(2)}) collective-permute-start(bf16[1152,256]{1,0:T(8,128)(2,1)} %add_convert_fusion.3), channel_id=1, source_target_pairs={{0,1},{1,2},{2,3},{3,0},{4,5},{5,6},{6,7},{7,4},{8,9},{9,10},{10,1... | collective-permute-start | bytes 1769480 | tf_op jit(solution)/shard_map/ppermute | solution.py:174
  86.2 27.1 %collective-permute-start.4 = (bf16[1152,256]{1,0:T(8,128)(2,1)}, bf16[1152,256]{1,0:T(8,128)(2,1)}, u32[]{:S(2)}, u32[]{:S(2)}) collective-permute-start(bf16[1152,256]{1,0:T(8,128)(2,1)} %add_convert_fusion.4), channel_id=1, source_target_pairs={{0,2},{1,3},{2,0},{3,1},{4,6},{5,7},{6,4},{7,5},{8,10},{9,11},{10,... | collective-permute-start | bytes 1769480 | tf_op jit(solution)/shard_map/ppermute | solution.py:174
  89.7 26.3 %all-to-all-start.1 = ((bf16[16,72,512]{2,1,0:T(8,128)(2,1)}), bf16[16,72,512]{2,1,0:T(8,128)(2,1)S(1)}, u32[]{:S(2)}, u32[]{:S(2)}) async-start(bf16[16,72,512]{2,1,0:T(8,128)(2,1)} %bitcast.73), calls=%async_computation.1 | async-start | bytes 2359296 | tf_op jit(solution)/shard_map/all_to_all | solution.py:179
  116.0 8.3 %copy-start.1 = (s32[4]{0:T(128)S(1)}, s32[4]{0:T(128)}, u32[]{:S(2)}) copy-start(s32[4]{0:T(128)} %constant.78) | copy-start | bytes 52
  116.0 14.7 %all-to-all-start.2 = ((bf16[16,72,256]{2,1,0:T(8,128)(2,1)}), bf16[16,72,256]{2,1,0:T(8,128)(2,1)S(1)}, u32[]{:S(2)}, u32[]{:S(2)}) async-start(bf16[16,72,256]{2,1,0:T(8,128)(2,1)} %bitcast.22), calls=%async_computation.2 | async-start | bytes 1179648 | tf_op jit(solution)/shard_map/all_to_all | solution.py:179
  121.3 10.6 %collective-permute-start.11 = (bf16[256,512]{1,0:T(8,128)(2,1)S(1)}, bf16[256,512]{1,0:T(8,128)(2,1)S(1)}, u32[]{:S(2)}, u32[]{:S(2)}) collective-permute-start(bf16[256,512]{1,0:T(8,128)(2,1)S(1)} %shard_map.74), channel_id=1, source_target_pairs={{0,3},{1,0},{2,1},{3,2},{4,7},{5,4},{6,5},{7,6},{8,11},{9,8},{10,9... | collective-permute-start | bytes 786440 | tf_op jit(solution)/shard_map/ppermute | solution.py:174
  121.4 13.2 %collective-permute-start.10 = (bf16[256,512]{1,0:T(8,128)(2,1)S(1)}, bf16[256,512]{1,0:T(8,128)(2,1)S(1)}, u32[]{:S(2)}, u32[]{:S(2)}) collective-permute-start(bf16[256,512]{1,0:T(8,128)(2,1)S(1)} %shard_map.74), channel_id=1, source_target_pairs={{0,1},{1,2},{2,3},{3,0},{4,5},{5,6},{6,7},{7,4},{8,9},{9,10},{10,1... | collective-permute-start | bytes 786440 | tf_op jit(solution)/shard_map/ppermute | solution.py:174
  122.8 11.7 %collective-permute-start.9 = (bf16[256,512]{1,0:T(8,128)(2,1)S(1)}, bf16[256,512]{1,0:T(8,128)(2,1)S(1)}, u32[]{:S(2)}, u32[]{:S(2)}) collective-permute-start(bf16[256,512]{1,0:T(8,128)(2,1)S(1)} %shard_map.74), channel_id=1, source_target_pairs={{0,2},{1,3},{2,0},{3,1},{4,6},{5,7},{6,4},{7,5},{8,10},{9,11},{10,... | collective-permute-start | bytes 786440 | tf_op jit(solution)/shard_map/ppermute | solution.py:174
  131.1 8.5 %collective-permute-start.13 = (bf16[256,256]{1,0:T(8,128)(2,1)S(1)}, bf16[256,256]{1,0:T(8,128)(2,1)S(1)}, u32[]{:S(2)}, u32[]{:S(2)}) collective-permute-start(bf16[256,256]{1,0:T(8,128)(2,1)S(1)} %shard_map.75.refs_5_), channel_id=1, source_target_pairs={{0,2},{1,3},{2,0},{3,1},{4,6},{5,7},{6,4},{7,5},{8,10},{9,11},{10,... | collective-permute-start | bytes 393224 | tf_op jit(solution)/shard_map/ppermute | solution.py:174
  131.8 9.8 %collective-permute-start.14 = (bf16[256,256]{1,0:T(8,128)(2,1)S(1)}, bf16[256,256]{1,0:T(8,128)(2,1)S(1)}, u32[]{:S(2)}, u32[]{:S(2)}) collective-permute-start(bf16[256,256]{1,0:T(8,128)(2,1)S(1)} %shard_map.75.refs_5_), channel_id=1, source_target_pairs={{0,1},{1,2},{2,3},{3,0},{4,5},{5,6},{6,7},{7,4},{8,9},{9,10},{10,1... | collective-permute-start | bytes 393224 | tf_op jit(solution)/shard_map/ppermute | solution.py:174
  131.8 10.7 %collective-permute-start.15 = (bf16[256,256]{1,0:T(8,128)(2,1)S(1)}, bf16[256,256]{1,0:T(8,128)(2,1)S(1)}, u32[]{:S(2)}, u32[]{:S(2)}) collective-permute-start(bf16[256,256]{1,0:T(8,128)(2,1)S(1)} %shard_map.75.refs_5_), channel_id=1, source_target_pairs={{0,3},{1,0},{2,1},{3,2},{4,7},{5,4},{6,5},{7,6},{8,11},{9,8},{10,9... | collective-permute-start | bytes 393224 | tf_op jit(solution)/shard_map/ppermute | solution.py:174
  134.7 8.0 %collective-permute-start.12 = (bf16[256,512]{1,0:T(8,128)(2,1)S(1)}, bf16[256,512]{1,0:T(8,128)(2,1)S(1)}, u32[]{:S(2)}, u32[]{:S(2)}) collective-permute-start(bf16[256,512]{1,0:T(8,128)(2,1)S(1)} %add_convert_fusion.6.refs_0_), channel_id=1, source_target_pairs={{0,64},{64,0},{1,65},{65,1},{2,66},{66,2},{3,67},{67,3},{4,68},{68... | collective-permute-start | bytes 786440 | tf_op jit(solution)/shard_map/ppermute | solution.py:169
  139.6 3.1 %collective-permute-start.19 = (bf16[256,256]{1,0:T(8,128)(2,1)S(1)}, bf16[256,256]{1,0:T(8,128)(2,1)S(1)}, u32[]{:S(2)}, u32[]{:S(2)}) collective-permute-start(bf16[256,256]{1,0:T(8,128)(2,1)S(1)} %shard_map.75.refs_5_), channel_id=1, source_target_pairs={{0,64},{64,0},{1,65},{65,1},{2,66},{66,2},{3,67},{67,3},{4,68},{68... | collective-permute-start | bytes 393224 | tf_op jit(solution)/shard_map/ppermute | solution.py:169
  139.6 3.0 %collective-permute-start.16 = (bf16[256,256]{1,0:T(8,128)(2,1)S(1)}, bf16[256,256]{1,0:T(8,128)(2,1)S(1)}, u32[]{:S(2)}, u32[]{:S(2)}) collective-permute-start(bf16[256,256]{1,0:T(8,128)(2,1)S(1)} %collective-permute-done.13.refs_2_), channel_id=1, source_target_pairs={{0,64},{64,0},{1,65},{65,1},{2,66},{66,2},{3,67},{67,3},{4,68},{68... | collective-permute-start | bytes 393224 | tf_op jit(solution)/shard_map/ppermute | solution.py:169
  141.7 1.9 %collective-permute-start.17 = (bf16[256,256]{1,0:T(8,128)(2,1)S(1)}, bf16[256,256]{1,0:T(8,128)(2,1)S(1)}, u32[]{:S(2)}, u32[]{:S(2)}) collective-permute-start(bf16[256,256]{1,0:T(8,128)(2,1)S(1)} %collective-permute-done.14.refs_3_), channel_id=1, source_target_pairs={{0,64},{64,0},{1,65},{65,1},{2,66},{66,2},{3,67},{67,3},{4,68},{68... | collective-permute-start | bytes 393224 | tf_op jit(solution)/shard_map/ppermute | solution.py:169
  142.6 1.3 collective-permute-start.18
  (2 other events, 12.0 us)

commit v4 on v3

--- a/solution.py
+++ b/solution.py
@@ -14,35 +14,46 @@
 HALF = D // 2
 WIDE = 512
 THIN = 256
-Z_STEPS = (2, 1, 3, 0)
+Z_STEPS = (1, 3, 2, 0)
 EPSILON = 1e-05
 F32 = jnp.float32
 BF16 = jnp.bfloat16
 ROUTE_VMEM = 60 * 1024 * 1024
 MATMUL_VMEM = 16 * 1024 * 1024
+ROUTE_BLOCK = 128
+NORM_STEPS = TOK_DEV // ROUTE_BLOCK
+PICK_STEPS = 2
+PICK = EXPERTS // PICK_STEPS
+NORM_ROWS = 16
 NT = (((1,), (1,)), ((), ()))
 
 
-def route_kernel(tok_ref, gain_ref, router_ref, ids_ref, buf_ref, mix_ref, normed_ref, key_ref):
+def slot_rows(keys):
+    slot = lax.broadcasted_iota(jnp.int32, (CAP, TOK_DEV), 0).astype(F32)
+    return jnp.concatenate([(slot == keys[e : e + 1, :]).astype(F32) for e in range(keys.shape[0])], axis=0).astype(BF16)
+
+
+def route_kernel(tok_ref, gain_ref, router_ref, ids_ref, rows_ref, mix_ref, normed_ref, key_t_ref):
     step = pl.program_id(0)
-    experts_a_step = EXPERTS // pl.num_programs(0)
-
-    @pl.when(step == 0)
+    core = lax.axis_index("pp")
+
+    def norm_rows(part, carry):
+        inner = pl.ds(pl.multiple_of(part * NORM_ROWS, NORM_ROWS), NORM_ROWS)
+        outer = pl.ds(pl.multiple_of(step * ROUTE_BLOCK + part * NORM_ROWS, NORM_ROWS), NORM_ROWS)
+        values = tok_ref[inner, :].astype(F32)
+        shifted = values - jnp.mean(values, axis=-1, keepdims=True)
+        spread = jnp.mean(shifted * shifted, axis=-1, keepdims=True)
+        normed = (shifted * lax.rsqrt(spread + EPSILON) * gain_ref[...]).astype(BF16)
+        normed_ref[0, outer, :] = normed[:, :HALF]
+        normed_ref[1, outer, :] = normed[:, HALF:]
+        return carry
+
+    @pl.when(step < NORM_STEPS)
     def _():
-        def norm_rows(part, carry):
-            rows = pl.ds(pl.multiple_of(part * 32, 32), 32)
-            values = tok_ref[rows, :].astype(F32)
-            shifted = values - jnp.mean(values, axis=-1, keepdims=True)
-            spread = jnp.mean(shifted * shifted, axis=-1, keepdims=True)
-            normed = (shifted * lax.rsqrt(spread + EPSILON) * gain_ref[...]).astype(BF16)
-            normed_ref[0, rows, :] = normed[:, :HALF]
-            normed_ref[1, rows, :] = normed[:, HALF:]
-            return carry
-
-        lax.fori_loop(0, TOK_DEV // 32, norm_rows, 0)
-        logits = lax.dot_general(normed_ref[0], router_ref[:, :HALF], NT, preferred_element_type=F32)
-        logits += lax.dot_general(normed_ref[1], router_ref[:, HALF:], NT, preferred_element_type=F32)
-
+        lax.fori_loop(0, ROUTE_BLOCK // NORM_ROWS, norm_rows, 0, unroll=True)
+
+    @pl.when(step == NORM_STEPS - 1)
+    def _():
         named = jnp.zeros((EXPERTS, TOK_DEV), jnp.int32)
         expert = lax.broadcasted_iota(jnp.int32, (EXPERTS, TOK_DEV), 0)
         for k in range(TOP):
@@ -54,11 +65,14 @@
         same = (row == col).astype(F32).astype(BF16)
         named_bf = named.astype(BF16)
         place_t = lax.dot_general(named_bf, earlier, NT, preferred_element_type=F32)
-        key_ref[...] = jnp.where(named > 0.5, place_t, -1.0)
+        key_t = jnp.where(named > 0.5, place_t, -1.0)
+        key_t_ref[...] = key_t
+        logits = lax.dot_general(normed_ref[0], router_ref[:, :HALF], NT, preferred_element_type=F32)
+        logits += lax.dot_general(normed_ref[1], router_ref[:, HALF:], NT, preferred_element_type=F32)
         place = lax.dot_general(earlier, named_bf, NT, preferred_element_type=F32)
         chosen = lax.dot_general(same, named_bf, NT, preferred_element_type=F32) > 0.5
+        weight = jnp.where(chosen, jnp.exp(logits), 0.0)
         key = jnp.where(chosen, place, -1.0)
-        weight = jnp.where(chosen, jnp.exp(logits), 0.0)
         gate = weight / jnp.sum(weight, axis=1, keepdims=True)
 
         slot = lax.broadcasted_iota(jnp.int32, (EXPERTS, ROWS), 1)
@@ -70,37 +84,30 @@
         gate_wide = jnp.dot(gate.astype(BF16), spread_out, preferred_element_type=F32)
         mix_ref[...] = jnp.where(key_wide == slot_in, gate_wide, 0.0).astype(BF16)
 
-    keys = key_ref[pl.ds(pl.multiple_of(step * experts_a_step, experts_a_step), experts_a_step), :]
-    slot_row = lax.broadcasted_iota(jnp.int32, (CAP, TOK_DEV), 0).astype(F32)
-    picks = [(slot_row == keys[e : e + 1, :]).astype(F32) for e in range(experts_a_step)]
-    pick = jnp.concatenate(picks, axis=0).astype(BF16)
-    buf_ref[...] = jnp.dot(pick, normed_ref[lax.axis_index("pp")], preferred_element_type=F32).astype(BF16)
+    @pl.when(step >= NORM_STEPS - 1)
+    def _():
+        keys = key_t_ref[pl.ds(pl.multiple_of((step - NORM_STEPS + 1) * PICK, PICK), PICK), :]
+        rows_ref[...] = jnp.dot(slot_rows(keys), normed_ref[core], preferred_element_type=F32).astype(BF16)
 
 
 def route(tokens, norm_gain, router_weight, expert_ids):
-    steps = 2
     whole = lambda i: (0, 0)
+    shapes = [((ROWS, HALF), BF16), ((TOK_DEV, ROWS), BF16)]
     return pl.pallas_call(
         route_kernel,
-        grid=(steps,),
+        grid=(NORM_STEPS + PICK_STEPS - 1,),
         in_specs=[
-            pl.BlockSpec((TOK_DEV, D), whole),
+            pl.BlockSpec((ROUTE_BLOCK, D), lambda i: (jnp.minimum(i, NORM_STEPS - 1), 0)),
             pl.BlockSpec((1, D), whole),
             pl.BlockSpec((EXPERTS, D), whole),
             pl.BlockSpec((TOP, TOK_DEV), whole),
         ],
         out_specs=[
-            pl.BlockSpec((ROWS // steps, HALF), lambda i: (i, 0)),
+            pl.BlockSpec((PICK * CAP, HALF), lambda i: (jnp.maximum(i - NORM_STEPS + 1, 0), 0)),
             pl.BlockSpec((TOK_DEV, ROWS), whole),
         ],
-        out_shape=[
-            jax.ShapeDtypeStruct((ROWS, HALF), BF16),
-            jax.ShapeDtypeStruct((TOK_DEV, ROWS), BF16),
-        ],
-        scratch_shapes=[
-            pltpu.VMEM((2, TOK_DEV, HALF), BF16),
-            pltpu.VMEM((EXPERTS, TOK_DEV), F32),
-        ],
+        out_shape=[jax.ShapeDtypeStruct(shape, kind) for shape, kind in shapes],
+        scratch_shapes=[pltpu.VMEM((2, TOK_DEV, HALF), BF16), pltpu.VMEM((EXPERTS, TOK_DEV), F32)],
         compiler_params=pltpu.CompilerParams(vmem_limit_bytes=ROUTE_VMEM),
         cost_estimate=pl.CostEstimate(flops=2 * ROWS * TOK_DEV * HALF, bytes_accessed=6_000_000, transcendentals=0),
     )(tokens, norm_gain.reshape(1, D), router_weight.T, expert_ids.T)
@@ -179,6 +186,10 @@
     return lax.all_to_all(rows.reshape(EXPERTS, CAP, width), "ep", split_axis=0, concat_axis=0, tiled=True).reshape(ROWS, width)
 
 
+def after(earlier, values):
+    return lax.optimization_barrier((earlier, values))[1]
+
+
 def on_device(tokens, norm_gain, router_weight, expert_ids, up_weight, down_weight):
     core = lax.axis_index("pp").astype(jnp.int32)
     z = lax.axis_index("dp").astype(jnp.int32)

time: 146 us -> 143 us (0.979)
  waiting for transfers between devices: 28.3 us -> 22.2 us
  starting transfers between devices: 28.4 us -> 31.8 us
    ppermute x9, waiting for transfers between devices: 19.4 us -> 15.7 us  [along_z(): lax.ppermute(values, 'dp', [(i, (i + step) % count) for i in range(count)])]
    ppermute x9, starting transfers between devices: 10.6 us -> 14 us  [along_z(): lax.ppermute(values, 'dp', [(i, (i + step) % count) for i in range(count)])]
    all_to_all x2, waiting for transfers between devices: 6.4 us -> 4.37 us  [to_experts(): lax.all_to_all(rows.reshape(EXPERTS, CAP, width), 'ep', split_axis=0, con...]
  transfers between devices with their start and end apart: 22 -> 22, of which waited for: 7 -> 7; matrix products, arithmetic and copies ran while one was open for 14% -> 15% of each run, Pallas kernels for 1% -> 1%
where the time goes in v4:
time: 143 us; the launch traced here: 142 us
  blocking collectives  50.6 us (35%)
  starting transfers between devices  31.8 us (22%)
  matrix products  23.3 us (16%)
  waiting for transfers between devices  22.2 us (16%)
  Pallas kernels  8.92 us (6%)
  other arithmetic  2.9 us (2%)
  local copies, waits for them, and re-layouts  1.9 us (1%)
    all_to_all x1, blocking collectives, to_experts(): lax.all_to_all(rows.reshape(EXPERTS, CAP, width), 'ep', split_axis=0, con...  50.6 us
    dot_general x12, matrix products, product(): return jnp.dot(rows, weight, preferred_element_type=F32)  23.3 us
    ppermute x9, waiting for transfers between devices, along_z(): lax.ppermute(values, 'dp', [(i, (i + step) % count) for i in range(count)])  15.7 us
    ppermute x9, starting transfers between devices, along_z(): lax.ppermute(values, 'dp', [(i, (i + step) % count) for i in range(count)])  14 us
    ppermute x11, starting transfers between devices, swap(): return lax.ppermute(values, 'pp', [(0, 1), (1, 0)])  10.3 us
    all_to_all x2, starting transfers between devices, to_experts(): lax.all_to_all(rows.reshape(EXPERTS, CAP, width), 'ep', split_axis=0, con...  7.43 us
    pallas_call x1, Pallas kernels, route(): pl.pallas_call(route_kernel, grid=(NORM_STEPS + PICK_STEPS - 1,), in_spec...  6.33 us
    all_to_all x2, waiting for transfers between devices, to_experts(): lax.all_to_all(rows.reshape(EXPERTS, CAP, width), 'ep', split_axis=0, con...  4.37 us
  transfers between devices with their start and end apart: 22, of which 7 were waited for; matrix products, arithmetic and copies ran while one was open for 15% of the time, Pallas kernels for 1%

profile of v4, /device:TPU:1, one launch (start us, length us, event | category | flops | bytes accessed | tf_op | source)
XLA Modules:
  0.0 142.0 jit_solution(14346733089412015273)
XLA Ops:
  0.0 6.3 %shard_map.73 = (bf16[1152,1536]{1,0:T(8,128)(2,1)}, bf16[256,1152]{1,0:T(8,128)(2,1)}) custom-call(bf16[256,3072]{1,0:T(8,128)(2,1)} %tok_ref.1, f32[1,3072]{1,0:T(1,128)} %bitcast.79, bf16[16,3072]{1,0:T(8,128)(2,1)} %bitcast.78, s32[4,256]{1,0:T(4,128)} %bitcast.80), custom_call_target="tpu_custom_call" | custom-call | flops 905969664 | bytes 6000000 | tf_op jit(solution)/shard_map/pallas_call | solution.py:96
  6.3 50.6 %all_to_all.15 = bf16[16,72,1536]{2,1,0:T(8,128)(2,1)S(1)} all-to-all(bf16[16,72,1536]{2,1,0:T(8,128)(2,1)} %bitcast.72), channel_id=1, replica_groups=mesh['pp'=2,'ep'=16,'dp'=4] {'ep'}, dimensions={0} | all-to-all | bytes 7077888 | tf_op jit(solution)/shard_map/all_to_all | solution.py:186
  56.9 1.8 %collective-permute-start = (bf16[1152,1536]{1,0:T(8,128)(2,1)S(1)}, bf16[1152,1536]{1,0:T(8,128)(2,1)}, u32[]{:S(2)}, u32[]{:S(2)}) collective-permute-start(bf16[1152,1536]{1,0:T(8,128)(2,1)S(1)} %bitcast.70), channel_id=1, source_target_pairs={{0,64},{64,0},{1,65},{65,1},{2,66},{66,2},{3,67},{67,3},{4,68},{68... | collective-permute-start | bytes 10616840 | tf_op jit(solution)/shard_map/ppermute | solution.py:176
  58.7 4.7 %fusion.1 = f32[1152,768]{1,0:T(8,128)S(1)} fusion(bf16[1152,1536]{1,0:T(8,128)(2,1)S(1)} %bitcast.71, bf16[2,1536,768]{2,1,0:T(8,128)(2,1)} %bitcast.76, s32[]{:T(128)S(6)} %select_n.68), kind=kOutput, calls=%fused_computation.8 | convolution fusion | flops 2717908992 | bytes 9437188 | tf_op jit(solution)/shard_map/dot_general | solution.py:117
  64.7 6.0 %multiply_convert_fusion = bf16[1152,768]{1,0:T(8,128)(2,1)S(1)} fusion(f32[1152,768]{1,0:T(8,128)S(1)} %fusion.1, bf16[1152,1536]{1,0:T(8,128)(2,1)} %collective-permute-done, bf16[2,1536,768]{2,1,0:T(8,128)(2,1)} %bitcast.77, s32[]{:T(128)S(6)} %select_n.69), kind=kOutput, calls=%fused_computation.1 | convolution fusion | flops 2723217408 | bytes 11206660 | tf_op jit(solution)/shard_map/dot_general | solution.py:117
  75.1 1.5 %convolution_convert_fusion.4 = bf16[1152,256]{1,0:T(8,128)(2,1)} fusion(bf16[1152,768]{1,0:T(8,128)(2,1)S(1)} %multiply_convert_fusion, bf16[1,768,3072]{2,1,0:T(8,128)(2,1)S(1)} %bitcast.75, s32[]{:T(128)S(6)} %select_n.73), kind=kOutput, calls=%fused_computation.6 | convolution fusion | flops 453279744 | bytes 2752516 | tf_op jit(solution)/shard_map/dot_general | solution.py:117
  76.9 1.5 %add_convert_fusion.2 = bf16[1152,256]{1,0:T(8,128)(2,1)} fusion(bf16[1152,256]{1,0:T(8,128)(2,1)S(1)} %collective-permute-done.7, bf16[1152,768]{1,0:T(8,128)(2,1)S(1)} %multiply_convert_fusion, bf16[1,768,3072]{2,1,0:T(8,128)(2,1)S(1)} %bitcast.75, s32[]{:T(128)S(6)} %select_n.81), kind=kOutput, calls=%fused_computation.14 | convolution fusion | flops 453869568 | bytes 3342340 | tf_op jit(solution)/shard_map/dot_general | solution.py:117
  78.4 3.6 %collective-permute-start.8 = (bf16[1152,256]{1,0:T(8,128)(2,1)}, bf16[1152,256]{1,0:T(8,128)(2,1)}, u32[]{:S(2)}, u32[]{:S(2)}) collective-permute-start(bf16[1152,256]{1,0:T(8,128)(2,1)} %add_convert_fusion.2), channel_id=1, source_target_pairs={{0,2},{1,3},{2,0},{3,1},{4,6},{5,7},{6,4},{7,5},{8,10},{9,11},{10,... | collective-permute-start | bytes 1769480 | tf_op jit(solution)/shard_map/ppermute | solution.py:181
  82.0 1.5 %add_convert_fusion.3 = bf16[1152,256]{1,0:T(8,128)(2,1)} fusion(bf16[1152,256]{1,0:T(8,128)(2,1)S(1)} %collective-permute-done.5, bf16[1152,768]{1,0:T(8,128)(2,1)S(1)} %multiply_convert_fusion, bf16[1,768,3072]{2,1,0:T(8,128)(2,1)S(1)} %bitcast.75, s32[]{:T(128)S(6)} %select_n.78), kind=kOutput, calls=%fused_computation.15 | convolution fusion | flops 453869568 | bytes 3342340 | tf_op jit(solution)/shard_map/dot_general | solution.py:117
  83.9 1.5 %add_convert_fusion.4 = bf16[1152,256]{1,0:T(8,128)(2,1)} fusion(bf16[1152,256]{1,0:T(8,128)(2,1)S(1)} %collective-permute-done.3, bf16[1152,768]{1,0:T(8,128)(2,1)S(1)} %multiply_convert_fusion, bf16[1,768,3072]{2,1,0:T(8,128)(2,1)S(1)} %bitcast.75, s32[]{:T(128)S(6)} %select_n.75), kind=kOutput, calls=%fused_computation.16 | convolution fusion | flops 453869568 | bytes 3342340 | tf_op jit(solution)/shard_map/dot_general | solution.py:117
  86.4 2.1 %add_convert_fusion = bf16[1152,512]{1,0:T(8,128)(2,1)} fusion(bf16[1152,512]{1,0:T(8,128)(2,1)S(1)} %collective-permute-done.1, bf16[1152,768]{1,0:T(8,128)(2,1)S(1)} %multiply_convert_fusion, bf16[1,768,3072]{2,1,0:T(8,128)(2,1)S(1)} %bitcast.75, s32[]{:T(128)S(6)} %select_n.66), kind=kOutput, calls=%fused_computation.10 | convolution fusion | flops 907739136 | bytes 4915204 | tf_op jit(solution)/shard_map/dot_general | solution.py:117
  88.5 3.7 %all-to-all-start.1 = ((bf16[16,72,512]{2,1,0:T(8,128)(2,1)}), bf16[16,72,512]{2,1,0:T(8,128)(2,1)S(1)}, u32[]{:S(2)}, u32[]{:S(2)}) async-start(bf16[16,72,512]{2,1,0:T(8,128)(2,1)} %bitcast.73), calls=%async_computation.1 | async-start | bytes 2359296 | tf_op jit(solution)/shard_map/all_to_all | solution.py:186
  92.3 1.6 %fusion.28 = f32[1152,256]{1,0:T(8,128)S(1)} fusion(bf16[1152,768]{1,0:T(8,128)(2,1)S(1)} %multiply_convert_fusion, bf16[1,768,3072]{2,1,0:T(8,128)(2,1)} %param.12, s32[]{:T(128)S(6)} %select_n.72), kind=kOutput, calls=%fused_computation.34 | convolution fusion | flops 452984832 | bytes 3342340 | tf_op jit(solution)/shard_map/dot_general | solution.py:117
  93.9 2.0 %collective-permute-done.8 = bf16[1152,256]{1,0:T(8,128)(2,1)} collective-permute-done((bf16[1152,256]{1,0:T(8,128)(2,1)}, bf16[1152,256]{1,0:T(8,128)(2,1)}, u32[]{:S(2)}, u32[]{:S(2)}) %collective-permute-start.8) | collective-permute-done | bytes 589856 | tf_op jit(solution)/shard_map/ppermute | solution.py:181
  96.0 13.1 %collective-permute-done.6 = bf16[1152,256]{1,0:T(8,128)(2,1)} collective-permute-done((bf16[1152,256]{1,0:T(8,128)(2,1)}, bf16[1152,256]{1,0:T(8,128)(2,1)}, u32[]{:S(2)}, u32[]{:S(2)}) %collective-permute-start.6) | collective-permute-done | bytes 589856 | tf_op jit(solution)/shard_map/ppermute | solution.py:181
  109.0 2.6 %add_convert_fusion.1 = bf16[1152,256]{1,0:T(8,128)(2,1)} fusion(bf16[1152,256]{1,0:T(8,128)(2,1)} %collective-permute-done.8, bf16[1152,256]{1,0:T(8,128)(2,1)} %collective-permute-done.6, bf16[1152,256]{1,0:T(8,128)(2,1)} %collective-permute-done.4, f32[1152,256]{1,0:T(8,128)S(1)} %fusion.28, bf16[1152,256]{1,0:T(8,128)(2,1)S(1)} %collective-permute-done.2), kind=kLoop, calls=%fused_computation.13 | loop fusion | flops 3244032 | bytes 4128768 | tf_op jit(solution)/shard_map/convert_element_type | solution.py:217
  111.7 3.7 %all-to-all-start.2 = ((bf16[16,72,256]{2,1,0:T(8,128)(2,1)}), bf16[16,72,256]{2,1,0:T(8,128)(2,1)S(1)}, u32[]{:S(2)}, u32[]{:S(2)}) async-start(bf16[16,72,256]{2,1,0:T(8,128)(2,1)} %bitcast.22), calls=%async_computation.2 | async-start | bytes 1179648 | tf_op jit(solution)/shard_map/all_to_all | solution.py:186
  116.9 2.8 %collective-permute-start.11 = (bf16[256,512]{1,0:T(8,128)(2,1)S(1)}, bf16[256,512]{1,0:T(8,128)(2,1)S(1)}, u32[]{:S(2)}, u32[]{:S(2)}) collective-permute-start(bf16[256,512]{1,0:T(8,128)(2,1)S(1)} %shard_map.74), channel_id=1, source_target_pairs={{0,2},{1,3},{2,0},{3,1},{4,6},{5,7},{6,4},{7,5},{8,10},{9,11},{10,... | collective-permute-start | bytes 786440 | tf_op jit(solution)/shard_map/ppermute | solution.py:181
  122.1 4.4 %all-to-all-done.2 = bf16[16,72,256]{2,1,0:T(8,128)(2,1)S(1)} async-done(((bf16[16,72,256]{2,1,0:T(8,128)(2,1)}), bf16[16,72,256]{2,1,0:T(8,128)(2,1)S(1)}, u32[]{:S(2)}, u32[]{:S(2)}) %all-to-all-start.2) | async-done | bytes 589856 | tf_op jit(solution)/shard_map/all_to_all | solution.py:186
  127.8 2.5 %collective-permute-start.14 = (bf16[256,256]{1,0:T(8,128)(2,1)S(1)}, bf16[256,256]{1,0:T(8,128)(2,1)S(1)}, u32[]{:S(2)}, u32[]{:S(2)}) collective-permute-start(bf16[256,256]{1,0:T(8,128)(2,1)S(1)} %shard_map.75.refs_5_), channel_id=1, source_target_pairs={{0,3},{1,0},{2,1},{3,2},{4,7},{5,4},{6,5},{7,6},{8,11},{9,8},{10,9... | collective-permute-start | bytes 393224 | tf_op jit(solution)/shard_map/ppermute | solution.py:181
  132.3 2.2 %collective-permute-start.12 = (bf16[256,512]{1,0:T(8,128)(2,1)S(1)}, bf16[256,512]{1,0:T(8,128)(2,1)S(1)}, u32[]{:S(2)}, u32[]{:S(2)}) collective-permute-start(bf16[256,512]{1,0:T(8,128)(2,1)S(1)} %add_convert_fusion.6.refs_0_), channel_id=1, source_target_pairs={{0,64},{64,0},{1,65},{65,1},{2,66},{66,2},{3,67},{67,3},{4,68},{68... | collective-permute-start | bytes 786440 | tf_op jit(solution)/shard_map/ppermute | solution.py:176
  134.6 2.0 %collective-permute-start.16 = (bf16[256,256]{1,0:T(8,128)(2,1)S(1)}, bf16[256,256]{1,0:T(8,128)(2,1)S(1)}, u32[]{:S(2)}, u32[]{:S(2)}) collective-permute-start(bf16[256,256]{1,0:T(8,128)(2,1)S(1)} %collective-permute-done.13.refs_2_), channel_id=1, source_target_pairs={{0,64},{64,0},{1,65},{65,1},{2,66},{66,2},{3,67},{67,3},{4,68},{68... | collective-permute-start | bytes 393224 | tf_op jit(solution)/shard_map/ppermute | solution.py:176
  137.1 2.1 %collective-permute-start.18 = (bf16[256,256]{1,0:T(8,128)(2,1)S(1)}, bf16[256,256]{1,0:T(8,128)(2,1)S(1)}, u32[]{:S(2)}, u32[]{:S(2)}) collective-permute-start(bf16[256,256]{1,0:T(8,128)(2,1)S(1)} %collective-permute-done.15.refs_4_), channel_id=1, source_target_pairs={{0,64},{64,0},{1,65},{65,1},{2,66},{66,2},{3,67},{67,3},{4,68},{68... | collective-permute-start | bytes 393224 | tf_op jit(solution)/shard_map/ppermute | solution.py:176
  140.1 1.8 %shard_map.76 = bf16[256,3072]{1,0:T(8,128)(2,1)} custom-call(s32[10]{0:T(128)S(1)} %pad_add_fusion.at_ref, bf16[256,512]{1,0:T(8,128)(2,1)S(1)} %add_convert_fusion.6.refs_0_, bf16[256,512]{1,0:T(8,128)(2,1)S(1)} %collective-permute-done.12.refs_1_, bf16[256,256]{1,0:T(8,128)(2,1)S(1)} %collective-permute-done.13.refs_2_, ...), custom_call_target="tpu_custom_call" | custom-call | bytes 3000000 | tf_op jit(solution)/shard_map/pallas_call | solution.py:164
  (53 shorter events, 16.1 us)
Async XLA Ops:
  56.9 7.8 %collective-permute-start = (bf16[1152,1536]{1,0:T(8,128)(2,1)S(1)}, bf16[1152,1536]{1,0:T(8,128)(2,1)}, u32[]{:S(2)}, u32[]{:S(2)}) collective-permute-start(bf16[1152,1536]{1,0:T(8,128)(2,1)S(1)} %bitcast.70), channel_id=1, source_target_pairs={{0,64},{64,0},{1,65},{65,1},{2,66},{66,2},{3,67},{67,3},{4,68},{68... | collective-permute-start | bytes 10616840 | tf_op jit(solution)/shard_map/ppermute | solution.py:176
  58.7 12.0 %slice-start = ((s8[4718592]{0:T(1024)(128)(4,1)}), s8[4194304]{0:T(1024)(128)(4,1)S(1)}, s32[]{:S(2)}) async-start(s8[4718592]{0:T(1024)(128)(4,1)} %bitcast.74), calls=%async_computation.3 | async-start | bytes 8388608
  71.8 14.6 %collective-permute-start.1 = (bf16[1152,512]{1,0:T(8,128)(2,1)S(1)}, bf16[1152,512]{1,0:T(8,128)(2,1)S(1)}, u32[]{:S(2)}, u32[]{:S(2)}) collective-permute-start(bf16[1152,512]{1,0:T(8,128)(2,1)S(1)} %convolution_convert_fusion), channel_id=1, source_target_pairs={{0,64},{64,0},{1,65},{65,1},{2,66},{66,2},{3,67},{67,3},{4,68},{68... | collective-permute-start | bytes 3538952 | tf_op jit(solution)/shard_map/ppermute | solution.py:176
  72.9 4.0 %collective-permute-start.7 = (bf16[1152,256]{1,0:T(8,128)(2,1)S(1)}, bf16[1152,256]{1,0:T(8,128)(2,1)S(1)}, u32[]{:S(2)}, u32[]{:S(2)}) collective-permute-start(bf16[1152,256]{1,0:T(8,128)(2,1)S(1)} %convolution_convert_fusion.1), channel_id=1, source_target_pairs={{0,64},{64,0},{1,65},{65,1},{2,66},{66,2},{3,67},{67,3},{4,68},{68... | collective-permute-start | bytes 1769480 | tf_op jit(solution)/shard_map/ppermute | solution.py:176
  73.8 8.2 %collective-permute-start.5 = (bf16[1152,256]{1,0:T(8,128)(2,1)S(1)}, bf16[1152,256]{1,0:T(8,128)(2,1)S(1)}, u32[]{:S(2)}, u32[]{:S(2)}) collective-permute-start(bf16[1152,256]{1,0:T(8,128)(2,1)S(1)} %convolution_convert_fusion.2), channel_id=1, source_target_pairs={{0,64},{64,0},{1,65},{65,1},{2,66},{66,2},{3,67},{67,3},{4,68},{68... | collective-permute-start | bytes 1769480 | tf_op jit(solution)/shard_map/ppermute | solution.py:176
  74.9 9.0 %collective-permute-start.3 = (bf16[1152,256]{1,0:T(8,128)(2,1)S(1)}, bf16[1152,256]{1,0:T(8,128)(2,1)S(1)}, u32[]{:S(2)}, u32[]{:S(2)}) collective-permute-start(bf16[1152,256]{1,0:T(8,128)(2,1)S(1)} %convolution_convert_fusion.3), channel_id=1, source_target_pairs={{0,64},{64,0},{1,65},{65,1},{2,66},{66,2},{3,67},{67,3},{4,68},{68... | collective-permute-start | bytes 1769480 | tf_op jit(solution)/shard_map/ppermute | solution.py:176
  76.5 17.4 %collective-permute-start.2 = (bf16[1152,256]{1,0:T(8,128)(2,1)}, bf16[1152,256]{1,0:T(8,128)(2,1)S(1)}, u32[]{:S(2)}, u32[]{:S(2)}) collective-permute-start(bf16[1152,256]{1,0:T(8,128)(2,1)} %convolution_convert_fusion.4), channel_id=1, source_target_pairs={{0,64},{64,0},{1,65},{65,1},{2,66},{66,2},{3,67},{67,3},{4,68},{68... | collective-permute-start | bytes 1769480 | tf_op jit(solution)/shard_map/ppermute | solution.py:176
  78.4 17.6 %collective-permute-start.8 = (bf16[1152,256]{1,0:T(8,128)(2,1)}, bf16[1152,256]{1,0:T(8,128)(2,1)}, u32[]{:S(2)}, u32[]{:S(2)}) collective-permute-start(bf16[1152,256]{1,0:T(8,128)(2,1)} %add_convert_fusion.2), channel_id=1, source_target_pairs={{0,2},{1,3},{2,0},{3,1},{4,6},{5,7},{6,4},{7,5},{8,10},{9,11},{10,... | collective-permute-start | bytes 1769480 | tf_op jit(solution)/shard_map/ppermute | solution.py:181
  83.5 25.6 %collective-permute-start.6 = (bf16[1152,256]{1,0:T(8,128)(2,1)}, bf16[1152,256]{1,0:T(8,128)(2,1)}, u32[]{:S(2)}, u32[]{:S(2)}) collective-permute-start(bf16[1152,256]{1,0:T(8,128)(2,1)} %add_convert_fusion.3), channel_id=1, source_target_pairs={{0,3},{1,0},{2,1},{3,2},{4,7},{5,4},{6,5},{7,6},{8,11},{9,8},{10,9... | collective-permute-start | bytes 1769480 | tf_op jit(solution)/shard_map/ppermute | solution.py:181
  85.3 23.7 %collective-permute-start.4 = (bf16[1152,256]{1,0:T(8,128)(2,1)}, bf16[1152,256]{1,0:T(8,128)(2,1)}, u32[]{:S(2)}, u32[]{:S(2)}) collective-permute-start(bf16[1152,256]{1,0:T(8,128)(2,1)} %add_convert_fusion.4), channel_id=1, source_target_pairs={{0,1},{1,2},{2,3},{3,0},{4,5},{5,6},{6,7},{7,4},{8,9},{9,10},{10,1... | collective-permute-start | bytes 1769480 | tf_op jit(solution)/shard_map/ppermute | solution.py:181
  88.5 23.1 %all-to-all-start.1 = ((bf16[16,72,512]{2,1,0:T(8,128)(2,1)}), bf16[16,72,512]{2,1,0:T(8,128)(2,1)S(1)}, u32[]{:S(2)}, u32[]{:S(2)}) async-start(bf16[16,72,512]{2,1,0:T(8,128)(2,1)} %bitcast.73), calls=%async_computation.1 | async-start | bytes 2359296 | tf_op jit(solution)/shard_map/all_to_all | solution.py:186
  111.7 10.4 %copy-start.1 = (s32[4]{0:T(128)S(1)}, s32[4]{0:T(128)}, u32[]{:S(2)}) copy-start(s32[4]{0:T(128)} %constant.78) | copy-start | bytes 52
  111.7 14.8 %all-to-all-start.2 = ((bf16[16,72,256]{2,1,0:T(8,128)(2,1)}), bf16[16,72,256]{2,1,0:T(8,128)(2,1)S(1)}, u32[]{:S(2)}, u32[]{:S(2)}) async-start(bf16[16,72,256]{2,1,0:T(8,128)(2,1)} %bitcast.22), calls=%async_computation.2 | async-start | bytes 1179648 | tf_op jit(solution)/shard_map/all_to_all | solution.py:186
  116.9 13.4 %collective-permute-start.11 = (bf16[256,512]{1,0:T(8,128)(2,1)S(1)}, bf16[256,512]{1,0:T(8,128)(2,1)S(1)}, u32[]{:S(2)}, u32[]{:S(2)}) collective-permute-start(bf16[256,512]{1,0:T(8,128)(2,1)S(1)} %shard_map.74), channel_id=1, source_target_pairs={{0,2},{1,3},{2,0},{3,1},{4,6},{5,7},{6,4},{7,5},{8,10},{9,11},{10,... | collective-permute-start | bytes 786440 | tf_op jit(solution)/shard_map/ppermute | solution.py:181
  119.7 12.3 %collective-permute-start.10 = (bf16[256,512]{1,0:T(8,128)(2,1)S(1)}, bf16[256,512]{1,0:T(8,128)(2,1)S(1)}, u32[]{:S(2)}, u32[]{:S(2)}) collective-permute-start(bf16[256,512]{1,0:T(8,128)(2,1)S(1)} %shard_map.74), channel_id=1, source_target_pairs={{0,3},{1,0},{2,1},{3,2},{4,7},{5,4},{6,5},{7,6},{8,11},{9,8},{10,9... | collective-permute-start | bytes 786440 | tf_op jit(solution)/shard_map/ppermute | solution.py:181
  120.2 11.9 %collective-permute-start.9 = (bf16[256,512]{1,0:T(8,128)(2,1)S(1)}, bf16[256,512]{1,0:T(8,128)(2,1)S(1)}, u32[]{:S(2)}, u32[]{:S(2)}) collective-permute-start(bf16[256,512]{1,0:T(8,128)(2,1)S(1)} %shard_map.74), channel_id=1, source_target_pairs={{0,1},{1,2},{2,3},{3,0},{4,5},{5,6},{6,7},{7,4},{8,9},{9,10},{10,1... | collective-permute-start | bytes 786440 | tf_op jit(solution)/shard_map/ppermute | solution.py:181
  126.8 7.8 %collective-permute-start.13 = (bf16[256,256]{1,0:T(8,128)(2,1)S(1)}, bf16[256,256]{1,0:T(8,128)(2,1)S(1)}, u32[]{:S(2)}, u32[]{:S(2)}) collective-permute-start(bf16[256,256]{1,0:T(8,128)(2,1)S(1)} %shard_map.75.refs_5_), channel_id=1, source_target_pairs={{0,1},{1,2},{2,3},{3,0},{4,5},{5,6},{6,7},{7,4},{8,9},{9,10},{10,1... | collective-permute-start | bytes 393224 | tf_op jit(solution)/shard_map/ppermute | solution.py:181
  127.8 8.8 %collective-permute-start.14 = (bf16[256,256]{1,0:T(8,128)(2,1)S(1)}, bf16[256,256]{1,0:T(8,128)(2,1)S(1)}, u32[]{:S(2)}, u32[]{:S(2)}) collective-permute-start(bf16[256,256]{1,0:T(8,128)(2,1)S(1)} %shard_map.75.refs_5_), channel_id=1, source_target_pairs={{0,3},{1,0},{2,1},{3,2},{4,7},{5,4},{6,5},{7,6},{8,11},{9,8},{10,9... | collective-permute-start | bytes 393224 | tf_op jit(solution)/shard_map/ppermute | solution.py:181
  130.3 6.8 %collective-permute-start.15 = (bf16[256,256]{1,0:T(8,128)(2,1)S(1)}, bf16[256,256]{1,0:T(8,128)(2,1)S(1)}, u32[]{:S(2)}, u32[]{:S(2)}) collective-permute-start(bf16[256,256]{1,0:T(8,128)(2,1)S(1)} %shard_map.75.refs_5_), channel_id=1, source_target_pairs={{0,2},{1,3},{2,0},{3,1},{4,6},{5,7},{6,4},{7,5},{8,10},{9,11},{10,... | collective-permute-start | bytes 393224 | tf_op jit(solution)/shard_map/ppermute | solution.py:181
  132.3 6.9 %collective-permute-start.12 = (bf16[256,512]{1,0:T(8,128)(2,1)S(1)}, bf16[256,512]{1,0:T(8,128)(2,1)S(1)}, u32[]{:S(2)}, u32[]{:S(2)}) collective-permute-start(bf16[256,512]{1,0:T(8,128)(2,1)S(1)} %add_convert_fusion.6.refs_0_), channel_id=1, source_target_pairs={{0,64},{64,0},{1,65},{65,1},{2,66},{66,2},{3,67},{67,3},{4,68},{68... | collective-permute-start | bytes 786440 | tf_op jit(solution)/shard_map/ppermute | solution.py:176
  134.5 4.7 %collective-permute-start.19 = (bf16[256,256]{1,0:T(8,128)(2,1)S(1)}, bf16[256,256]{1,0:T(8,128)(2,1)S(1)}, u32[]{:S(2)}, u32[]{:S(2)}) collective-permute-start(bf16[256,256]{1,0:T(8,128)(2,1)S(1)} %shard_map.75.refs_5_), channel_id=1, source_target_pairs={{0,64},{64,0},{1,65},{65,1},{2,66},{66,2},{3,67},{67,3},{4,68},{68... | collective-permute-start | bytes 393224 | tf_op jit(solution)/shard_map/ppermute | solution.py:176
  134.6 4.6 %collective-permute-start.16 = (bf16[256,256]{1,0:T(8,128)(2,1)S(1)}, bf16[256,256]{1,0:T(8,128)(2,1)S(1)}, u32[]{:S(2)}, u32[]{:S(2)}) collective-permute-start(bf16[256,256]{1,0:T(8,128)(2,1)S(1)} %collective-permute-done.13.refs_2_), channel_id=1, source_target_pairs={{0,64},{64,0},{1,65},{65,1},{2,66},{66,2},{3,67},{67,3},{4,68},{68... | collective-permute-start | bytes 393224 | tf_op jit(solution)/shard_map/ppermute | solution.py:176
  136.6 2.6 %collective-permute-start.17 = (bf16[256,256]{1,0:T(8,128)(2,1)S(1)}, bf16[256,256]{1,0:T(8,128)(2,1)S(1)}, u32[]{:S(2)}, u32[]{:S(2)}) collective-permute-start(bf16[256,256]{1,0:T(8,128)(2,1)S(1)} %collective-permute-done.14.refs_3_), channel_id=1, source_target_pairs={{0,64},{64,0},{1,65},{65,1},{2,66},{66,2},{3,67},{67,3},{4,68},{68... | collective-permute-start | bytes 393224 | tf_op jit(solution)/shard_map/ppermute | solution.py:176
  137.1 3.0 %collective-permute-start.18 = (bf16[256,256]{1,0:T(8,128)(2,1)S(1)}, bf16[256,256]{1,0:T(8,128)(2,1)S(1)}, u32[]{:S(2)}, u32[]{:S(2)}) collective-permute-start(bf16[256,256]{1,0:T(8,128)(2,1)S(1)} %collective-permute-done.15.refs_4_), channel_id=1, source_target_pairs={{0,64},{64,0},{1,65},{65,1},{2,66},{66,2},{3,67},{67,3},{4,68},{68... | collective-permute-start | bytes 393224 | tf_op jit(solution)/shard_map/ppermute | solution.py:176
  (2 other events, 12.0 us)

commit v5 on v4

v5 whole, which is shorter than its diff:
```python
import jax
import jax.numpy as jnp
from jax import lax
from jax.experimental import pallas as pl
from jax.experimental.pallas import tpu as pltpu
from jax.sharding import PartitionSpec as P

D = 3072
EXPERTS = 16
TOP = 4
TOK_DEV = 256
CAP = 72
ROWS = EXPERTS * CAP
HALF = D // 2
WIDE = 512
THIN = 256
Z_STEPS = (1, 3, 2, 0)
EPSILON = 1e-05
F32 = jnp.float32
BF16 = jnp.bfloat16
ROUTE_VMEM = 60 * 1024 * 1024
MATMUL_VMEM = 6 * 1024 * 1024
ROUTE_BLOCK = 64
PICK = 4
NORM_ROWS = 16
NT = (((1,), (1,)), ((), ()))


def slot_rows(keys):
    slot = lax.broadcasted_iota(jnp.int32, (CAP, TOK_DEV), 0).astype(F32)
    return jnp.concatenate([(slot == keys[e : e + 1, :]).astype(F32) for e in range(keys.shape[0])], axis=0).astype(BF16)


def route_kernel(tok_hbm, gain_hbm, router_hbm, ids_hbm, rows_hbm, mix_hbm, tok_ref, gain_ref, router_ref, ids_ref, normed_ref, rows_ref, mix_ref, sems, out_sems):
    small = [
        pltpu.make_async_copy(ids_hbm, ids_ref, sems.at[0]),
        pltpu.make_async_copy(gain_hbm, gain_ref, sems.at[1]),
        pltpu.make_async_copy(router_hbm, router_ref, sems.at[2]),
    ]
    blocks = [pl.ds(begin, ROUTE_BLOCK) for begin in range(0, TOK_DEV, ROUTE_BLOCK)]
    loads = [pltpu.make_async_copy(tok_hbm.at[block], tok_ref.at[block], sems.at[3 + i]) for i, block in enumerate(blocks)]
    for copy in small[:2] + loads + small[2:]:
        copy.start()

    small[0].wait()
    named = jnp.zeros((EXPERTS, TOK_DEV), jnp.int32)
    expert = lax.broadcasted_iota(jnp.int32, (EXPERTS, TOK_DEV), 0)
    for k in range(TOP):
        named += (ids_ref[k : k + 1, :] == expert).astype(jnp.int32)
    named = named.astype(F32)
    row = lax.broadcasted_iota(jnp.int32, (TOK_DEV, TOK_DEV), 0)
    col = lax.broadcasted_iota(jnp.int32, (TOK_DEV, TOK_DEV), 1)
    earlier = (row > col).astype(F32).astype(BF16)
    same = (row == col).astype(F32).astype(BF16)
    named_bf = named.astype(BF16)
    place_t = lax.dot_general(named_bf, earlier, NT, preferred_element_type=F32)
    key_t = jnp.where(named > 0.5, place_t, -1.0)
    place = lax.dot_general(earlier, named_bf, NT, preferred_element_type=F32)
    chosen = lax.dot_general(same, named_bf, NT, preferred_element_type=F32) > 0.5
    key = jnp.where(chosen, place, -1.0)

    def norm_rows(part, carry):
        rows = pl.ds(pl.multiple_of(part * NORM_ROWS, NORM_ROWS), NORM_ROWS)
        values = tok_ref[rows, :].astype(F32)
        shifted = values - jnp.mean(values, axis=-1, keepdims=True)
        spread = jnp.mean(shifted * shifted, axis=-1, keepdims=True)
        normed = (shifted * lax.rsqrt(spread + EPSILON) * gain_ref[...]).astype(BF16)
        normed_ref[0, rows, :] = normed[:, :HALF]
        normed_ref[1, rows, :] = normed[:, HALF:]
        return carry

    small[1].wait()
    turns = ROUTE_BLOCK // NORM_ROWS
    for i, copy in enumerate(loads):
        copy.wait()
        lax.fori_loop(i * turns, (i + 1) * turns, norm_rows, 0, unroll=True)

    core = lax.axis_index("pp")
    stores = []
    for i in range(EXPERTS // PICK):
        rows = pl.ds(i * PICK * CAP, PICK * CAP)
        pick = slot_rows(key_t[i * PICK : (i + 1) * PICK, :])
        rows_ref[rows, :] = jnp.dot(pick, normed_ref[core], preferred_element_type=F32).astype(BF16)
        stores.append(pltpu.make_async_copy(rows_ref.at[rows], rows_hbm.at[rows], out_sems.at[i]))
        stores[-1].start()

    small[2].wait()
    logits = lax.dot_general(normed_ref[0], router_ref[:, :HALF], NT, preferred_element_type=F32)
    logits += lax.dot_general(normed_ref[1], router_ref[:, HALF:], NT, preferred_element_type=F32)
    weight = jnp.where(chosen, jnp.exp(logits), 0.0)
    gate = weight / jnp.sum(weight, axis=1, keepdims=True)
    slot = lax.broadcasted_iota(jnp.int32, (EXPERTS, ROWS), 1)
    first = lax.broadcasted_iota(jnp.int32, (EXPERTS, ROWS), 0) * CAP
    inside = (slot >= first) & (slot < first + CAP)
    spread_out = inside.astype(F32).astype(BF16)
    slot_in = jnp.sum(jnp.where(inside, slot - first, 0).astype(F32), axis=0, keepdims=True)
    key_wide = jnp.dot(key.astype(BF16), spread_out, preferred_element_type=F32)
    gate_wide = jnp.dot(gate.astype(BF16), spread_out, preferred_element_type=F32)
    mix_ref[...] = jnp.where(key_wide == slot_in, gate_wide, 0.0).astype(BF16)
    stores.append(pltpu.make_async_copy(mix_ref, mix_hbm, out_sems.at[EXPERTS // PICK]))
    stores[-1].start()
    for copy in stores:
        copy.wait()


def route(tokens, norm_gain, router_weight, expert_ids):
    shapes = [((ROWS, HALF), BF16), ((TOK_DEV, ROWS), BF16)]
    held = [((TOK_DEV, D), BF16), ((1, D), F32), ((EXPERTS, D), BF16), ((TOP, TOK_DEV), jnp.int32), ((2, TOK_DEV, HALF), BF16)]
    anywhere = pl.BlockSpec(memory_space=pl.ANY)
    return pl.pallas_call(
        route_kernel,
        in_specs=[anywhere] * 4,
        out_specs=[anywhere] * 2,
        out_shape=[jax.ShapeDtypeStruct(shape, kind) for shape, kind in shapes],
        scratch_shapes=[pltpu.VMEM(shape, kind) for shape, kind in held + shapes]
        + [pltpu.SemaphoreType.DMA((3 + TOK_DEV // ROUTE_BLOCK,)), pltpu.SemaphoreType.DMA((EXPERTS // PICK + 1,))],
        compiler_params=pltpu.CompilerParams(vmem_limit_bytes=ROUTE_VMEM),
        cost_estimate=pl.CostEstimate(flops=2 * ROWS * TOK_DEV * HALF, bytes_accessed=6_000_000, transcendentals=0),
    )(tokens, norm_gain.reshape(1, D), router_weight.T, expert_ids.T)


def product(rows, weight):
    return jnp.dot(rows, weight, preferred_element_type=F32)


def columns(weight, start, width):
    return lax.dynamic_slice_in_dim(weight, start, width, axis=1)


def mix_kernel(mix_ref, rows_ref, out_ref):
    out_ref[...] = jnp.dot(mix_ref[...], rows_ref[...], preferred_element_type=F32).astype(BF16)


def mix_add_kernel(tok_ref, mix_ref, rows_ref, out_ref):
    total = jnp.dot(mix_ref[...], rows_ref[...], preferred_element_type=F32)
    out_ref[...] = (tok_ref[...].astype(F32) + total).astype(BF16)


def mix(mix_matrix, rows):
    return pl.pallas_call(
        mix_kernel,
        out_shape=jax.ShapeDtypeStruct((TOK_DEV, rows.shape[1]), BF16),
        compiler_params=pltpu.CompilerParams(vmem_limit_bytes=MATMUL_VMEM),
        cost_estimate=pl.CostEstimate(flops=2 * TOK_DEV * rows.size, bytes_accessed=2_000_000, transcendentals=0),
    )(mix_matrix, rows)


def mix_add(tokens, mix_matrix, rows):
    return pl.pallas_call(
        mix_add_kernel,
        out_shape=jax.ShapeDtypeStruct((TOK_DEV, rows.shape[1]), BF16),
        compiler_params=pltpu.CompilerParams(vmem_limit_bytes=MATMUL_VMEM),
        cost_estimate=pl.CostEstimate(flops=2 * TOK_DEV * rows.size, bytes_accessed=2_000_000, transcendentals=0),
    )(tokens, mix_matrix, rows)


def assemble_kernel(at_ref, *refs):
    pieces, out_ref, sems = refs[:-2], refs[-2], refs[-1]
    copies = []
    for i, piece in enumerate(pieces):
        start = pl.multiple_of(at_ref[i] * 256, 256)
        copies.append(pltpu.make_async_copy(piece, out_ref.at[:, pl.ds(start, piece.shape[1])], sems.at[i]))
    for copy in copies:
        copy.start()
    for copy in copies:
        copy.wait()


def assemble(at, pieces):
    return pl.pallas_call(
        assemble_kernel,
        in_specs=[pl.BlockSpec(memory_space=pltpu.SMEM)] + [pl.BlockSpec(memory_space=pl.ANY)] * len(pieces),
        out_specs=pl.BlockSpec(memory_space=pl.ANY),
        out_shape=jax.ShapeDtypeStruct((TOK_DEV, D), BF16),
        scratch_shapes=[pltpu.SemaphoreType.DMA((len(pieces),))],
        compiler_params=pltpu.CompilerParams(vmem_limit_bytes=MATMUL_VMEM),
        cost_estimate=pl.CostEstimate(flops=0, bytes_accessed=3_000_000, transcendentals=0),
    )(at, *pieces)


def swap(values):
    return lax.ppermute(values, "pp", [(0, 1), (1, 0)])


def along_z(values, step):
    count = lax.axis_size("dp")
    return lax.ppermute(values, "dp", [(i, (i + step) % count) for i in range(count)])


def to_experts(rows):
    width = rows.shape[1]
    return lax.all_to_all(rows.reshape(EXPERTS, CAP, width), "ep", split_axis=0, concat_axis=0, tiled=True).reshape(ROWS, width)


def silu(value):
    return 0.5 * value * (1.0 + jnp.tanh(0.5 * value))


def after(earlier, values):
    return lax.optimization_barrier((earlier, values))[1]


def on_device(tokens, norm_gain, router_weight, expert_ids, up_weight, down_weight):
    core = lax.axis_index("pp").astype(jnp.int32)
    z = lax.axis_index("dp").astype(jnp.int32)
    other = 1 - core
    up = up_weight.reshape(2, HALF, up_weight.shape[2])
    down = down_weight[0]

    outgoing, mix_matrix = route(tokens, norm_gain, router_weight, expert_ids)
    token_wide = lax.dynamic_slice(tokens, (0, core * HALF), (TOK_DEV, WIDE))
    token_thin = lax.dynamic_slice(tokens, (0, core * HALF + WIDE + z * THIN), (TOK_DEV, THIN))
    mine = to_experts(outgoing)
    theirs = swap(mine)
    hidden = silu(product(mine, up[core]) + product(theirs, up[other])).astype(BF16)

    def partial_sums(start, width):
        got = swap(product(hidden, columns(down, other * HALF + start, width)).astype(BF16))
        return (product(hidden, columns(down, core * HALF + start, width)) + got.astype(F32)).astype(BF16)

    def place(step):
        return WIDE + (z + step) % 4 * THIN

    sent = [partial_sums(place(step), THIN) for step in Z_STEPS[:-1]]
    arrived = [along_z(piece, step) for piece, step in zip(sent, Z_STEPS[:-1])]
    wide = partial_sums(0, WIDE)
    kept = partial_sums(place(0), THIN)
    thin_sum = lax.optimization_barrier(kept).astype(F32)
    for piece in arrived:
        thin_sum = thin_sum + piece.astype(F32)
    wide_rows, thin_sum = lax.optimization_barrier((to_experts(wide), thin_sum.astype(BF16)))
    wide_part = mix(mix_matrix, wide_rows)
    thin_own = mix_add(token_thin, mix_matrix, to_experts(thin_sum))

    wide_own = token_wide.astype(F32) + wide_part.astype(F32)
    for step in Z_STEPS[:-1]:
        wide_own = wide_own + along_z(wide_part, step).astype(F32)
    wide_own = wide_own.astype(BF16)
    thin_all = [along_z(thin_own, step) for step in Z_STEPS[:-1]] + [thin_own]
    pieces = [wide_own, swap(wide_own)] + thin_all + [swap(piece) for piece in thin_all]
    sources = (z - jnp.array(Z_STEPS, jnp.int32)) % 4
    places = jnp.concatenate([jnp.stack([core * 6, other * 6]), core * 6 + 2 + sources, other * 6 + 2 + sources])
    return assemble(places.astype(jnp.int32), pieces)


def solution(mesh):
    in_specs = (
        P("ep", None),
        P(),
        P(),
        P("ep", None),
        P("ep", None, ("pp", "dp")),
        P("ep", ("pp", "dp"), None),
    )
    return jax.shard_map(on_device, mesh=mesh, in_specs=in_specs, out_specs=P("ep", None), check_vma=False)
```

time: 143 us -> 141 us (0.986)
    ppermute x9, starting transfers between devices: 14 us -> 12.1 us  [along_z(): lax.ppermute(values, 'dp', [(i, (i + step) % count) for i in range(count)])]
    all_to_all x2, waiting for transfers between devices: 4.37 us -> 6.14 us  [to_experts(): lax.all_to_all(rows.reshape(EXPERTS, CAP, width), 'ep', split_axis=0, con...]
    convert_element_type x1, other arithmetic: 2.63 us -> 1.15 us  [on_device(): thin_sum.astype(BF16)]
  transfers between devices with their start and end apart: 22 -> 22, of which waited for: 7 -> 6; matrix products, arithmetic and copies ran while one was open for 15% -> 14% of each run, Pallas kernels for 1% -> 1%
where the time goes in v5:
time: 141 us; the launch traced here: 140 us
  blocking collectives  50.6 us (36%)
  starting transfers between devices  30.9 us (22%)
  matrix products  23.8 us (17%)
  waiting for transfers between devices  23.2 us (16%)
  Pallas kernels  8.26 us (6%)
  other arithmetic  2.36 us (2%)
    all_to_all x1, blocking collectives, to_experts(): lax.all_to_all(rows.reshape(EXPERTS, CAP, width), 'ep', split_axis=0, con...  50.6 us
    dot_general x12, matrix products, product(): return jnp.dot(rows, weight, preferred_element_type=F32)  23.8 us
    ppermute x9, waiting for transfers between devices, along_z(): lax.ppermute(values, 'dp', [(i, (i + step) % count) for i in range(count)])  14.9 us
    ppermute x9, starting transfers between devices, along_z(): lax.ppermute(values, 'dp', [(i, (i + step) % count) for i in range(count)])  12.1 us
    ppermute x11, starting transfers between devices, swap(): return lax.ppermute(values, 'pp', [(0, 1), (1, 0)])  10.7 us
    all_to_all x2, starting transfers between devices, to_experts(): lax.all_to_all(rows.reshape(EXPERTS, CAP, width), 'ep', split_axis=0, con...  8.12 us
    all_to_all x2, waiting for transfers between devices, to_experts(): lax.all_to_all(rows.reshape(EXPERTS, CAP, width), 'ep', split_axis=0, con...  6.14 us
    pallas_call x1, Pallas kernels, route(): pl.pallas_call(route_kernel, in_specs=[anywhere] * 4, out_specs=[anywhere...  5.66 us
  transfers between devices with their start and end apart: 22, of which 6 were waited for; matrix products, arithmetic and copies ran while one was open for 14% of the time, Pallas kernels for 1%

profile of v5, /device:TPU:1, one launch (start us, length us, event | category | flops | bytes accessed | tf_op | source)
XLA Modules:
  0.0 140.4 jit_solution(13817533116658390725)
XLA Ops:
  0.0 5.7 %shard_map.73 = (bf16[1152,1536]{1,0:T(8,128)(2,1)}, bf16[256,1152]{1,0:T(8,128)(2,1)}) custom-call(bf16[256,3072]{1,0:T(8,128)(2,1)} %tok_hbm.1, f32[1,3072]{1,0:T(1,128)} %bitcast.80, bf16[16,3072]{1,0:T(8,128)(2,1)} %bitcast.79, s32[4,256]{1,0:T(4,128)} %bitcast.81), custom_call_target="tpu_custom_call" | custom-call | flops 905969664 | bytes 6000000 | tf_op jit(solution)/shard_map/pallas_call | solution.py:110
  5.7 50.6 %all_to_all.15 = bf16[16,72,1536]{2,1,0:T(8,128)(2,1)S(1)} all-to-all(bf16[16,72,1536]{2,1,0:T(8,128)(2,1)} %bitcast.74), channel_id=1, replica_groups=mesh['pp'=2,'ep'=16,'dp'=4] {'ep'}, dimensions={0} | all-to-all | bytes 7077888 | tf_op jit(solution)/shard_map/all_to_all | solution.py:192
  56.2 1.8 %collective-permute-start = (bf16[1152,1536]{1,0:T(8,128)(2,1)S(1)}, bf16[1152,1536]{1,0:T(8,128)(2,1)}, u32[]{:S(2)}, u32[]{:S(2)}) collective-permute-start(bf16[1152,1536]{1,0:T(8,128)(2,1)S(1)} %bitcast.72), channel_id=1, source_target_pairs={{0,64},{64,0},{1,65},{65,1},{2,66},{66,2},{3,67},{67,3},{4,68},{68... | collective-permute-start | bytes 10616840 | tf_op jit(solution)/shard_map/ppermute | solution.py:182
  58.1 4.7 %fusion.2 = f32[1152,768]{1,0:T(8,128)S(1)} fusion(bf16[1152,1536]{1,0:T(8,128)(2,1)S(1)} %bitcast.73, bf16[2,1536,768]{2,1,0:T(8,128)(2,1)} %bitcast.75, s32[]{:T(128)S(6)} %select_n.67), kind=kOutput, calls=%fused_computation.9 | convolution fusion | flops 2717908992 | bytes 9437188 | tf_op jit(solution)/shard_map/dot_general | solution.py:123
  64.0 5.9 %multiply_convert_fusion = bf16[1152,768]{1,0:T(8,128)(2,1)S(1)} fusion(f32[1152,768]{1,0:T(8,128)S(1)} %fusion.2, bf16[1152,1536]{1,0:T(8,128)(2,1)} %collective-permute-done, bf16[2,1536,768]{2,1,0:T(8,128)(2,1)} %bitcast.76, s32[]{:T(128)S(6)} %select_n.68), kind=kOutput, calls=%fused_computation.2 | convolution fusion | flops 2722332672 | bytes 11206660 | tf_op jit(solution)/shard_map/dot_general | solution.py:123
  74.5 1.5 %convolution_convert_fusion.4 = bf16[1152,256]{1,0:T(8,128)(2,1)} fusion(bf16[1152,768]{1,0:T(8,128)(2,1)S(1)} %multiply_convert_fusion, bf16[1,768,3072]{2,1,0:T(8,128)(2,1)S(1)} %bitcast.78, s32[]{:T(128)S(6)} %select_n.72), kind=kOutput, calls=%fused_computation.7 | convolution fusion | flops 453279744 | bytes 2752516 | tf_op jit(solution)/shard_map/dot_general | solution.py:123
  76.4 1.5 %add_convert_fusion.2 = bf16[1152,256]{1,0:T(8,128)(2,1)} fusion(bf16[1152,256]{1,0:T(8,128)(2,1)S(1)} %collective-permute-done.7, bf16[1152,768]{1,0:T(8,128)(2,1)S(1)} %multiply_convert_fusion, bf16[1,768,3072]{2,1,0:T(8,128)(2,1)S(1)} %bitcast.78, s32[]{:T(128)S(6)} %select_n.80), kind=kOutput, calls=%fused_computation.15 | convolution fusion | flops 453869568 | bytes 3342340 | tf_op jit(solution)/shard_map/dot_general | solution.py:123
  77.9 3.6 %collective-permute-start.8 = (bf16[1152,256]{1,0:T(8,128)(2,1)}, bf16[1152,256]{1,0:T(8,128)(2,1)S(1)}, u32[]{:S(2)}, u32[]{:S(2)}) collective-permute-start(bf16[1152,256]{1,0:T(8,128)(2,1)} %add_convert_fusion.2), channel_id=1, source_target_pairs={{0,2},{1,3},{2,0},{3,1},{4,6},{5,7},{6,4},{7,5},{8,10},{9,11},{10,... | collective-permute-start | bytes 1769480 | tf_op jit(solution)/shard_map/ppermute | solution.py:187
  81.5 1.5 %add_convert_fusion.3 = bf16[1152,256]{1,0:T(8,128)(2,1)} fusion(bf16[1152,256]{1,0:T(8,128)(2,1)S(1)} %collective-permute-done.5, bf16[1152,768]{1,0:T(8,128)(2,1)S(1)} %multiply_convert_fusion, bf16[1,768,3072]{2,1,0:T(8,128)(2,1)S(1)} %bitcast.78, s32[]{:T(128)S(6)} %select_n.77), kind=kOutput, calls=%fused_computation.16 | convolution fusion | flops 453869568 | bytes 3342340 | tf_op jit(solution)/shard_map/dot_general | solution.py:123
  83.4 1.5 %add_convert_fusion.4 = bf16[1152,256]{1,0:T(8,128)(2,1)} fusion(bf16[1152,256]{1,0:T(8,128)(2,1)S(1)} %collective-permute-done.3, bf16[1152,768]{1,0:T(8,128)(2,1)S(1)} %multiply_convert_fusion, bf16[1,768,3072]{2,1,0:T(8,128)(2,1)S(1)} %bitcast.78, s32[]{:T(128)S(6)} %select_n.74), kind=kOutput, calls=%fused_computation.17 | convolution fusion | flops 453869568 | bytes 3342340 | tf_op jit(solution)/shard_map/dot_general | solution.py:123
  85.9 2.1 %add_convert_fusion = bf16[1152,512]{1,0:T(8,128)(2,1)} fusion(bf16[1152,512]{1,0:T(8,128)(2,1)S(1)} %collective-permute-done.1, bf16[1152,768]{1,0:T(8,128)(2,1)S(1)} %multiply_convert_fusion, bf16[1,768,3072]{2,1,0:T(8,128)(2,1)S(1)} %bitcast.78, s32[]{:T(128)S(6)} %select_n.66), kind=kOutput, calls=%fused_computation.11 | convolution fusion | flops 907739136 | bytes 4915204 | tf_op jit(solution)/shard_map/dot_general | solution.py:123
  88.1 3.7 %all-to-all-start.1 = ((bf16[16,72,512]{2,1,0:T(8,128)(2,1)}), bf16[16,72,512]{2,1,0:T(8,128)(2,1)S(1)}, u32[]{:S(2)}, u32[]{:S(2)}) async-start(bf16[16,72,512]{2,1,0:T(8,128)(2,1)} %bitcast.12), calls=%async_computation.1 | async-start | bytes 2359296 | tf_op jit(solution)/shard_map/all_to_all | solution.py:192
  91.8 2.2 %add_convert_fusion.5 = bf16[1152,256]{1,0:T(8,128)(2,1)S(1)} fusion(bf16[1152,256]{1,0:T(8,128)(2,1)S(1)} %collective-permute-done.2, bf16[1152,768]{1,0:T(8,128)(2,1)} %copy-done.2, bf16[1,768,3072]{2,1,0:T(8,128)(2,1)} %param.12, s32[]{:T(128)S(6)} %select_n.71), kind=kOutput, calls=%fused_computation.18 | convolution fusion | flops 453869568 | bytes 3342340 | tf_op jit(solution)/shard_map/dot_general | solution.py:123
  94.0 1.4 collective-permute-done.8
  95.4 13.2 %collective-permute-done.6 = bf16[1152,256]{1,0:T(8,128)(2,1)S(1)} collective-permute-done((bf16[1152,256]{1,0:T(8,128)(2,1)}, bf16[1152,256]{1,0:T(8,128)(2,1)S(1)}, u32[]{:S(2)}, u32[]{:S(2)}) %collective-permute-start.6) | collective-permute-done | bytes 589856 | tf_op jit(solution)/shard_map/ppermute | solution.py:187
  109.7 4.4 %all-to-all-start.2 = ((bf16[16,72,256]{2,1,0:T(8,128)(2,1)}), bf16[16,72,256]{2,1,0:T(8,128)(2,1)S(1)}, u32[]{:S(2)}, u32[]{:S(2)}) async-start(bf16[16,72,256]{2,1,0:T(8,128)(2,1)} %bitcast.22), calls=%async_computation.2 | async-start | bytes 1179648 | tf_op jit(solution)/shard_map/all_to_all | solution.py:192
  114.7 1.9 %collective-permute-start.11 = (bf16[256,512]{1,0:T(8,128)(2,1)S(1)}, bf16[256,512]{1,0:T(8,128)(2,1)S(1)}, u32[]{:S(2)}, u32[]{:S(2)}) collective-permute-start(bf16[256,512]{1,0:T(8,128)(2,1)S(1)} %shard_map.74), channel_id=1, source_target_pairs={{0,2},{1,3},{2,0},{3,1},{4,6},{5,7},{6,4},{7,5},{8,10},{9,11},{10,... | collective-permute-start | bytes 786440 | tf_op jit(solution)/shard_map/ppermute | solution.py:187
  116.6 1.3 collective-permute-start.10
  119.0 6.1 %all-to-all-done.2 = bf16[16,72,256]{2,1,0:T(8,128)(2,1)S(1)} async-done(((bf16[16,72,256]{2,1,0:T(8,128)(2,1)}), bf16[16,72,256]{2,1,0:T(8,128)(2,1)S(1)}, u32[]{:S(2)}, u32[]{:S(2)}) %all-to-all-start.2) | async-done | bytes 589856 | tf_op jit(solution)/shard_map/all_to_all | solution.py:192
  126.3 2.0 %collective-permute-start.14 = (bf16[256,256]{1,0:T(8,128)(2,1)S(1)}, bf16[256,256]{1,0:T(8,128)(2,1)S(1)}, u32[]{:S(2)}, u32[]{:S(2)}) collective-permute-start(bf16[256,256]{1,0:T(8,128)(2,1)S(1)} %shard_map.75.refs_5_), channel_id=1, source_target_pairs={{0,3},{1,0},{2,1},{3,2},{4,7},{5,4},{6,5},{7,6},{8,11},{9,8},{10,9... | collective-permute-start | bytes 393224 | tf_op jit(solution)/shard_map/ppermute | solution.py:187
  130.5 2.6 %collective-permute-start.12 = (bf16[256,512]{1,0:T(8,128)(2,1)S(1)}, bf16[256,512]{1,0:T(8,128)(2,1)S(1)}, u32[]{:S(2)}, u32[]{:S(2)}) collective-permute-start(bf16[256,512]{1,0:T(8,128)(2,1)S(1)} %add_convert_fusion.6.refs_0_), channel_id=1, source_target_pairs={{0,64},{64,0},{1,65},{65,1},{2,66},{66,2},{3,67},{67,3},{4,68},{68... | collective-permute-start | bytes 786440 | tf_op jit(solution)/shard_map/ppermute | solution.py:182
  133.2 2.0 %collective-permute-start.16 = (bf16[256,256]{1,0:T(8,128)(2,1)S(1)}, bf16[256,256]{1,0:T(8,128)(2,1)S(1)}, u32[]{:S(2)}, u32[]{:S(2)}) collective-permute-start(bf16[256,256]{1,0:T(8,128)(2,1)S(1)} %collective-permute-done.13.refs_2_), channel_id=1, source_target_pairs={{0,64},{64,0},{1,65},{65,1},{2,66},{66,2},{3,67},{67,3},{4,68},{68... | collective-permute-start | bytes 393224 | tf_op jit(solution)/shard_map/ppermute | solution.py:182
  135.3 2.2 %collective-permute-start.18 = (bf16[256,256]{1,0:T(8,128)(2,1)S(1)}, bf16[256,256]{1,0:T(8,128)(2,1)S(1)}, u32[]{:S(2)}, u32[]{:S(2)}) collective-permute-start(bf16[256,256]{1,0:T(8,128)(2,1)S(1)} %collective-permute-done.15.refs_4_), channel_id=1, source_target_pairs={{0,64},{64,0},{1,65},{65,1},{2,66},{66,2},{3,67},{67,3},{4,68},{68... | collective-permute-start | bytes 393224 | tf_op jit(solution)/shard_map/ppermute | solution.py:182
  138.5 1.8 %shard_map.76 = bf16[256,3072]{1,0:T(8,128)(2,1)} custom-call(s32[10]{0:T(128)S(1)} %pad_add_fusion.at_ref, bf16[256,512]{1,0:T(8,128)(2,1)S(1)} %add_convert_fusion.6.refs_0_, bf16[256,512]{1,0:T(8,128)(2,1)S(1)} %collective-permute-done.12.refs_1_, bf16[256,256]{1,0:T(8,128)(2,1)S(1)} %collective-permute-done.13.refs_2_, ...), custom_call_target="tpu_custom_call" | custom-call | bytes 3000000 | tf_op jit(solution)/shard_map/pallas_call | solution.py:170
  (54 shorter events, 15.0 us)
Async XLA Ops:
  56.2 7.8 %collective-permute-start = (bf16[1152,1536]{1,0:T(8,128)(2,1)S(1)}, bf16[1152,1536]{1,0:T(8,128)(2,1)}, u32[]{:S(2)}, u32[]{:S(2)}) collective-permute-start(bf16[1152,1536]{1,0:T(8,128)(2,1)S(1)} %bitcast.72), channel_id=1, source_target_pairs={{0,64},{64,0},{1,65},{65,1},{2,66},{66,2},{3,67},{67,3},{4,68},{68... | collective-permute-start | bytes 10616840 | tf_op jit(solution)/shard_map/ppermute | solution.py:182
  70.0 15.9 %copy-start.2 = (bf16[1152,768]{1,0:T(8,128)(2,1)}, bf16[1152,768]{1,0:T(8,128)(2,1)S(1)}, u32[]{:S(2)}) copy-start(bf16[1152,768]{1,0:T(8,128)(2,1)S(1)} %multiply_convert_fusion) | copy-start | bytes 5308420
  71.1 14.8 %collective-permute-start.1 = (bf16[1152,512]{1,0:T(8,128)(2,1)S(1)}, bf16[1152,512]{1,0:T(8,128)(2,1)S(1)}, u32[]{:S(2)}, u32[]{:S(2)}) collective-permute-start(bf16[1152,512]{1,0:T(8,128)(2,1)S(1)} %convolution_convert_fusion), channel_id=1, source_target_pairs={{0,64},{64,0},{1,65},{65,1},{2,66},{66,2},{3,67},{67,3},{4,68},{68... | collective-permute-start | bytes 3538952 | tf_op jit(solution)/shard_map/ppermute | solution.py:182
  72.2 4.2 %collective-permute-start.7 = (bf16[1152,256]{1,0:T(8,128)(2,1)S(1)}, bf16[1152,256]{1,0:T(8,128)(2,1)S(1)}, u32[]{:S(2)}, u32[]{:S(2)}) collective-permute-start(bf16[1152,256]{1,0:T(8,128)(2,1)S(1)} %convolution_convert_fusion.1), channel_id=1, source_target_pairs={{0,64},{64,0},{1,65},{65,1},{2,66},{66,2},{3,67},{67,3},{4,68},{68... | collective-permute-start | bytes 1769480 | tf_op jit(solution)/shard_map/ppermute | solution.py:182
  73.0 8.5 %collective-permute-start.5 = (bf16[1152,256]{1,0:T(8,128)(2,1)S(1)}, bf16[1152,256]{1,0:T(8,128)(2,1)S(1)}, u32[]{:S(2)}, u32[]{:S(2)}) collective-permute-start(bf16[1152,256]{1,0:T(8,128)(2,1)S(1)} %convolution_convert_fusion.2), channel_id=1, source_target_pairs={{0,64},{64,0},{1,65},{65,1},{2,66},{66,2},{3,67},{67,3},{4,68},{68... | collective-permute-start | bytes 1769480 | tf_op jit(solution)/shard_map/ppermute | solution.py:182
  74.2 9.2 %collective-permute-start.3 = (bf16[1152,256]{1,0:T(8,128)(2,1)S(1)}, bf16[1152,256]{1,0:T(8,128)(2,1)S(1)}, u32[]{:S(2)}, u32[]{:S(2)}) collective-permute-start(bf16[1152,256]{1,0:T(8,128)(2,1)S(1)} %convolution_convert_fusion.3), channel_id=1, source_target_pairs={{0,64},{64,0},{1,65},{65,1},{2,66},{66,2},{3,67},{67,3},{4,68},{68... | collective-permute-start | bytes 1769480 | tf_op jit(solution)/shard_map/ppermute | solution.py:182
  76.0 15.8 %collective-permute-start.2 = (bf16[1152,256]{1,0:T(8,128)(2,1)}, bf16[1152,256]{1,0:T(8,128)(2,1)S(1)}, u32[]{:S(2)}, u32[]{:S(2)}) collective-permute-start(bf16[1152,256]{1,0:T(8,128)(2,1)} %convolution_convert_fusion.4), channel_id=1, source_target_pairs={{0,64},{64,0},{1,65},{65,1},{2,66},{66,2},{3,67},{67,3},{4,68},{68... | collective-permute-start | bytes 1769480 | tf_op jit(solution)/shard_map/ppermute | solution.py:182
  77.9 17.5 %collective-permute-start.8 = (bf16[1152,256]{1,0:T(8,128)(2,1)}, bf16[1152,256]{1,0:T(8,128)(2,1)S(1)}, u32[]{:S(2)}, u32[]{:S(2)}) collective-permute-start(bf16[1152,256]{1,0:T(8,128)(2,1)} %add_convert_fusion.2), channel_id=1, source_target_pairs={{0,2},{1,3},{2,0},{3,1},{4,6},{5,7},{6,4},{7,5},{8,10},{9,11},{10,... | collective-permute-start | bytes 1769480 | tf_op jit(solution)/shard_map/ppermute | solution.py:187
  83.0 25.6 %collective-permute-start.6 = (bf16[1152,256]{1,0:T(8,128)(2,1)}, bf16[1152,256]{1,0:T(8,128)(2,1)S(1)}, u32[]{:S(2)}, u32[]{:S(2)}) collective-permute-start(bf16[1152,256]{1,0:T(8,128)(2,1)} %add_convert_fusion.3), channel_id=1, source_target_pairs={{0,3},{1,0},{2,1},{3,2},{4,7},{5,4},{6,5},{7,6},{8,11},{9,8},{10,9... | collective-permute-start | bytes 1769480 | tf_op jit(solution)/shard_map/ppermute | solution.py:187
  84.9 23.7 %collective-permute-start.4 = (bf16[1152,256]{1,0:T(8,128)(2,1)}, bf16[1152,256]{1,0:T(8,128)(2,1)S(1)}, u32[]{:S(2)}, u32[]{:S(2)}) collective-permute-start(bf16[1152,256]{1,0:T(8,128)(2,1)} %add_convert_fusion.4), channel_id=1, source_target_pairs={{0,1},{1,2},{2,3},{3,0},{4,5},{5,6},{6,7},{7,4},{8,9},{9,10},{10,1... | collective-permute-start | bytes 1769480 | tf_op jit(solution)/shard_map/ppermute | solution.py:187
  88.1 21.7 %all-to-all-start.1 = ((bf16[16,72,512]{2,1,0:T(8,128)(2,1)}), bf16[16,72,512]{2,1,0:T(8,128)(2,1)S(1)}, u32[]{:S(2)}, u32[]{:S(2)}) async-start(bf16[16,72,512]{2,1,0:T(8,128)(2,1)} %bitcast.12), calls=%async_computation.1 | async-start | bytes 2359296 | tf_op jit(solution)/shard_map/all_to_all | solution.py:192
  93.9 20.2 %copy-start = (bf16[256,1152]{1,0:T(8,128)(2,1)S(1)}, bf16[256,1152]{1,0:T(8,128)(2,1)}, u32[]{:S(2)}) copy-start(bf16[256,1152]{1,0:T(8,128)(2,1)} %get-tuple-element.9.mix_ref) | copy-start | bytes 1769476
  109.7 15.4 %all-to-all-start.2 = ((bf16[16,72,256]{2,1,0:T(8,128)(2,1)}), bf16[16,72,256]{2,1,0:T(8,128)(2,1)S(1)}, u32[]{:S(2)}, u32[]{:S(2)}) async-start(bf16[16,72,256]{2,1,0:T(8,128)(2,1)} %bitcast.22), calls=%async_computation.2 | async-start | bytes 1179648 | tf_op jit(solution)/shard_map/all_to_all | solution.py:192
  114.7 13.6 %collective-permute-start.11 = (bf16[256,512]{1,0:T(8,128)(2,1)S(1)}, bf16[256,512]{1,0:T(8,128)(2,1)S(1)}, u32[]{:S(2)}, u32[]{:S(2)}) collective-permute-start(bf16[256,512]{1,0:T(8,128)(2,1)S(1)} %shard_map.74), channel_id=1, source_target_pairs={{0,2},{1,3},{2,0},{3,1},{4,6},{5,7},{6,4},{7,5},{8,10},{9,11},{10,... | collective-permute-start | bytes 786440 | tf_op jit(solution)/shard_map/ppermute | solution.py:187
  116.6 12.6 %collective-permute-start.10 = (bf16[256,512]{1,0:T(8,128)(2,1)S(1)}, bf16[256,512]{1,0:T(8,128)(2,1)S(1)}, u32[]{:S(2)}, u32[]{:S(2)}) collective-permute-start(bf16[256,512]{1,0:T(8,128)(2,1)S(1)} %shard_map.74), channel_id=1, source_target_pairs={{0,3},{1,0},{2,1},{3,2},{4,7},{5,4},{6,5},{7,6},{8,11},{9,8},{10,9... | collective-permute-start | bytes 786440 | tf_op jit(solution)/shard_map/ppermute | solution.py:187
  117.9 11.5 %collective-permute-start.9 = (bf16[256,512]{1,0:T(8,128)(2,1)S(1)}, bf16[256,512]{1,0:T(8,128)(2,1)S(1)}, u32[]{:S(2)}, u32[]{:S(2)}) collective-permute-start(bf16[256,512]{1,0:T(8,128)(2,1)S(1)} %shard_map.74), channel_id=1, source_target_pairs={{0,1},{1,2},{2,3},{3,0},{4,5},{5,6},{6,7},{7,4},{8,9},{9,10},{10,1... | collective-permute-start | bytes 786440 | tf_op jit(solution)/shard_map/ppermute | solution.py:187
  125.5 7.7 %collective-permute-start.13 = (bf16[256,256]{1,0:T(8,128)(2,1)S(1)}, bf16[256,256]{1,0:T(8,128)(2,1)S(1)}, u32[]{:S(2)}, u32[]{:S(2)}) collective-permute-start(bf16[256,256]{1,0:T(8,128)(2,1)S(1)} %shard_map.75.refs_5_), channel_id=1, source_target_pairs={{0,1},{1,2},{2,3},{3,0},{4,5},{5,6},{6,7},{7,4},{8,9},{9,10},{10,1... | collective-permute-start | bytes 393224 | tf_op jit(solution)/shard_map/ppermute | solution.py:187
  126.3 8.9 %collective-permute-start.14 = (bf16[256,256]{1,0:T(8,128)(2,1)S(1)}, bf16[256,256]{1,0:T(8,128)(2,1)S(1)}, u32[]{:S(2)}, u32[]{:S(2)}) collective-permute-start(bf16[256,256]{1,0:T(8,128)(2,1)S(1)} %shard_map.75.refs_5_), channel_id=1, source_target_pairs={{0,3},{1,0},{2,1},{3,2},{4,7},{5,4},{6,5},{7,6},{8,11},{9,8},{10,9... | collective-permute-start | bytes 393224 | tf_op jit(solution)/shard_map/ppermute | solution.py:187
  128.3 7.0 %collective-permute-start.15 = (bf16[256,256]{1,0:T(8,128)(2,1)S(1)}, bf16[256,256]{1,0:T(8,128)(2,1)S(1)}, u32[]{:S(2)}, u32[]{:S(2)}) collective-permute-start(bf16[256,256]{1,0:T(8,128)(2,1)S(1)} %shard_map.75.refs_5_), channel_id=1, source_target_pairs={{0,2},{1,3},{2,0},{3,1},{4,6},{5,7},{6,4},{7,5},{8,10},{9,11},{10,... | collective-permute-start | bytes 393224 | tf_op jit(solution)/shard_map/ppermute | solution.py:187
  130.5 7.0 %collective-permute-start.12 = (bf16[256,512]{1,0:T(8,128)(2,1)S(1)}, bf16[256,512]{1,0:T(8,128)(2,1)S(1)}, u32[]{:S(2)}, u32[]{:S(2)}) collective-permute-start(bf16[256,512]{1,0:T(8,128)(2,1)S(1)} %add_convert_fusion.6.refs_0_), channel_id=1, source_target_pairs={{0,64},{64,0},{1,65},{65,1},{2,66},{66,2},{3,67},{67,3},{4,68},{68... | collective-permute-start | bytes 786440 | tf_op jit(solution)/shard_map/ppermute | solution.py:182
  133.1 4.5 %collective-permute-start.19 = (bf16[256,256]{1,0:T(8,128)(2,1)S(1)}, bf16[256,256]{1,0:T(8,128)(2,1)S(1)}, u32[]{:S(2)}, u32[]{:S(2)}) collective-permute-start(bf16[256,256]{1,0:T(8,128)(2,1)S(1)} %shard_map.75.refs_5_), channel_id=1, source_target_pairs={{0,64},{64,0},{1,65},{65,1},{2,66},{66,2},{3,67},{67,3},{4,68},{68... | collective-permute-start | bytes 393224 | tf_op jit(solution)/shard_map/ppermute | solution.py:182
  133.2 4.4 %collective-permute-start.16 = (bf16[256,256]{1,0:T(8,128)(2,1)S(1)}, bf16[256,256]{1,0:T(8,128)(2,1)S(1)}, u32[]{:S(2)}, u32[]{:S(2)}) collective-permute-start(bf16[256,256]{1,0:T(8,128)(2,1)S(1)} %collective-permute-done.13.refs_2_), channel_id=1, source_target_pairs={{0,64},{64,0},{1,65},{65,1},{2,66},{66,2},{3,67},{67,3},{4,68},{68... | collective-permute-start | bytes 393224 | tf_op jit(solution)/shard_map/ppermute | solution.py:182
  135.2 2.4 %collective-permute-start.17 = (bf16[256,256]{1,0:T(8,128)(2,1)S(1)}, bf16[256,256]{1,0:T(8,128)(2,1)S(1)}, u32[]{:S(2)}, u32[]{:S(2)}) collective-permute-start(bf16[256,256]{1,0:T(8,128)(2,1)S(1)} %collective-permute-done.14.refs_3_), channel_id=1, source_target_pairs={{0,64},{64,0},{1,65},{65,1},{2,66},{66,2},{3,67},{67,3},{4,68},{68... | collective-permute-start | bytes 393224 | tf_op jit(solution)/shard_map/ppermute | solution.py:182
  135.3 3.2 %collective-permute-start.18 = (bf16[256,256]{1,0:T(8,128)(2,1)S(1)}, bf16[256,256]{1,0:T(8,128)(2,1)S(1)}, u32[]{:S(2)}, u32[]{:S(2)}) collective-permute-start(bf16[256,256]{1,0:T(8,128)(2,1)S(1)} %collective-permute-done.15.refs_4_), channel_id=1, source_target_pairs={{0,64},{64,0},{1,65},{65,1},{2,66},{66,2},{3,67},{67,3},{4,68},{68... | collective-permute-start | bytes 393224 | tf_op jit(solution)/shard_map/ppermute | solution.py:182
  (3 other events, 28.4 us)

commit v6 on v5

--- a/solution.py
+++ b/solution.py
@@ -15,6 +15,7 @@
 WIDE = 512
 THIN = 256
 Z_STEPS = (1, 3, 2, 0)
+TAIL_STEPS = (2, 1, 3, 0)
 EPSILON = 1e-05
 F32 = jnp.float32
 BF16 = jnp.bfloat16
@@ -236,9 +237,9 @@
     for step in Z_STEPS[:-1]:
         wide_own = wide_own + along_z(wide_part, step).astype(F32)
     wide_own = wide_own.astype(BF16)
-    thin_all = [along_z(thin_own, step) for step in Z_STEPS[:-1]] + [thin_own]
+    thin_all = [along_z(thin_own, step) for step in TAIL_STEPS[:-1]] + [thin_own]
     pieces = [wide_own, swap(wide_own)] + thin_all + [swap(piece) for piece in thin_all]
-    sources = (z - jnp.array(Z_STEPS, jnp.int32)) % 4
+    sources = (z - jnp.array(TAIL_STEPS, jnp.int32)) % 4
     places = jnp.concatenate([jnp.stack([core * 6, other * 6]), core * 6 + 2 + sources, other * 6 + 2 + sources])
     return assemble(places.astype(jnp.int32), pieces)
 

time: 141 us -> 140 us (level)
    ppermute x11, starting transfers between devices: 10.7 us -> 8.44 us  [swap(): return lax.ppermute(values, 'pp', [(0, 1), (1, 0)])]
where the time goes in v6:
time: 140 us; the launch traced here: 139 us
  blocking collectives  50.6 us (36%)
  starting transfers between devices  29.9 us (21%)
  matrix products  23.8 us (17%)
  waiting for transfers between devices  23.3 us (17%)
  Pallas kernels  8.26 us (6%)
  other arithmetic  2.36 us (2%)
    all_to_all x1, blocking collectives, to_experts(): lax.all_to_all(rows.reshape(EXPERTS, CAP, width), 'ep', split_axis=0, con...  50.6 us
    dot_general x12, matrix products, product(): return jnp.dot(rows, weight, preferred_element_type=F32)  23.8 us
    ppermute x9, waiting for transfers between devices, along_z(): lax.ppermute(values, 'dp', [(i, (i + step) % count) for i in range(count)])  14.6 us
    ppermute x9, starting transfers between devices, along_z(): lax.ppermute(values, 'dp', [(i, (i + step) % count) for i in range(count)])  13.4 us
    ppermute x11, starting transfers between devices, swap(): return lax.ppermute(values, 'pp', [(0, 1), (1, 0)])  8.44 us
    all_to_all x2, starting transfers between devices, to_experts(): lax.all_to_all(rows.reshape(EXPERTS, CAP, width), 'ep', split_axis=0, con...  8.12 us
    all_to_all x2, waiting for transfers between devices, to_experts(): lax.all_to_all(rows.reshape(EXPERTS, CAP, width), 'ep', split_axis=0, con...  6.14 us
    pallas_call x1, Pallas kernels, route(): pl.pallas_call(route_kernel, in_specs=[anywhere] * 4, out_specs=[anywhere...  5.66 us
  transfers between devices with their start and end apart: 22, of which 6 were waited for; matrix products, arithmetic and copies ran while one was open for 14% of the time, Pallas kernels for 1%

profile of v6, /device:TPU:1, one launch (start us, length us, event | category | flops | bytes accessed | tf_op | source)
XLA Modules:
  0.0 139.5 jit_solution(4404209125392564827)
XLA Ops:
  0.0 5.7 %shard_map.73 = (bf16[1152,1536]{1,0:T(8,128)(2,1)}, bf16[256,1152]{1,0:T(8,128)(2,1)}) custom-call(bf16[256,3072]{1,0:T(8,128)(2,1)} %tok_hbm.1, f32[1,3072]{1,0:T(1,128)} %bitcast.80, bf16[16,3072]{1,0:T(8,128)(2,1)} %bitcast.79, s32[4,256]{1,0:T(4,128)} %bitcast.81), custom_call_target="tpu_custom_call" | custom-call | flops 905969664 | bytes 6000000 | tf_op jit(solution)/shard_map/pallas_call | solution.py:111
  5.7 50.6 %all_to_all.15 = bf16[16,72,1536]{2,1,0:T(8,128)(2,1)S(1)} all-to-all(bf16[16,72,1536]{2,1,0:T(8,128)(2,1)} %bitcast.74), channel_id=1, replica_groups=mesh['pp'=2,'ep'=16,'dp'=4] {'ep'}, dimensions={0} | all-to-all | bytes 7077888 | tf_op jit(solution)/shard_map/all_to_all | solution.py:193
  56.2 1.8 %collective-permute-start = (bf16[1152,1536]{1,0:T(8,128)(2,1)S(1)}, bf16[1152,1536]{1,0:T(8,128)(2,1)}, u32[]{:S(2)}, u32[]{:S(2)}) collective-permute-start(bf16[1152,1536]{1,0:T(8,128)(2,1)S(1)} %bitcast.72), channel_id=1, source_target_pairs={{0,64},{64,0},{1,65},{65,1},{2,66},{66,2},{3,67},{67,3},{4,68},{68... | collective-permute-start | bytes 10616840 | tf_op jit(solution)/shard_map/ppermute | solution.py:183
  58.1 4.7 %fusion.2 = f32[1152,768]{1,0:T(8,128)S(1)} fusion(bf16[1152,1536]{1,0:T(8,128)(2,1)S(1)} %bitcast.73, bf16[2,1536,768]{2,1,0:T(8,128)(2,1)} %bitcast.75, s32[]{:T(128)S(6)} %select_n.67), kind=kOutput, calls=%fused_computation.9 | convolution fusion | flops 2717908992 | bytes 9437188 | tf_op jit(solution)/shard_map/dot_general | solution.py:124
  64.0 5.9 %multiply_convert_fusion = bf16[1152,768]{1,0:T(8,128)(2,1)S(1)} fusion(f32[1152,768]{1,0:T(8,128)S(1)} %fusion.2, bf16[1152,1536]{1,0:T(8,128)(2,1)} %collective-permute-done, bf16[2,1536,768]{2,1,0:T(8,128)(2,1)} %bitcast.76, s32[]{:T(128)S(6)} %select_n.68), kind=kOutput, calls=%fused_computation.2 | convolution fusion | flops 2722332672 | bytes 11206660 | tf_op jit(solution)/shard_map/dot_general | solution.py:124
  74.5 1.5 %convolution_convert_fusion.4 = bf16[1152,256]{1,0:T(8,128)(2,1)} fusion(bf16[1152,768]{1,0:T(8,128)(2,1)S(1)} %multiply_convert_fusion, bf16[1,768,3072]{2,1,0:T(8,128)(2,1)S(1)} %bitcast.78, s32[]{:T(128)S(6)} %select_n.72), kind=kOutput, calls=%fused_computation.7 | convolution fusion | flops 453279744 | bytes 2752516 | tf_op jit(solution)/shard_map/dot_general | solution.py:124
  76.4 1.5 %add_convert_fusion.2 = bf16[1152,256]{1,0:T(8,128)(2,1)} fusion(bf16[1152,256]{1,0:T(8,128)(2,1)S(1)} %collective-permute-done.7, bf16[1152,768]{1,0:T(8,128)(2,1)S(1)} %multiply_convert_fusion, bf16[1,768,3072]{2,1,0:T(8,128)(2,1)S(1)} %bitcast.78, s32[]{:T(128)S(6)} %select_n.80), kind=kOutput, calls=%fused_computation.15 | convolution fusion | flops 453869568 | bytes 3342340 | tf_op jit(solution)/shard_map/dot_general | solution.py:124
  77.9 3.6 %collective-permute-start.8 = (bf16[1152,256]{1,0:T(8,128)(2,1)}, bf16[1152,256]{1,0:T(8,128)(2,1)S(1)}, u32[]{:S(2)}, u32[]{:S(2)}) collective-permute-start(bf16[1152,256]{1,0:T(8,128)(2,1)} %add_convert_fusion.2), channel_id=1, source_target_pairs={{0,2},{1,3},{2,0},{3,1},{4,6},{5,7},{6,4},{7,5},{8,10},{9,11},{10,... | collective-permute-start | bytes 1769480 | tf_op jit(solution)/shard_map/ppermute | solution.py:188
  81.5 1.5 %add_convert_fusion.3 = bf16[1152,256]{1,0:T(8,128)(2,1)} fusion(bf16[1152,256]{1,0:T(8,128)(2,1)S(1)} %collective-permute-done.5, bf16[1152,768]{1,0:T(8,128)(2,1)S(1)} %multiply_convert_fusion, bf16[1,768,3072]{2,1,0:T(8,128)(2,1)S(1)} %bitcast.78, s32[]{:T(128)S(6)} %select_n.77), kind=kOutput, calls=%fused_computation.16 | convolution fusion | flops 453869568 | bytes 3342340 | tf_op jit(solution)/shard_map/dot_general | solution.py:124
  83.4 1.5 %add_convert_fusion.4 = bf16[1152,256]{1,0:T(8,128)(2,1)} fusion(bf16[1152,256]{1,0:T(8,128)(2,1)S(1)} %collective-permute-done.3, bf16[1152,768]{1,0:T(8,128)(2,1)S(1)} %multiply_convert_fusion, bf16[1,768,3072]{2,1,0:T(8,128)(2,1)S(1)} %bitcast.78, s32[]{:T(128)S(6)} %select_n.74), kind=kOutput, calls=%fused_computation.17 | convolution fusion | flops 453869568 | bytes 3342340 | tf_op jit(solution)/shard_map/dot_general | solution.py:124
  85.9 2.1 %add_convert_fusion = bf16[1152,512]{1,0:T(8,128)(2,1)} fusion(bf16[1152,512]{1,0:T(8,128)(2,1)S(1)} %collective-permute-done.1, bf16[1152,768]{1,0:T(8,128)(2,1)S(1)} %multiply_convert_fusion, bf16[1,768,3072]{2,1,0:T(8,128)(2,1)S(1)} %bitcast.78, s32[]{:T(128)S(6)} %select_n.66), kind=kOutput, calls=%fused_computation.11 | convolution fusion | flops 907739136 | bytes 4915204 | tf_op jit(solution)/shard_map/dot_general | solution.py:124
  88.1 3.7 %all-to-all-start.1 = ((bf16[16,72,512]{2,1,0:T(8,128)(2,1)}), bf16[16,72,512]{2,1,0:T(8,128)(2,1)S(1)}, u32[]{:S(2)}, u32[]{:S(2)}) async-start(bf16[16,72,512]{2,1,0:T(8,128)(2,1)} %bitcast.12), calls=%async_computation.1 | async-start | bytes 2359296 | tf_op jit(solution)/shard_map/all_to_all | solution.py:193
  91.8 2.2 %add_convert_fusion.5 = bf16[1152,256]{1,0:T(8,128)(2,1)S(1)} fusion(bf16[1152,256]{1,0:T(8,128)(2,1)S(1)} %collective-permute-done.2, bf16[1152,768]{1,0:T(8,128)(2,1)} %copy-done.2, bf16[1,768,3072]{2,1,0:T(8,128)(2,1)} %param.12, s32[]{:T(128)S(6)} %select_n.71), kind=kOutput, calls=%fused_computation.18 | convolution fusion | flops 453869568 | bytes 3342340 | tf_op jit(solution)/shard_map/dot_general | solution.py:124
  94.0 1.4 collective-permute-done.8
  95.4 13.2 %collective-permute-done.6 = bf16[1152,256]{1,0:T(8,128)(2,1)S(1)} collective-permute-done((bf16[1152,256]{1,0:T(8,128)(2,1)}, bf16[1152,256]{1,0:T(8,128)(2,1)S(1)}, u32[]{:S(2)}, u32[]{:S(2)}) %collective-permute-start.6) | collective-permute-done | bytes 589856 | tf_op jit(solution)/shard_map/ppermute | solution.py:188
  109.7 4.4 %all-to-all-start.2 = ((bf16[16,72,256]{2,1,0:T(8,128)(2,1)}), bf16[16,72,256]{2,1,0:T(8,128)(2,1)S(1)}, u32[]{:S(2)}, u32[]{:S(2)}) async-start(bf16[16,72,256]{2,1,0:T(8,128)(2,1)} %bitcast.22), calls=%async_computation.2 | async-start | bytes 1179648 | tf_op jit(solution)/shard_map/all_to_all | solution.py:193
  114.7 1.9 %collective-permute-start.11 = (bf16[256,512]{1,0:T(8,128)(2,1)S(1)}, bf16[256,512]{1,0:T(8,128)(2,1)S(1)}, u32[]{:S(2)}, u32[]{:S(2)}) collective-permute-start(bf16[256,512]{1,0:T(8,128)(2,1)S(1)} %shard_map.74), channel_id=1, source_target_pairs={{0,2},{1,3},{2,0},{3,1},{4,6},{5,7},{6,4},{7,5},{8,10},{9,11},{10,... | collective-permute-start | bytes 786440 | tf_op jit(solution)/shard_map/ppermute | solution.py:188
  116.6 1.3 collective-permute-start.10
  119.0 6.1 %all-to-all-done.2 = bf16[16,72,256]{2,1,0:T(8,128)(2,1)S(1)} async-done(((bf16[16,72,256]{2,1,0:T(8,128)(2,1)}), bf16[16,72,256]{2,1,0:T(8,128)(2,1)S(1)}, u32[]{:S(2)}, u32[]{:S(2)}) %all-to-all-start.2) | async-done | bytes 589856 | tf_op jit(solution)/shard_map/all_to_all | solution.py:193
  125.5 2.2 %collective-permute-start.13 = (bf16[256,256]{1,0:T(8,128)(2,1)S(1)}, bf16[256,256]{1,0:T(8,128)(2,1)S(1)}, u32[]{:S(2)}, u32[]{:S(2)}) collective-permute-start(bf16[256,256]{1,0:T(8,128)(2,1)S(1)} %shard_map.75.refs_5_), channel_id=1, source_target_pairs={{0,2},{1,3},{2,0},{3,1},{4,6},{5,7},{6,4},{7,5},{8,10},{9,11},{10,... | collective-permute-start | bytes 393224 | tf_op jit(solution)/shard_map/ppermute | solution.py:188
  128.3 2.1 %collective-permute-start.15 = (bf16[256,256]{1,0:T(8,128)(2,1)S(1)}, bf16[256,256]{1,0:T(8,128)(2,1)S(1)}, u32[]{:S(2)}, u32[]{:S(2)}) collective-permute-start(bf16[256,256]{1,0:T(8,128)(2,1)S(1)} %shard_map.75.refs_5_), channel_id=1, source_target_pairs={{0,3},{1,0},{2,1},{3,2},{4,7},{5,4},{6,5},{7,6},{8,11},{9,8},{10,9... | collective-permute-start | bytes 393224 | tf_op jit(solution)/shard_map/ppermute | solution.py:188
  131.5 2.8 %collective-permute-start.12 = (bf16[256,512]{1,0:T(8,128)(2,1)S(1)}, bf16[256,512]{1,0:T(8,128)(2,1)S(1)}, u32[]{:S(2)}, u32[]{:S(2)}) collective-permute-start(bf16[256,512]{1,0:T(8,128)(2,1)S(1)} %add_convert_fusion.6.refs_0_), channel_id=1, source_target_pairs={{0,64},{64,0},{1,65},{65,1},{2,66},{66,2},{3,67},{67,3},{4,68},{68... | collective-permute-start | bytes 786440 | tf_op jit(solution)/shard_map/ppermute | solution.py:183
  134.8 1.4 collective-permute-start.17
  137.6 1.8 %shard_map.76 = bf16[256,3072]{1,0:T(8,128)(2,1)} custom-call(s32[10]{0:T(128)S(1)} %pad_add_fusion.at_ref, bf16[256,512]{1,0:T(8,128)(2,1)S(1)} %add_convert_fusion.6.refs_0_, bf16[256,512]{1,0:T(8,128)(2,1)S(1)} %collective-permute-done.12.refs_1_, bf16[256,256]{1,0:T(8,128)(2,1)S(1)} %collective-permute-done.13.refs_2_, ...), custom_call_target="tpu_custom_call" | custom-call | bytes 3000000 | tf_op jit(solution)/shard_map/pallas_call | solution.py:171
  (54 shorter events, 14.3 us)
Async XLA Ops:
  56.2 7.8 %collective-permute-start = (bf16[1152,1536]{1,0:T(8,128)(2,1)S(1)}, bf16[1152,1536]{1,0:T(8,128)(2,1)}, u32[]{:S(2)}, u32[]{:S(2)}) collective-permute-start(bf16[1152,1536]{1,0:T(8,128)(2,1)S(1)} %bitcast.72), channel_id=1, source_target_pairs={{0,64},{64,0},{1,65},{65,1},{2,66},{66,2},{3,67},{67,3},{4,68},{68... | collective-permute-start | bytes 10616840 | tf_op jit(solution)/shard_map/ppermute | solution.py:183
  70.0 15.9 %copy-start.2 = (bf16[1152,768]{1,0:T(8,128)(2,1)}, bf16[1152,768]{1,0:T(8,128)(2,1)S(1)}, u32[]{:S(2)}) copy-start(bf16[1152,768]{1,0:T(8,128)(2,1)S(1)} %multiply_convert_fusion) | copy-start | bytes 5308420
  71.1 14.8 %collective-permute-start.1 = (bf16[1152,512]{1,0:T(8,128)(2,1)S(1)}, bf16[1152,512]{1,0:T(8,128)(2,1)S(1)}, u32[]{:S(2)}, u32[]{:S(2)}) collective-permute-start(bf16[1152,512]{1,0:T(8,128)(2,1)S(1)} %convolution_convert_fusion), channel_id=1, source_target_pairs={{0,64},{64,0},{1,65},{65,1},{2,66},{66,2},{3,67},{67,3},{4,68},{68... | collective-permute-start | bytes 3538952 | tf_op jit(solution)/shard_map/ppermute | solution.py:183
  72.2 4.2 %collective-permute-start.7 = (bf16[1152,256]{1,0:T(8,128)(2,1)S(1)}, bf16[1152,256]{1,0:T(8,128)(2,1)S(1)}, u32[]{:S(2)}, u32[]{:S(2)}) collective-permute-start(bf16[1152,256]{1,0:T(8,128)(2,1)S(1)} %convolution_convert_fusion.1), channel_id=1, source_target_pairs={{0,64},{64,0},{1,65},{65,1},{2,66},{66,2},{3,67},{67,3},{4,68},{68... | collective-permute-start | bytes 1769480 | tf_op jit(solution)/shard_map/ppermute | solution.py:183
  73.0 8.5 %collective-permute-start.5 = (bf16[1152,256]{1,0:T(8,128)(2,1)S(1)}, bf16[1152,256]{1,0:T(8,128)(2,1)S(1)}, u32[]{:S(2)}, u32[]{:S(2)}) collective-permute-start(bf16[1152,256]{1,0:T(8,128)(2,1)S(1)} %convolution_convert_fusion.2), channel_id=1, source_target_pairs={{0,64},{64,0},{1,65},{65,1},{2,66},{66,2},{3,67},{67,3},{4,68},{68... | collective-permute-start | bytes 1769480 | tf_op jit(solution)/shard_map/ppermute | solution.py:183
  74.2 9.2 %collective-permute-start.3 = (bf16[1152,256]{1,0:T(8,128)(2,1)S(1)}, bf16[1152,256]{1,0:T(8,128)(2,1)S(1)}, u32[]{:S(2)}, u32[]{:S(2)}) collective-permute-start(bf16[1152,256]{1,0:T(8,128)(2,1)S(1)} %convolution_convert_fusion.3), channel_id=1, source_target_pairs={{0,64},{64,0},{1,65},{65,1},{2,66},{66,2},{3,67},{67,3},{4,68},{68... | collective-permute-start | bytes 1769480 | tf_op jit(solution)/shard_map/ppermute | solution.py:183
  76.0 15.8 %collective-permute-start.2 = (bf16[1152,256]{1,0:T(8,128)(2,1)}, bf16[1152,256]{1,0:T(8,128)(2,1)S(1)}, u32[]{:S(2)}, u32[]{:S(2)}) collective-permute-start(bf16[1152,256]{1,0:T(8,128)(2,1)} %convolution_convert_fusion.4), channel_id=1, source_target_pairs={{0,64},{64,0},{1,65},{65,1},{2,66},{66,2},{3,67},{67,3},{4,68},{68... | collective-permute-start | bytes 1769480 | tf_op jit(solution)/shard_map/ppermute | solution.py:183
  77.9 17.5 %collective-permute-start.8 = (bf16[1152,256]{1,0:T(8,128)(2,1)}, bf16[1152,256]{1,0:T(8,128)(2,1)S(1)}, u32[]{:S(2)}, u32[]{:S(2)}) collective-permute-start(bf16[1152,256]{1,0:T(8,128)(2,1)} %add_convert_fusion.2), channel_id=1, source_target_pairs={{0,2},{1,3},{2,0},{3,1},{4,6},{5,7},{6,4},{7,5},{8,10},{9,11},{10,... | collective-permute-start | bytes 1769480 | tf_op jit(solution)/shard_map/ppermute | solution.py:188
  83.0 25.6 %collective-permute-start.6 = (bf16[1152,256]{1,0:T(8,128)(2,1)}, bf16[1152,256]{1,0:T(8,128)(2,1)S(1)}, u32[]{:S(2)}, u32[]{:S(2)}) collective-permute-start(bf16[1152,256]{1,0:T(8,128)(2,1)} %add_convert_fusion.3), channel_id=1, source_target_pairs={{0,3},{1,0},{2,1},{3,2},{4,7},{5,4},{6,5},{7,6},{8,11},{9,8},{10,9... | collective-permute-start | bytes 1769480 | tf_op jit(solution)/shard_map/ppermute | solution.py:188
  84.9 23.7 %collective-permute-start.4 = (bf16[1152,256]{1,0:T(8,128)(2,1)}, bf16[1152,256]{1,0:T(8,128)(2,1)S(1)}, u32[]{:S(2)}, u32[]{:S(2)}) collective-permute-start(bf16[1152,256]{1,0:T(8,128)(2,1)} %add_convert_fusion.4), channel_id=1, source_target_pairs={{0,1},{1,2},{2,3},{3,0},{4,5},{5,6},{6,7},{7,4},{8,9},{9,10},{10,1... | collective-permute-start | bytes 1769480 | tf_op jit(solution)/shard_map/ppermute | solution.py:188
  88.1 21.7 %all-to-all-start.1 = ((bf16[16,72,512]{2,1,0:T(8,128)(2,1)}), bf16[16,72,512]{2,1,0:T(8,128)(2,1)S(1)}, u32[]{:S(2)}, u32[]{:S(2)}) async-start(bf16[16,72,512]{2,1,0:T(8,128)(2,1)} %bitcast.12), calls=%async_computation.1 | async-start | bytes 2359296 | tf_op jit(solution)/shard_map/all_to_all | solution.py:193
  93.9 20.2 %copy-start = (bf16[256,1152]{1,0:T(8,128)(2,1)S(1)}, bf16[256,1152]{1,0:T(8,128)(2,1)}, u32[]{:S(2)}) copy-start(bf16[256,1152]{1,0:T(8,128)(2,1)} %get-tuple-element.9.mix_ref) | copy-start | bytes 1769476
  109.7 15.4 %all-to-all-start.2 = ((bf16[16,72,256]{2,1,0:T(8,128)(2,1)}), bf16[16,72,256]{2,1,0:T(8,128)(2,1)S(1)}, u32[]{:S(2)}, u32[]{:S(2)}) async-start(bf16[16,72,256]{2,1,0:T(8,128)(2,1)} %bitcast.22), calls=%async_computation.2 | async-start | bytes 1179648 | tf_op jit(solution)/shard_map/all_to_all | solution.py:193
  114.7 13.6 %collective-permute-start.11 = (bf16[256,512]{1,0:T(8,128)(2,1)S(1)}, bf16[256,512]{1,0:T(8,128)(2,1)S(1)}, u32[]{:S(2)}, u32[]{:S(2)}) collective-permute-start(bf16[256,512]{1,0:T(8,128)(2,1)S(1)} %shard_map.74), channel_id=1, source_target_pairs={{0,2},{1,3},{2,0},{3,1},{4,6},{5,7},{6,4},{7,5},{8,10},{9,11},{10,... | collective-permute-start | bytes 786440 | tf_op jit(solution)/shard_map/ppermute | solution.py:188
  116.6 13.8 %collective-permute-start.10 = (bf16[256,512]{1,0:T(8,128)(2,1)S(1)}, bf16[256,512]{1,0:T(8,128)(2,1)S(1)}, u32[]{:S(2)}, u32[]{:S(2)}) collective-permute-start(bf16[256,512]{1,0:T(8,128)(2,1)S(1)} %shard_map.74), channel_id=1, source_target_pairs={{0,3},{1,0},{2,1},{3,2},{4,7},{5,4},{6,5},{7,6},{8,11},{9,8},{10,9... | collective-permute-start | bytes 786440 | tf_op jit(solution)/shard_map/ppermute | solution.py:188
  117.9 12.5 %collective-permute-start.9 = (bf16[256,512]{1,0:T(8,128)(2,1)S(1)}, bf16[256,512]{1,0:T(8,128)(2,1)S(1)}, u32[]{:S(2)}, u32[]{:S(2)}) collective-permute-start(bf16[256,512]{1,0:T(8,128)(2,1)S(1)} %shard_map.74), channel_id=1, source_target_pairs={{0,1},{1,2},{2,3},{3,0},{4,5},{5,6},{6,7},{7,4},{8,9},{9,10},{10,1... | collective-permute-start | bytes 786440 | tf_op jit(solution)/shard_map/ppermute | solution.py:188
  125.5 8.9 %collective-permute-start.13 = (bf16[256,256]{1,0:T(8,128)(2,1)S(1)}, bf16[256,256]{1,0:T(8,128)(2,1)S(1)}, u32[]{:S(2)}, u32[]{:S(2)}) collective-permute-start(bf16[256,256]{1,0:T(8,128)(2,1)S(1)} %shard_map.75.refs_5_), channel_id=1, source_target_pairs={{0,2},{1,3},{2,0},{3,1},{4,6},{5,7},{6,4},{7,5},{8,10},{9,11},{10,... | collective-permute-start | bytes 393224 | tf_op jit(solution)/shard_map/ppermute | solution.py:188
  127.7 7.1 %collective-permute-start.14 = (bf16[256,256]{1,0:T(8,128)(2,1)S(1)}, bf16[256,256]{1,0:T(8,128)(2,1)S(1)}, u32[]{:S(2)}, u32[]{:S(2)}) collective-permute-start(bf16[256,256]{1,0:T(8,128)(2,1)S(1)} %shard_map.75.refs_5_), channel_id=1, source_target_pairs={{0,1},{1,2},{2,3},{3,0},{4,5},{5,6},{6,7},{7,4},{8,9},{9,10},{10,1... | collective-permute-start | bytes 393224 | tf_op jit(solution)/shard_map/ppermute | solution.py:188
  128.3 8.0 %collective-permute-start.15 = (bf16[256,256]{1,0:T(8,128)(2,1)S(1)}, bf16[256,256]{1,0:T(8,128)(2,1)S(1)}, u32[]{:S(2)}, u32[]{:S(2)}) collective-permute-start(bf16[256,256]{1,0:T(8,128)(2,1)S(1)} %shard_map.75.refs_5_), channel_id=1, source_target_pairs={{0,3},{1,0},{2,1},{3,2},{4,7},{5,4},{6,5},{7,6},{8,11},{9,8},{10,9... | collective-permute-start | bytes 393224 | tf_op jit(solution)/shard_map/ppermute | solution.py:188
  131.5 4.8 %collective-permute-start.12 = (bf16[256,512]{1,0:T(8,128)(2,1)S(1)}, bf16[256,512]{1,0:T(8,128)(2,1)S(1)}, u32[]{:S(2)}, u32[]{:S(2)}) collective-permute-start(bf16[256,512]{1,0:T(8,128)(2,1)S(1)} %add_convert_fusion.6.refs_0_), channel_id=1, source_target_pairs={{0,64},{64,0},{1,65},{65,1},{2,66},{66,2},{3,67},{67,3},{4,68},{68... | collective-permute-start | bytes 786440 | tf_op jit(solution)/shard_map/ppermute | solution.py:183
  134.3 2.0 %collective-permute-start.19 = (bf16[256,256]{1,0:T(8,128)(2,1)S(1)}, bf16[256,256]{1,0:T(8,128)(2,1)S(1)}, u32[]{:S(2)}, u32[]{:S(2)}) collective-permute-start(bf16[256,256]{1,0:T(8,128)(2,1)S(1)} %shard_map.75.refs_5_), channel_id=1, source_target_pairs={{0,64},{64,0},{1,65},{65,1},{2,66},{66,2},{3,67},{67,3},{4,68},{68... | collective-permute-start | bytes 393224 | tf_op jit(solution)/shard_map/ppermute | solution.py:183
  134.4 1.9 %collective-permute-start.16 = (bf16[256,256]{1,0:T(8,128)(2,1)S(1)}, bf16[256,256]{1,0:T(8,128)(2,1)S(1)}, u32[]{:S(2)}, u32[]{:S(2)}) collective-permute-start(bf16[256,256]{1,0:T(8,128)(2,1)S(1)} %collective-permute-done.13.refs_2_), channel_id=1, source_target_pairs={{0,64},{64,0},{1,65},{65,1},{2,66},{66,2},{3,67},{67,3},{4,68},{68... | collective-permute-start | bytes 393224 | tf_op jit(solution)/shard_map/ppermute | solution.py:183
  134.8 2.4 %collective-permute-start.17 = (bf16[256,256]{1,0:T(8,128)(2,1)S(1)}, bf16[256,256]{1,0:T(8,128)(2,1)S(1)}, u32[]{:S(2)}, u32[]{:S(2)}) collective-permute-start(bf16[256,256]{1,0:T(8,128)(2,1)S(1)} %collective-permute-done.14.refs_3_), channel_id=1, source_target_pairs={{0,64},{64,0},{1,65},{65,1},{2,66},{66,2},{3,67},{67,3},{4,68},{68... | collective-permute-start | bytes 393224 | tf_op jit(solution)/shard_map/ppermute | solution.py:183
  136.2 1.3 collective-permute-start.18
  (3 other events, 28.4 us)

commit v7 on v6

--- a/solution.py
+++ b/solution.py
@@ -21,8 +21,8 @@
 BF16 = jnp.bfloat16
 ROUTE_VMEM = 60 * 1024 * 1024
 MATMUL_VMEM = 6 * 1024 * 1024
-ROUTE_BLOCK = 64
-PICK = 4
+ROUTE_BLOCK = 128
+PICK = 2
 NORM_ROWS = 16
 NT = (((1,), (1,)), ((), ()))
 
@@ -32,7 +32,7 @@
     return jnp.concatenate([(slot == keys[e : e + 1, :]).astype(F32) for e in range(keys.shape[0])], axis=0).astype(BF16)
 
 
-def route_kernel(tok_hbm, gain_hbm, router_hbm, ids_hbm, rows_hbm, mix_hbm, tok_ref, gain_ref, router_ref, ids_ref, normed_ref, rows_ref, mix_ref, sems, out_sems):
+def route_kernel(tok_hbm, gain_hbm, router_hbm, ids_hbm, rows_hbm, key_hbm, gate_hbm, tok_ref, gain_ref, router_ref, ids_ref, normed_ref, rows_ref, key_ref, gate_ref, sems, out_sems):
     small = [
         pltpu.make_async_copy(ids_hbm, ids_ref, sems.at[0]),
         pltpu.make_async_copy(gain_hbm, gain_ref, sems.at[1]),
@@ -90,34 +90,49 @@
     logits += lax.dot_general(normed_ref[1], router_ref[:, HALF:], NT, preferred_element_type=F32)
     weight = jnp.where(chosen, jnp.exp(logits), 0.0)
     gate = weight / jnp.sum(weight, axis=1, keepdims=True)
+    key_ref[...] = key
+    gate_ref[...] = gate
+    for i, (here, there) in enumerate(((key_ref, key_hbm), (gate_ref, gate_hbm))):
+        stores.append(pltpu.make_async_copy(here, there, out_sems.at[EXPERTS // PICK + i]))
+        stores[-1].start()
+    for copy in stores:
+        copy.wait()
+
+
+def route(tokens, norm_gain, router_weight, expert_ids):
+    shapes = [((ROWS, HALF), BF16), ((TOK_DEV, EXPERTS), F32), ((TOK_DEV, EXPERTS), F32)]
+    held = [((TOK_DEV, D), BF16), ((1, D), F32), ((EXPERTS, D), BF16), ((TOP, TOK_DEV), jnp.int32), ((2, TOK_DEV, HALF), BF16)]
+    anywhere = pl.BlockSpec(memory_space=pl.ANY)
+    return pl.pallas_call(
+        route_kernel,
+        in_specs=[anywhere] * 4,
+        out_specs=[anywhere] * 3,
+        out_shape=[jax.ShapeDtypeStruct(shape, kind) for shape, kind in shapes],
+        scratch_shapes=[pltpu.VMEM(shape, kind) for shape, kind in held + shapes]
+        + [pltpu.SemaphoreType.DMA((3 + TOK_DEV // ROUTE_BLOCK,)), pltpu.SemaphoreType.DMA((EXPERTS // PICK + 2,))],
+        compiler_params=pltpu.CompilerParams(vmem_limit_bytes=ROUTE_VMEM),
+        cost_estimate=pl.CostEstimate(flops=2 * ROWS * TOK_DEV * HALF, bytes_accessed=6_000_000, transcendentals=0),
+    )(tokens, norm_gain.reshape(1, D), router_weight.T, expert_ids.T)
+
+
+def mix_matrix_kernel(key_ref, gate_ref, mix_ref):
     slot = lax.broadcasted_iota(jnp.int32, (EXPERTS, ROWS), 1)
     first = lax.broadcasted_iota(jnp.int32, (EXPERTS, ROWS), 0) * CAP
     inside = (slot >= first) & (slot < first + CAP)
     spread_out = inside.astype(F32).astype(BF16)
     slot_in = jnp.sum(jnp.where(inside, slot - first, 0).astype(F32), axis=0, keepdims=True)
-    key_wide = jnp.dot(key.astype(BF16), spread_out, preferred_element_type=F32)
-    gate_wide = jnp.dot(gate.astype(BF16), spread_out, preferred_element_type=F32)
+    key_wide = jnp.dot(key_ref[...].astype(BF16), spread_out, preferred_element_type=F32)
+    gate_wide = jnp.dot(gate_ref[...].astype(BF16), spread_out, preferred_element_type=F32)
     mix_ref[...] = jnp.where(key_wide == slot_in, gate_wide, 0.0).astype(BF16)
-    stores.append(pltpu.make_async_copy(mix_ref, mix_hbm, out_sems.at[EXPERTS // PICK]))
-    stores[-1].start()
-    for copy in stores:
-        copy.wait()
-
-
-def route(tokens, norm_gain, router_weight, expert_ids):
-    shapes = [((ROWS, HALF), BF16), ((TOK_DEV, ROWS), BF16)]
-    held = [((TOK_DEV, D), BF16), ((1, D), F32), ((EXPERTS, D), BF16), ((TOP, TOK_DEV), jnp.int32), ((2, TOK_DEV, HALF), BF16)]
-    anywhere = pl.BlockSpec(memory_space=pl.ANY)
-    return pl.pallas_call(
-        route_kernel,
-        in_specs=[anywhere] * 4,
-        out_specs=[anywhere] * 2,
-        out_shape=[jax.ShapeDtypeStruct(shape, kind) for shape, kind in shapes],
-        scratch_shapes=[pltpu.VMEM(shape, kind) for shape, kind in held + shapes]
-        + [pltpu.SemaphoreType.DMA((3 + TOK_DEV // ROUTE_BLOCK,)), pltpu.SemaphoreType.DMA((EXPERTS // PICK + 1,))],
-        compiler_params=pltpu.CompilerParams(vmem_limit_bytes=ROUTE_VMEM),
-        cost_estimate=pl.CostEstimate(flops=2 * ROWS * TOK_DEV * HALF, bytes_accessed=6_000_000, transcendentals=0),
-    )(tokens, norm_gain.reshape(1, D), router_weight.T, expert_ids.T)
+
+
+def mix_matrix_of(key, gate):
+    return pl.pallas_call(
+        mix_matrix_kernel,
+        out_shape=jax.ShapeDtypeStruct((TOK_DEV, ROWS), BF16),
+        compiler_params=pltpu.CompilerParams(vmem_limit_bytes=MATMUL_VMEM),
+        cost_estimate=pl.CostEstimate(flops=4 * ROWS * TOK_DEV * EXPERTS, bytes_accessed=1_000_000, transcendentals=0),
+    )(key, gate)
 
 
 def product(rows, weight):
@@ -208,7 +223,7 @@
     up = up_weight.reshape(2, HALF, up_weight.shape[2])
     down = down_weight[0]
 
-    outgoing, mix_matrix = route(tokens, norm_gain, router_weight, expert_ids)
+    outgoing, key, gate = route(tokens, norm_gain, router_weight, expert_ids)
     token_wide = lax.dynamic_slice(tokens, (0, core * HALF), (TOK_DEV, WIDE))
     token_thin = lax.dynamic_slice(tokens, (0, core * HALF + WIDE + z * THIN), (TOK_DEV, THIN))
     mine = to_experts(outgoing)
@@ -229,12 +244,13 @@
     thin_sum = lax.optimization_barrier(kept).astype(F32)
     for piece in arrived:
         thin_sum = thin_sum + piece.astype(F32)
+    mix_matrix = mix_matrix_of(*lax.optimization_barrier((wide, key, gate))[1:])
     wide_rows, thin_sum = lax.optimization_barrier((to_experts(wide), thin_sum.astype(BF16)))
     wide_part = mix(mix_matrix, wide_rows)
     thin_own = mix_add(token_thin, mix_matrix, to_experts(thin_sum))
 
     wide_own = token_wide.astype(F32) + wide_part.astype(F32)
-    for step in Z_STEPS[:-1]:
+    for step in (3, 1, 2):
         wide_own = wide_own + along_z(wide_part, step).astype(F32)
     wide_own = wide_own.astype(BF16)
     thin_all = [along_z(thin_own, step) for step in TAIL_STEPS[:-1]] + [thin_own]

time: 140 us -> 140 us (level)
    all_to_all x2, waiting for transfers between devices: 6.14 us -> 4.59 us  [to_experts(): lax.all_to_all(rows.reshape(EXPERTS, CAP, width), 'ep', split_axis=0, con...]
  transfers between devices with their start and end apart: 22 -> 22, of which waited for: 6 -> 7; matrix products, arithmetic and copies ran while one was open for 14% -> 15% of each run, Pallas kernels for 1% -> 1%
where the time goes in v7:
time: 140 us; the launch traced here: 139 us
  blocking collectives  50.6 us (36%)
  starting transfers between devices  30.6 us (22%)
  matrix products  24 us (17%)
  waiting for transfers between devices  22.4 us (16%)
  Pallas kernels  7.82 us (6%)
  other arithmetic  2.35 us (2%)
    all_to_all x1, blocking collectives, to_experts(): lax.all_to_all(rows.reshape(EXPERTS, CAP, width), 'ep', split_axis=0, con...  50.6 us
    dot_general x12, matrix products, product(): return jnp.dot(rows, weight, preferred_element_type=F32)  24 us
    ppermute x9, waiting for transfers between devices, along_z(): lax.ppermute(values, 'dp', [(i, (i + step) % count) for i in range(count)])  15.4 us
    ppermute x9, starting transfers between devices, along_z(): lax.ppermute(values, 'dp', [(i, (i + step) % count) for i in range(count)])  14.3 us
    all_to_all x2, starting transfers between devices, to_experts(): lax.all_to_all(rows.reshape(EXPERTS, CAP, width), 'ep', split_axis=0, con...  8.25 us
    ppermute x11, starting transfers between devices, swap(): return lax.ppermute(values, 'pp', [(0, 1), (1, 0)])  7.99 us
    pallas_call x1, Pallas kernels, route(): pl.pallas_call(route_kernel, in_specs=[anywhere] * 4, out_specs=[anywhere...  4.78 us
    all_to_all x2, waiting for transfers between devices, to_experts(): lax.all_to_all(rows.reshape(EXPERTS, CAP, width), 'ep', split_axis=0, con...  4.59 us
  transfers between devices with their start and end apart: 22, of which 7 were waited for; matrix products, arithmetic and copies ran while one was open for 15% of the time, Pallas kernels for 1%

profile of v7, /device:TPU:1, one launch (start us, length us, event | category | flops | bytes accessed | tf_op | source)
XLA Modules:
  0.0 139.1 jit_solution(9589571366221718392)
XLA Ops:
  0.0 4.8 %shard_map.73 = (bf16[1152,1536]{1,0:T(8,128)(2,1)}, f32[256,16]{1,0:T(8,128)}, f32[256,16]{1,0:T(8,128)}) custom-call(bf16[256,3072]{1,0:T(8,128)(2,1)} %tok_hbm.1, f32[1,3072]{1,0:T(1,128)} %bitcast.80, bf16[16,3072]{1,0:T(8,128)(2,1)} %bitcast.79, s32[4,256]{1,0:T(4,128)} %bitcast.81), custom_call_target="tpu_custom_call" | custom-call | flops 905969664 | bytes 6000000 | tf_op jit(solution)/shard_map/pallas_call | solution.py:106
  4.8 50.6 %all_to_all.15 = bf16[16,72,1536]{2,1,0:T(8,128)(2,1)S(1)} all-to-all(bf16[16,72,1536]{2,1,0:T(8,128)(2,1)} %bitcast.74), channel_id=1, replica_groups=mesh['pp'=2,'ep'=16,'dp'=4] {'ep'}, dimensions={0} | all-to-all | bytes 7077888 | tf_op jit(solution)/shard_map/all_to_all | solution.py:208
  55.3 1.8 %collective-permute-start = (bf16[1152,1536]{1,0:T(8,128)(2,1)S(1)}, bf16[1152,1536]{1,0:T(8,128)(2,1)}, u32[]{:S(2)}, u32[]{:S(2)}) collective-permute-start(bf16[1152,1536]{1,0:T(8,128)(2,1)S(1)} %bitcast.72), channel_id=1, source_target_pairs={{0,64},{64,0},{1,65},{65,1},{2,66},{66,2},{3,67},{67,3},{4,68},{68... | collective-permute-start | bytes 10616840 | tf_op jit(solution)/shard_map/ppermute | solution.py:198
  57.2 4.7 %fusion.2 = f32[1152,768]{1,0:T(8,128)S(1)} fusion(bf16[1152,1536]{1,0:T(8,128)(2,1)S(1)} %bitcast.73, bf16[2,1536,768]{2,1,0:T(8,128)(2,1)} %bitcast.75, s32[]{:T(128)S(6)} %select_n.67), kind=kOutput, calls=%fused_computation.9 | convolution fusion | flops 2717908992 | bytes 9437188 | tf_op jit(solution)/shard_map/dot_general | solution.py:139
  61.9 1.2 collective-permute-done
  63.2 5.9 %multiply_convert_fusion = bf16[1152,768]{1,0:T(8,128)(2,1)S(1)} fusion(f32[1152,768]{1,0:T(8,128)S(1)} %fusion.2, bf16[1152,1536]{1,0:T(8,128)(2,1)} %collective-permute-done, bf16[2,1536,768]{2,1,0:T(8,128)(2,1)} %bitcast.76, s32[]{:T(128)S(6)} %select_n.68), kind=kOutput, calls=%fused_computation.2 | convolution fusion | flops 2722332672 | bytes 11206660 | tf_op jit(solution)/shard_map/dot_general | solution.py:139
  73.7 1.5 %convolution_convert_fusion.4 = bf16[1152,256]{1,0:T(8,128)(2,1)} fusion(bf16[1152,768]{1,0:T(8,128)(2,1)S(1)} %multiply_convert_fusion, bf16[1,768,3072]{2,1,0:T(8,128)(2,1)S(1)} %bitcast.78, s32[]{:T(128)S(6)} %select_n.72), kind=kOutput, calls=%fused_computation.7 | convolution fusion | flops 453279744 | bytes 2752516 | tf_op jit(solution)/shard_map/dot_general | solution.py:139
  75.5 1.5 %add_convert_fusion.2 = bf16[1152,256]{1,0:T(8,128)(2,1)} fusion(bf16[1152,256]{1,0:T(8,128)(2,1)S(1)} %collective-permute-done.7, bf16[1152,768]{1,0:T(8,128)(2,1)S(1)} %multiply_convert_fusion, bf16[1,768,3072]{2,1,0:T(8,128)(2,1)S(1)} %bitcast.78, s32[]{:T(128)S(6)} %select_n.80), kind=kOutput, calls=%fused_computation.15 | convolution fusion | flops 453869568 | bytes 3342340 | tf_op jit(solution)/shard_map/dot_general | solution.py:139
  77.0 3.6 %collective-permute-start.8 = (bf16[1152,256]{1,0:T(8,128)(2,1)}, bf16[1152,256]{1,0:T(8,128)(2,1)S(1)}, u32[]{:S(2)}, u32[]{:S(2)}) collective-permute-start(bf16[1152,256]{1,0:T(8,128)(2,1)} %add_convert_fusion.2), channel_id=1, source_target_pairs={{0,2},{1,3},{2,0},{3,1},{4,6},{5,7},{6,4},{7,5},{8,10},{9,11},{10,... | collective-permute-start | bytes 1769480 | tf_op jit(solution)/shard_map/ppermute | solution.py:203
  80.6 1.5 %add_convert_fusion.3 = bf16[1152,256]{1,0:T(8,128)(2,1)} fusion(bf16[1152,256]{1,0:T(8,128)(2,1)S(1)} %collective-permute-done.5, bf16[1152,768]{1,0:T(8,128)(2,1)S(1)} %multiply_convert_fusion, bf16[1,768,3072]{2,1,0:T(8,128)(2,1)S(1)} %bitcast.78, s32[]{:T(128)S(6)} %select_n.77), kind=kOutput, calls=%fused_computation.16 | convolution fusion | flops 453869568 | bytes 3342340 | tf_op jit(solution)/shard_map/dot_general | solution.py:139
  82.5 1.5 %add_convert_fusion.4 = bf16[1152,256]{1,0:T(8,128)(2,1)} fusion(bf16[1152,256]{1,0:T(8,128)(2,1)S(1)} %collective-permute-done.3, bf16[1152,768]{1,0:T(8,128)(2,1)S(1)} %multiply_convert_fusion, bf16[1,768,3072]{2,1,0:T(8,128)(2,1)S(1)} %bitcast.78, s32[]{:T(128)S(6)} %select_n.74), kind=kOutput, calls=%fused_computation.17 | convolution fusion | flops 453869568 | bytes 3342340 | tf_op jit(solution)/shard_map/dot_general | solution.py:139
  85.0 2.1 %add_convert_fusion = bf16[1152,512]{1,0:T(8,128)(2,1)} fusion(bf16[1152,512]{1,0:T(8,128)(2,1)S(1)} %collective-permute-done.1, bf16[1152,768]{1,0:T(8,128)(2,1)S(1)} %multiply_convert_fusion, bf16[1,768,3072]{2,1,0:T(8,128)(2,1)S(1)} %bitcast.78, s32[]{:T(128)S(6)} %select_n.66), kind=kOutput, calls=%fused_computation.11 | convolution fusion | flops 907739136 | bytes 4915204 | tf_op jit(solution)/shard_map/dot_general | solution.py:139
  87.2 3.7 %all-to-all-start.1 = ((bf16[16,72,512]{2,1,0:T(8,128)(2,1)}), bf16[16,72,512]{2,1,0:T(8,128)(2,1)S(1)}, u32[]{:S(2)}, u32[]{:S(2)}) async-start(bf16[16,72,512]{2,1,0:T(8,128)(2,1)} %bitcast.12), calls=%async_computation.1 | async-start | bytes 2359296 | tf_op jit(solution)/shard_map/all_to_all | solution.py:208
  90.9 2.4 %add_convert_fusion.5 = bf16[1152,256]{1,0:T(8,128)(2,1)S(1)} fusion(bf16[1152,256]{1,0:T(8,128)(2,1)} %collective-permute-done.2, bf16[1152,768]{1,0:T(8,128)(2,1)} %copy-done.3, bf16[1,768,3072]{2,1,0:T(8,128)(2,1)} %param.12, s32[]{:T(128)S(6)} %select_n.71), kind=kOutput, calls=%fused_computation.18 | convolution fusion | flops 453869568 | bytes 3342340 | tf_op jit(solution)/shard_map/dot_general | solution.py:139
  94.5 13.1 %collective-permute-done.6 = bf16[1152,256]{1,0:T(8,128)(2,1)S(1)} collective-permute-done((bf16[1152,256]{1,0:T(8,128)(2,1)}, bf16[1152,256]{1,0:T(8,128)(2,1)S(1)}, u32[]{:S(2)}, u32[]{:S(2)}) %collective-permute-start.6) | collective-permute-done | bytes 589856 | tf_op jit(solution)/shard_map/ppermute | solution.py:203
  108.7 4.6 %all-to-all-start.2 = ((bf16[16,72,256]{2,1,0:T(8,128)(2,1)}), bf16[16,72,256]{2,1,0:T(8,128)(2,1)S(1)}, u32[]{:S(2)}, u32[]{:S(2)}) async-start(bf16[16,72,256]{2,1,0:T(8,128)(2,1)} %bitcast.22), calls=%async_computation.2 | async-start | bytes 1179648 | tf_op jit(solution)/shard_map/all_to_all | solution.py:208
  114.3 1.8 %collective-permute-start.11 = (bf16[256,512]{1,0:T(8,128)(2,1)S(1)}, bf16[256,512]{1,0:T(8,128)(2,1)S(1)}, u32[]{:S(2)}, u32[]{:S(2)}) collective-permute-start(bf16[256,512]{1,0:T(8,128)(2,1)S(1)} %shard_map.75), channel_id=1, source_target_pairs={{0,2},{1,3},{2,0},{3,1},{4,6},{5,7},{6,4},{7,5},{8,10},{9,11},{10,... | collective-permute-start | bytes 786440 | tf_op jit(solution)/shard_map/ppermute | solution.py:203
  116.8 2.0 %collective-permute-start.9 = (bf16[256,512]{1,0:T(8,128)(2,1)S(1)}, bf16[256,512]{1,0:T(8,128)(2,1)S(1)}, u32[]{:S(2)}, u32[]{:S(2)}) collective-permute-start(bf16[256,512]{1,0:T(8,128)(2,1)S(1)} %shard_map.75), channel_id=1, source_target_pairs={{0,3},{1,0},{2,1},{3,2},{4,7},{5,4},{6,5},{7,6},{8,11},{9,8},{10,9... | collective-permute-start | bytes 786440 | tf_op jit(solution)/shard_map/ppermute | solution.py:203
  119.7 4.6 %all-to-all-done.2 = bf16[16,72,256]{2,1,0:T(8,128)(2,1)S(1)} async-done(((bf16[16,72,256]{2,1,0:T(8,128)(2,1)}), bf16[16,72,256]{2,1,0:T(8,128)(2,1)S(1)}, u32[]{:S(2)}, u32[]{:S(2)}) %all-to-all-start.2) | async-done | bytes 589856 | tf_op jit(solution)/shard_map/all_to_all | solution.py:208
  124.6 2.1 %collective-permute-start.13 = (bf16[256,256]{1,0:T(8,128)(2,1)S(1)}, bf16[256,256]{1,0:T(8,128)(2,1)S(1)}, u32[]{:S(2)}, u32[]{:S(2)}) collective-permute-start(bf16[256,256]{1,0:T(8,128)(2,1)S(1)} %shard_map.76.refs_5_), channel_id=1, source_target_pairs={{0,2},{1,3},{2,0},{3,1},{4,6},{5,7},{6,4},{7,5},{8,10},{9,11},{10,... | collective-permute-start | bytes 393224 | tf_op jit(solution)/shard_map/ppermute | solution.py:203
  127.0 2.3 %collective-permute-start.15 = (bf16[256,256]{1,0:T(8,128)(2,1)S(1)}, bf16[256,256]{1,0:T(8,128)(2,1)S(1)}, u32[]{:S(2)}, u32[]{:S(2)}) collective-permute-start(bf16[256,256]{1,0:T(8,128)(2,1)S(1)} %shard_map.76.refs_5_), channel_id=1, source_target_pairs={{0,3},{1,0},{2,1},{3,2},{4,7},{5,4},{6,5},{7,6},{8,11},{9,8},{10,9... | collective-permute-start | bytes 393224 | tf_op jit(solution)/shard_map/ppermute | solution.py:203
  131.5 1.7 %collective-permute-start.12 = (bf16[256,512]{1,0:T(8,128)(2,1)S(1)}, bf16[256,512]{1,0:T(8,128)(2,1)S(1)}, u32[]{:S(2)}, u32[]{:S(2)}) collective-permute-start(bf16[256,512]{1,0:T(8,128)(2,1)S(1)} %add_convert_fusion.6.refs_0_), channel_id=1, source_target_pairs={{0,64},{64,0},{1,65},{65,1},{2,66},{66,2},{3,67},{67,3},{4,68},{68... | collective-permute-start | bytes 786440 | tf_op jit(solution)/shard_map/ppermute | solution.py:198
  134.5 1.3 collective-permute-start.17
  137.2 1.8 %shard_map.77 = bf16[256,3072]{1,0:T(8,128)(2,1)} custom-call(s32[10]{0:T(128)S(1)} %pad_add_fusion.at_ref, bf16[256,512]{1,0:T(8,128)(2,1)S(1)} %add_convert_fusion.6.refs_0_, bf16[256,512]{1,0:T(8,128)(2,1)S(1)} %collective-permute-done.12.refs_1_, bf16[256,256]{1,0:T(8,128)(2,1)S(1)} %collective-permute-done.13.refs_2_, ...), custom_call_target="tpu_custom_call" | custom-call | bytes 3000000 | tf_op jit(solution)/shard_map/pallas_call | solution.py:186
  (57 shorter events, 16.7 us)
Async XLA Ops:
  55.3 7.8 %collective-permute-start = (bf16[1152,1536]{1,0:T(8,128)(2,1)S(1)}, bf16[1152,1536]{1,0:T(8,128)(2,1)}, u32[]{:S(2)}, u32[]{:S(2)}) collective-permute-start(bf16[1152,1536]{1,0:T(8,128)(2,1)S(1)} %bitcast.72), channel_id=1, source_target_pairs={{0,64},{64,0},{1,65},{65,1},{2,66},{66,2},{3,67},{67,3},{4,68},{68... | collective-permute-start | bytes 10616840 | tf_op jit(solution)/shard_map/ppermute | solution.py:198
  70.2 14.8 %collective-permute-start.1 = (bf16[1152,512]{1,0:T(8,128)(2,1)S(1)}, bf16[1152,512]{1,0:T(8,128)(2,1)S(1)}, u32[]{:S(2)}, u32[]{:S(2)}) collective-permute-start(bf16[1152,512]{1,0:T(8,128)(2,1)S(1)} %convolution_convert_fusion), channel_id=1, source_target_pairs={{0,64},{64,0},{1,65},{65,1},{2,66},{66,2},{3,67},{67,3},{4,68},{68... | collective-permute-start | bytes 3538952 | tf_op jit(solution)/shard_map/ppermute | solution.py:198
  71.3 4.2 %collective-permute-start.7 = (bf16[1152,256]{1,0:T(8,128)(2,1)S(1)}, bf16[1152,256]{1,0:T(8,128)(2,1)S(1)}, u32[]{:S(2)}, u32[]{:S(2)}) collective-permute-start(bf16[1152,256]{1,0:T(8,128)(2,1)S(1)} %convolution_convert_fusion.1), channel_id=1, source_target_pairs={{0,64},{64,0},{1,65},{65,1},{2,66},{66,2},{3,67},{67,3},{4,68},{68... | collective-permute-start | bytes 1769480 | tf_op jit(solution)/shard_map/ppermute | solution.py:198
  72.2 8.5 %collective-permute-start.5 = (bf16[1152,256]{1,0:T(8,128)(2,1)S(1)}, bf16[1152,256]{1,0:T(8,128)(2,1)S(1)}, u32[]{:S(2)}, u32[]{:S(2)}) collective-permute-start(bf16[1152,256]{1,0:T(8,128)(2,1)S(1)} %convolution_convert_fusion.2), channel_id=1, source_target_pairs={{0,64},{64,0},{1,65},{65,1},{2,66},{66,2},{3,67},{67,3},{4,68},{68... | collective-permute-start | bytes 1769480 | tf_op jit(solution)/shard_map/ppermute | solution.py:198
  73.3 9.2 %collective-permute-start.3 = (bf16[1152,256]{1,0:T(8,128)(2,1)S(1)}, bf16[1152,256]{1,0:T(8,128)(2,1)S(1)}, u32[]{:S(2)}, u32[]{:S(2)}) collective-permute-start(bf16[1152,256]{1,0:T(8,128)(2,1)S(1)} %convolution_convert_fusion.3), channel_id=1, source_target_pairs={{0,64},{64,0},{1,65},{65,1},{2,66},{66,2},{3,67},{67,3},{4,68},{68... | collective-permute-start | bytes 1769480 | tf_op jit(solution)/shard_map/ppermute | solution.py:198
  75.1 15.7 %collective-permute-start.2 = (bf16[1152,256]{1,0:T(8,128)(2,1)}, bf16[1152,256]{1,0:T(8,128)(2,1)}, u32[]{:S(2)}, u32[]{:S(2)}) collective-permute-start(bf16[1152,256]{1,0:T(8,128)(2,1)} %convolution_convert_fusion.4), channel_id=1, source_target_pairs={{0,64},{64,0},{1,65},{65,1},{2,66},{66,2},{3,67},{67,3},{4,68},{68... | collective-permute-start | bytes 1769480 | tf_op jit(solution)/shard_map/ppermute | solution.py:198
  77.0 17.5 %collective-permute-start.8 = (bf16[1152,256]{1,0:T(8,128)(2,1)}, bf16[1152,256]{1,0:T(8,128)(2,1)S(1)}, u32[]{:S(2)}, u32[]{:S(2)}) collective-permute-start(bf16[1152,256]{1,0:T(8,128)(2,1)} %add_convert_fusion.2), channel_id=1, source_target_pairs={{0,2},{1,3},{2,0},{3,1},{4,6},{5,7},{6,4},{7,5},{8,10},{9,11},{10,... | collective-permute-start | bytes 1769480 | tf_op jit(solution)/shard_map/ppermute | solution.py:203
  82.1 25.4 %collective-permute-start.6 = (bf16[1152,256]{1,0:T(8,128)(2,1)}, bf16[1152,256]{1,0:T(8,128)(2,1)S(1)}, u32[]{:S(2)}, u32[]{:S(2)}) collective-permute-start(bf16[1152,256]{1,0:T(8,128)(2,1)} %add_convert_fusion.3), channel_id=1, source_target_pairs={{0,3},{1,0},{2,1},{3,2},{4,7},{5,4},{6,5},{7,6},{8,11},{9,8},{10,9... | collective-permute-start | bytes 1769480 | tf_op jit(solution)/shard_map/ppermute | solution.py:203
  83.9 23.6 %collective-permute-start.4 = (bf16[1152,256]{1,0:T(8,128)(2,1)}, bf16[1152,256]{1,0:T(8,128)(2,1)S(1)}, u32[]{:S(2)}, u32[]{:S(2)}) collective-permute-start(bf16[1152,256]{1,0:T(8,128)(2,1)} %add_convert_fusion.4), channel_id=1, source_target_pairs={{0,1},{1,2},{2,3},{3,0},{4,5},{5,6},{6,7},{7,4},{8,9},{9,10},{10,1... | collective-permute-start | bytes 1769480 | tf_op jit(solution)/shard_map/ppermute | solution.py:203
  87.2 21.5 %all-to-all-start.1 = ((bf16[16,72,512]{2,1,0:T(8,128)(2,1)}), bf16[16,72,512]{2,1,0:T(8,128)(2,1)S(1)}, u32[]{:S(2)}, u32[]{:S(2)}) async-start(bf16[16,72,512]{2,1,0:T(8,128)(2,1)} %bitcast.12), calls=%async_computation.1 | async-start | bytes 2359296 | tf_op jit(solution)/shard_map/all_to_all | solution.py:208
  93.2 20.0 %copy-start = (f32[256,16]{1,0:T(8,128)S(1)}, f32[256,16]{1,0:T(8,128)}, u32[]{:S(2)}) copy-start(f32[256,16]{1,0:T(8,128)} %get-tuple-element.15.key_ref) | copy-start | bytes 49156
  93.3 20.0 %copy-start.1 = (f32[256,16]{1,0:T(8,128)S(1)}, f32[256,16]{1,0:T(8,128)}, u32[]{:S(2)}) copy-start(f32[256,16]{1,0:T(8,128)} %get-tuple-element.16.gate_ref) | copy-start | bytes 49156
  108.7 15.6 %all-to-all-start.2 = ((bf16[16,72,256]{2,1,0:T(8,128)(2,1)}), bf16[16,72,256]{2,1,0:T(8,128)(2,1)S(1)}, u32[]{:S(2)}, u32[]{:S(2)}) async-start(bf16[16,72,256]{2,1,0:T(8,128)(2,1)} %bitcast.22), calls=%async_computation.2 | async-start | bytes 1179648 | tf_op jit(solution)/shard_map/all_to_all | solution.py:208
  114.3 12.7 %collective-permute-start.11 = (bf16[256,512]{1,0:T(8,128)(2,1)S(1)}, bf16[256,512]{1,0:T(8,128)(2,1)S(1)}, u32[]{:S(2)}, u32[]{:S(2)}) collective-permute-start(bf16[256,512]{1,0:T(8,128)(2,1)S(1)} %shard_map.75), channel_id=1, source_target_pairs={{0,2},{1,3},{2,0},{3,1},{4,6},{5,7},{6,4},{7,5},{8,10},{9,11},{10,... | collective-permute-start | bytes 786440 | tf_op jit(solution)/shard_map/ppermute | solution.py:203
  116.1 14.3 %collective-permute-start.10 = (bf16[256,512]{1,0:T(8,128)(2,1)S(1)}, bf16[256,512]{1,0:T(8,128)(2,1)S(1)}, u32[]{:S(2)}, u32[]{:S(2)}) collective-permute-start(bf16[256,512]{1,0:T(8,128)(2,1)S(1)} %shard_map.75), channel_id=1, source_target_pairs={{0,1},{1,2},{2,3},{3,0},{4,5},{5,6},{6,7},{7,4},{8,9},{9,10},{10,1... | collective-permute-start | bytes 786440 | tf_op jit(solution)/shard_map/ppermute | solution.py:203
  116.8 13.6 %collective-permute-start.9 = (bf16[256,512]{1,0:T(8,128)(2,1)S(1)}, bf16[256,512]{1,0:T(8,128)(2,1)S(1)}, u32[]{:S(2)}, u32[]{:S(2)}) collective-permute-start(bf16[256,512]{1,0:T(8,128)(2,1)S(1)} %shard_map.75), channel_id=1, source_target_pairs={{0,3},{1,0},{2,1},{3,2},{4,7},{5,4},{6,5},{7,6},{8,11},{9,8},{10,9... | collective-permute-start | bytes 786440 | tf_op jit(solution)/shard_map/ppermute | solution.py:203
  124.6 8.8 %collective-permute-start.13 = (bf16[256,256]{1,0:T(8,128)(2,1)S(1)}, bf16[256,256]{1,0:T(8,128)(2,1)S(1)}, u32[]{:S(2)}, u32[]{:S(2)}) collective-permute-start(bf16[256,256]{1,0:T(8,128)(2,1)S(1)} %shard_map.76.refs_5_), channel_id=1, source_target_pairs={{0,2},{1,3},{2,0},{3,1},{4,6},{5,7},{6,4},{7,5},{8,10},{9,11},{10,... | collective-permute-start | bytes 393224 | tf_op jit(solution)/shard_map/ppermute | solution.py:203
  126.7 7.8 %collective-permute-start.14 = (bf16[256,256]{1,0:T(8,128)(2,1)S(1)}, bf16[256,256]{1,0:T(8,128)(2,1)S(1)}, u32[]{:S(2)}, u32[]{:S(2)}) collective-permute-start(bf16[256,256]{1,0:T(8,128)(2,1)S(1)} %shard_map.76.refs_5_), channel_id=1, source_target_pairs={{0,1},{1,2},{2,3},{3,0},{4,5},{5,6},{6,7},{7,4},{8,9},{9,10},{10,1... | collective-permute-start | bytes 393224 | tf_op jit(solution)/shard_map/ppermute | solution.py:203
  127.0 8.8 %collective-permute-start.15 = (bf16[256,256]{1,0:T(8,128)(2,1)S(1)}, bf16[256,256]{1,0:T(8,128)(2,1)S(1)}, u32[]{:S(2)}, u32[]{:S(2)}) collective-permute-start(bf16[256,256]{1,0:T(8,128)(2,1)S(1)} %shard_map.76.refs_5_), channel_id=1, source_target_pairs={{0,3},{1,0},{2,1},{3,2},{4,7},{5,4},{6,5},{7,6},{8,11},{9,8},{10,9... | collective-permute-start | bytes 393224 | tf_op jit(solution)/shard_map/ppermute | solution.py:203
  131.5 4.4 %collective-permute-start.12 = (bf16[256,512]{1,0:T(8,128)(2,1)S(1)}, bf16[256,512]{1,0:T(8,128)(2,1)S(1)}, u32[]{:S(2)}, u32[]{:S(2)}) collective-permute-start(bf16[256,512]{1,0:T(8,128)(2,1)S(1)} %add_convert_fusion.6.refs_0_), channel_id=1, source_target_pairs={{0,64},{64,0},{1,65},{65,1},{2,66},{66,2},{3,67},{67,3},{4,68},{68... | collective-permute-start | bytes 786440 | tf_op jit(solution)/shard_map/ppermute | solution.py:198
  133.3 2.6 %collective-permute-start.19 = (bf16[256,256]{1,0:T(8,128)(2,1)S(1)}, bf16[256,256]{1,0:T(8,128)(2,1)S(1)}, u32[]{:S(2)}, u32[]{:S(2)}) collective-permute-start(bf16[256,256]{1,0:T(8,128)(2,1)S(1)} %shard_map.76.refs_5_), channel_id=1, source_target_pairs={{0,64},{64,0},{1,65},{65,1},{2,66},{66,2},{3,67},{67,3},{4,68},{68... | collective-permute-start | bytes 393224 | tf_op jit(solution)/shard_map/ppermute | solution.py:198
  133.4 2.5 %collective-permute-start.16 = (bf16[256,256]{1,0:T(8,128)(2,1)S(1)}, bf16[256,256]{1,0:T(8,128)(2,1)S(1)}, u32[]{:S(2)}, u32[]{:S(2)}) collective-permute-start(bf16[256,256]{1,0:T(8,128)(2,1)S(1)} %collective-permute-done.13.refs_2_), channel_id=1, source_target_pairs={{0,64},{64,0},{1,65},{65,1},{2,66},{66,2},{3,67},{67,3},{4,68},{68... | collective-permute-start | bytes 393224 | tf_op jit(solution)/shard_map/ppermute | solution.py:198
  134.5 2.3 %collective-permute-start.17 = (bf16[256,256]{1,0:T(8,128)(2,1)S(1)}, bf16[256,256]{1,0:T(8,128)(2,1)S(1)}, u32[]{:S(2)}, u32[]{:S(2)}) collective-permute-start(bf16[256,256]{1,0:T(8,128)(2,1)S(1)} %collective-permute-done.14.refs_3_), channel_id=1, source_target_pairs={{0,64},{64,0},{1,65},{65,1},{2,66},{66,2},{3,67},{67,3},{4,68},{68... | collective-permute-start | bytes 393224 | tf_op jit(solution)/shard_map/ppermute | solution.py:198
  135.8 1.3 collective-permute-start.18
  (4 other events, 41.4 us)

commit v8 on v7

--- a/solution.py
+++ b/solution.py
@@ -15,7 +15,7 @@
 WIDE = 512
 THIN = 256
 Z_STEPS = (1, 3, 2, 0)
-TAIL_STEPS = (2, 1, 3, 0)
+TAIL_STEPS = (2, 3, 1, 0)
 EPSILON = 1e-05
 F32 = jnp.float32
 BF16 = jnp.bfloat16

time: 140 us -> 140 us (level)
  transfers between devices with their start and end apart: 22 -> 22, of which waited for: 7 -> 6; matrix products, arithmetic and copies ran while one was open for 15% -> 15% of each run, Pallas kernels for 1% -> 1%
where the time goes in v8:
time: 140 us; the launch traced here: 139 us
  blocking collectives  50.6 us (36%)
  starting transfers between devices  30.1 us (22%)
  matrix products  24 us (17%)
  waiting for transfers between devices  23.3 us (17%)
  Pallas kernels  7.82 us (6%)
  other arithmetic  2.35 us (2%)
    all_to_all x1, blocking collectives, to_experts(): lax.all_to_all(rows.reshape(EXPERTS, CAP, width), 'ep', split_axis=0, con...  50.6 us
    dot_general x12, matrix products, product(): return jnp.dot(rows, weight, preferred_element_type=F32)  24 us
    ppermute x9, waiting for transfers between devices, along_z(): lax.ppermute(values, 'dp', [(i, (i + step) % count) for i in range(count)])  16.6 us
    ppermute x9, starting transfers between devices, along_z(): lax.ppermute(values, 'dp', [(i, (i + step) % count) for i in range(count)])  13.1 us
    ppermute x11, starting transfers between devices, swap(): return lax.ppermute(values, 'pp', [(0, 1), (1, 0)])  8.77 us
    all_to_all x2, starting transfers between devices, to_experts(): lax.all_to_all(rows.reshape(EXPERTS, CAP, width), 'ep', split_axis=0, con...  8.25 us
    pallas_call x1, Pallas kernels, route(): pl.pallas_call(route_kernel, in_specs=[anywhere] * 4, out_specs=[anywhere...  4.78 us
    all_to_all x2, waiting for transfers between devices, to_experts(): lax.all_to_all(rows.reshape(EXPERTS, CAP, width), 'ep', split_axis=0, con...  4.59 us
  transfers between devices with their start and end apart: 22, of which 6 were waited for; matrix products, arithmetic and copies ran while one was open for 15% of the time, Pallas kernels for 1%

profile of v8, /device:TPU:1, one launch (start us, length us, event | category | flops | bytes accessed | tf_op | source)
XLA Modules:
  0.0 139.5 jit_solution(16156904808544141304)
XLA Ops:
  0.0 4.8 %shard_map.73 = (bf16[1152,1536]{1,0:T(8,128)(2,1)}, f32[256,16]{1,0:T(8,128)}, f32[256,16]{1,0:T(8,128)}) custom-call(bf16[256,3072]{1,0:T(8,128)(2,1)} %tok_hbm.1, f32[1,3072]{1,0:T(1,128)} %bitcast.80, bf16[16,3072]{1,0:T(8,128)(2,1)} %bitcast.79, s32[4,256]{1,0:T(4,128)} %bitcast.81), custom_call_target="tpu_custom_call" | custom-call | flops 905969664 | bytes 6000000 | tf_op jit(solution)/shard_map/pallas_call | solution.py:106
  4.8 50.6 %all_to_all.15 = bf16[16,72,1536]{2,1,0:T(8,128)(2,1)S(1)} all-to-all(bf16[16,72,1536]{2,1,0:T(8,128)(2,1)} %bitcast.74), channel_id=1, replica_groups=mesh['pp'=2,'ep'=16,'dp'=4] {'ep'}, dimensions={0} | all-to-all | bytes 7077888 | tf_op jit(solution)/shard_map/all_to_all | solution.py:208
  55.3 1.8 %collective-permute-start = (bf16[1152,1536]{1,0:T(8,128)(2,1)S(1)}, bf16[1152,1536]{1,0:T(8,128)(2,1)}, u32[]{:S(2)}, u32[]{:S(2)}) collective-permute-start(bf16[1152,1536]{1,0:T(8,128)(2,1)S(1)} %bitcast.72), channel_id=1, source_target_pairs={{0,64},{64,0},{1,65},{65,1},{2,66},{66,2},{3,67},{67,3},{4,68},{68... | collective-permute-start | bytes 10616840 | tf_op jit(solution)/shard_map/ppermute | solution.py:198
  57.2 4.7 %fusion.2 = f32[1152,768]{1,0:T(8,128)S(1)} fusion(bf16[1152,1536]{1,0:T(8,128)(2,1)S(1)} %bitcast.73, bf16[2,1536,768]{2,1,0:T(8,128)(2,1)} %bitcast.75, s32[]{:T(128)S(6)} %select_n.67), kind=kOutput, calls=%fused_computation.9 | convolution fusion | flops 2717908992 | bytes 9437188 | tf_op jit(solution)/shard_map/dot_general | solution.py:139
  61.9 1.2 collective-permute-done
  63.2 5.9 %multiply_convert_fusion = bf16[1152,768]{1,0:T(8,128)(2,1)S(1)} fusion(f32[1152,768]{1,0:T(8,128)S(1)} %fusion.2, bf16[1152,1536]{1,0:T(8,128)(2,1)} %collective-permute-done, bf16[2,1536,768]{2,1,0:T(8,128)(2,1)} %bitcast.76, s32[]{:T(128)S(6)} %select_n.68), kind=kOutput, calls=%fused_computation.2 | convolution fusion | flops 2722332672 | bytes 11206660 | tf_op jit(solution)/shard_map/dot_general | solution.py:139
  73.7 1.5 %convolution_convert_fusion.4 = bf16[1152,256]{1,0:T(8,128)(2,1)} fusion(bf16[1152,768]{1,0:T(8,128)(2,1)S(1)} %multiply_convert_fusion, bf16[1,768,3072]{2,1,0:T(8,128)(2,1)S(1)} %bitcast.78, s32[]{:T(128)S(6)} %select_n.72), kind=kOutput, calls=%fused_computation.7 | convolution fusion | flops 453279744 | bytes 2752516 | tf_op jit(solution)/shard_map/dot_general | solution.py:139
  75.5 1.5 %add_convert_fusion.2 = bf16[1152,256]{1,0:T(8,128)(2,1)} fusion(bf16[1152,256]{1,0:T(8,128)(2,1)S(1)} %collective-permute-done.7, bf16[1152,768]{1,0:T(8,128)(2,1)S(1)} %multiply_convert_fusion, bf16[1,768,3072]{2,1,0:T(8,128)(2,1)S(1)} %bitcast.78, s32[]{:T(128)S(6)} %select_n.80), kind=kOutput, calls=%fused_computation.15 | convolution fusion | flops 453869568 | bytes 3342340 | tf_op jit(solution)/shard_map/dot_general | solution.py:139
  77.0 3.6 %collective-permute-start.8 = (bf16[1152,256]{1,0:T(8,128)(2,1)}, bf16[1152,256]{1,0:T(8,128)(2,1)S(1)}, u32[]{:S(2)}, u32[]{:S(2)}) collective-permute-start(bf16[1152,256]{1,0:T(8,128)(2,1)} %add_convert_fusion.2), channel_id=1, source_target_pairs={{0,2},{1,3},{2,0},{3,1},{4,6},{5,7},{6,4},{7,5},{8,10},{9,11},{10,... | collective-permute-start | bytes 1769480 | tf_op jit(solution)/shard_map/ppermute | solution.py:203
  80.6 1.5 %add_convert_fusion.3 = bf16[1152,256]{1,0:T(8,128)(2,1)} fusion(bf16[1152,256]{1,0:T(8,128)(2,1)S(1)} %collective-permute-done.5, bf16[1152,768]{1,0:T(8,128)(2,1)S(1)} %multiply_convert_fusion, bf16[1,768,3072]{2,1,0:T(8,128)(2,1)S(1)} %bitcast.78, s32[]{:T(128)S(6)} %select_n.77), kind=kOutput, calls=%fused_computation.16 | convolution fusion | flops 453869568 | bytes 3342340 | tf_op jit(solution)/shard_map/dot_general | solution.py:139
  82.5 1.5 %add_convert_fusion.4 = bf16[1152,256]{1,0:T(8,128)(2,1)} fusion(bf16[1152,256]{1,0:T(8,128)(2,1)S(1)} %collective-permute-done.3, bf16[1152,768]{1,0:T(8,128)(2,1)S(1)} %multiply_convert_fusion, bf16[1,768,3072]{2,1,0:T(8,128)(2,1)S(1)} %bitcast.78, s32[]{:T(128)S(6)} %select_n.74), kind=kOutput, calls=%fused_computation.17 | convolution fusion | flops 453869568 | bytes 3342340 | tf_op jit(solution)/shard_map/dot_general | solution.py:139
  85.0 2.1 %add_convert_fusion = bf16[1152,512]{1,0:T(8,128)(2,1)} fusion(bf16[1152,512]{1,0:T(8,128)(2,1)S(1)} %collective-permute-done.1, bf16[1152,768]{1,0:T(8,128)(2,1)S(1)} %multiply_convert_fusion, bf16[1,768,3072]{2,1,0:T(8,128)(2,1)S(1)} %bitcast.78, s32[]{:T(128)S(6)} %select_n.66), kind=kOutput, calls=%fused_computation.11 | convolution fusion | flops 907739136 | bytes 4915204 | tf_op jit(solution)/shard_map/dot_general | solution.py:139
  87.2 3.7 %all-to-all-start.1 = ((bf16[16,72,512]{2,1,0:T(8,128)(2,1)}), bf16[16,72,512]{2,1,0:T(8,128)(2,1)S(1)}, u32[]{:S(2)}, u32[]{:S(2)}) async-start(bf16[16,72,512]{2,1,0:T(8,128)(2,1)} %bitcast.12), calls=%async_computation.1 | async-start | bytes 2359296 | tf_op jit(solution)/shard_map/all_to_all | solution.py:208
  90.9 2.4 %add_convert_fusion.5 = bf16[1152,256]{1,0:T(8,128)(2,1)S(1)} fusion(bf16[1152,256]{1,0:T(8,128)(2,1)} %collective-permute-done.2, bf16[1152,768]{1,0:T(8,128)(2,1)} %copy-done.3, bf16[1,768,3072]{2,1,0:T(8,128)(2,1)} %param.12, s32[]{:T(128)S(6)} %select_n.71), kind=kOutput, calls=%fused_computation.18 | convolution fusion | flops 453869568 | bytes 3342340 | tf_op jit(solution)/shard_map/dot_general | solution.py:139
  94.5 13.1 %collective-permute-done.6 = bf16[1152,256]{1,0:T(8,128)(2,1)S(1)} collective-permute-done((bf16[1152,256]{1,0:T(8,128)(2,1)}, bf16[1152,256]{1,0:T(8,128)(2,1)S(1)}, u32[]{:S(2)}, u32[]{:S(2)}) %collective-permute-start.6) | collective-permute-done | bytes 589856 | tf_op jit(solution)/shard_map/ppermute | solution.py:203
  108.7 4.6 %all-to-all-start.2 = ((bf16[16,72,256]{2,1,0:T(8,128)(2,1)}), bf16[16,72,256]{2,1,0:T(8,128)(2,1)S(1)}, u32[]{:S(2)}, u32[]{:S(2)}) async-start(bf16[16,72,256]{2,1,0:T(8,128)(2,1)} %bitcast.22), calls=%async_computation.2 | async-start | bytes 1179648 | tf_op jit(solution)/shard_map/all_to_all | solution.py:208
  114.3 1.8 %collective-permute-start.11 = (bf16[256,512]{1,0:T(8,128)(2,1)S(1)}, bf16[256,512]{1,0:T(8,128)(2,1)S(1)}, u32[]{:S(2)}, u32[]{:S(2)}) collective-permute-start(bf16[256,512]{1,0:T(8,128)(2,1)S(1)} %shard_map.75), channel_id=1, source_target_pairs={{0,2},{1,3},{2,0},{3,1},{4,6},{5,7},{6,4},{7,5},{8,10},{9,11},{10,... | collective-permute-start | bytes 786440 | tf_op jit(solution)/shard_map/ppermute | solution.py:203
  116.8 2.0 %collective-permute-start.9 = (bf16[256,512]{1,0:T(8,128)(2,1)S(1)}, bf16[256,512]{1,0:T(8,128)(2,1)S(1)}, u32[]{:S(2)}, u32[]{:S(2)}) collective-permute-start(bf16[256,512]{1,0:T(8,128)(2,1)S(1)} %shard_map.75), channel_id=1, source_target_pairs={{0,3},{1,0},{2,1},{3,2},{4,7},{5,4},{6,5},{7,6},{8,11},{9,8},{10,9... | collective-permute-start | bytes 786440 | tf_op jit(solution)/shard_map/ppermute | solution.py:203
  119.7 4.6 %all-to-all-done.2 = bf16[16,72,256]{2,1,0:T(8,128)(2,1)S(1)} async-done(((bf16[16,72,256]{2,1,0:T(8,128)(2,1)}), bf16[16,72,256]{2,1,0:T(8,128)(2,1)S(1)}, u32[]{:S(2)}, u32[]{:S(2)}) %all-to-all-start.2) | async-done | bytes 589856 | tf_op jit(solution)/shard_map/all_to_all | solution.py:208
  124.6 2.1 %collective-permute-start.13 = (bf16[256,256]{1,0:T(8,128)(2,1)S(1)}, bf16[256,256]{1,0:T(8,128)(2,1)S(1)}, u32[]{:S(2)}, u32[]{:S(2)}) collective-permute-start(bf16[256,256]{1,0:T(8,128)(2,1)S(1)} %shard_map.76.refs_5_), channel_id=1, source_target_pairs={{0,2},{1,3},{2,0},{3,1},{4,6},{5,7},{6,4},{7,5},{8,10},{9,11},{10,... | collective-permute-start | bytes 393224 | tf_op jit(solution)/shard_map/ppermute | solution.py:203
  128.1 2.3 %collective-permute-done.10 = bf16[256,512]{1,0:T(8,128)(2,1)S(1)} collective-permute-done((bf16[256,512]{1,0:T(8,128)(2,1)S(1)}, bf16[256,512]{1,0:T(8,128)(2,1)S(1)}, u32[]{:S(2)}, u32[]{:S(2)}) %collective-permute-start.10) | collective-permute-done | bytes 262176 | tf_op jit(solution)/shard_map/ppermute | solution.py:203
  132.3 2.2 %collective-permute-start.16 = (bf16[256,256]{1,0:T(8,128)(2,1)S(1)}, bf16[256,256]{1,0:T(8,128)(2,1)S(1)}, u32[]{:S(2)}, u32[]{:S(2)}) collective-permute-start(bf16[256,256]{1,0:T(8,128)(2,1)S(1)} %collective-permute-done.13.refs_2_), channel_id=1, source_target_pairs={{0,64},{64,0},{1,65},{65,1},{2,66},{66,2},{3,67},{67,3},{4,68},{68... | collective-permute-start | bytes 393224 | tf_op jit(solution)/shard_map/ppermute | solution.py:198
  135.3 1.3 collective-permute-start.18
  137.6 1.8 %shard_map.77 = bf16[256,3072]{1,0:T(8,128)(2,1)} custom-call(s32[10]{0:T(128)S(1)} %pad_add_fusion.at_ref, bf16[256,512]{1,0:T(8,128)(2,1)S(1)} %add_convert_fusion.6.refs_0_, bf16[256,512]{1,0:T(8,128)(2,1)S(1)} %collective-permute-done.12.refs_1_, bf16[256,256]{1,0:T(8,128)(2,1)S(1)} %collective-permute-done.13.refs_2_, ...), custom_call_target="tpu_custom_call" | custom-call | bytes 3000000 | tf_op jit(solution)/shard_map/pallas_call | solution.py:186
  (57 shorter events, 16.7 us)
Async XLA Ops:
  55.3 7.8 %collective-permute-start = (bf16[1152,1536]{1,0:T(8,128)(2,1)S(1)}, bf16[1152,1536]{1,0:T(8,128)(2,1)}, u32[]{:S(2)}, u32[]{:S(2)}) collective-permute-start(bf16[1152,1536]{1,0:T(8,128)(2,1)S(1)} %bitcast.72), channel_id=1, source_target_pairs={{0,64},{64,0},{1,65},{65,1},{2,66},{66,2},{3,67},{67,3},{4,68},{68... | collective-permute-start | bytes 10616840 | tf_op jit(solution)/shard_map/ppermute | solution.py:198
  70.2 14.8 %collective-permute-start.1 = (bf16[1152,512]{1,0:T(8,128)(2,1)S(1)}, bf16[1152,512]{1,0:T(8,128)(2,1)S(1)}, u32[]{:S(2)}, u32[]{:S(2)}) collective-permute-start(bf16[1152,512]{1,0:T(8,128)(2,1)S(1)} %convolution_convert_fusion), channel_id=1, source_target_pairs={{0,64},{64,0},{1,65},{65,1},{2,66},{66,2},{3,67},{67,3},{4,68},{68... | collective-permute-start | bytes 3538952 | tf_op jit(solution)/shard_map/ppermute | solution.py:198
  71.3 4.2 %collective-permute-start.7 = (bf16[1152,256]{1,0:T(8,128)(2,1)S(1)}, bf16[1152,256]{1,0:T(8,128)(2,1)S(1)}, u32[]{:S(2)}, u32[]{:S(2)}) collective-permute-start(bf16[1152,256]{1,0:T(8,128)(2,1)S(1)} %convolution_convert_fusion.1), channel_id=1, source_target_pairs={{0,64},{64,0},{1,65},{65,1},{2,66},{66,2},{3,67},{67,3},{4,68},{68... | collective-permute-start | bytes 1769480 | tf_op jit(solution)/shard_map/ppermute | solution.py:198
  72.2 8.5 %collective-permute-start.5 = (bf16[1152,256]{1,0:T(8,128)(2,1)S(1)}, bf16[1152,256]{1,0:T(8,128)(2,1)S(1)}, u32[]{:S(2)}, u32[]{:S(2)}) collective-permute-start(bf16[1152,256]{1,0:T(8,128)(2,1)S(1)} %convolution_convert_fusion.2), channel_id=1, source_target_pairs={{0,64},{64,0},{1,65},{65,1},{2,66},{66,2},{3,67},{67,3},{4,68},{68... | collective-permute-start | bytes 1769480 | tf_op jit(solution)/shard_map/ppermute | solution.py:198
  73.3 9.2 %collective-permute-start.3 = (bf16[1152,256]{1,0:T(8,128)(2,1)S(1)}, bf16[1152,256]{1,0:T(8,128)(2,1)S(1)}, u32[]{:S(2)}, u32[]{:S(2)}) collective-permute-start(bf16[1152,256]{1,0:T(8,128)(2,1)S(1)} %convolution_convert_fusion.3), channel_id=1, source_target_pairs={{0,64},{64,0},{1,65},{65,1},{2,66},{66,2},{3,67},{67,3},{4,68},{68... | collective-permute-start | bytes 1769480 | tf_op jit(solution)/shard_map/ppermute | solution.py:198
  75.1 15.7 %collective-permute-start.2 = (bf16[1152,256]{1,0:T(8,128)(2,1)}, bf16[1152,256]{1,0:T(8,128)(2,1)}, u32[]{:S(2)}, u32[]{:S(2)}) collective-permute-start(bf16[1152,256]{1,0:T(8,128)(2,1)} %convolution_convert_fusion.4), channel_id=1, source_target_pairs={{0,64},{64,0},{1,65},{65,1},{2,66},{66,2},{3,67},{67,3},{4,68},{68... | collective-permute-start | bytes 1769480 | tf_op jit(solution)/shard_map/ppermute | solution.py:198
  77.0 17.5 %collective-permute-start.8 = (bf16[1152,256]{1,0:T(8,128)(2,1)}, bf16[1152,256]{1,0:T(8,128)(2,1)S(1)}, u32[]{:S(2)}, u32[]{:S(2)}) collective-permute-start(bf16[1152,256]{1,0:T(8,128)(2,1)} %add_convert_fusion.2), channel_id=1, source_target_pairs={{0,2},{1,3},{2,0},{3,1},{4,6},{5,7},{6,4},{7,5},{8,10},{9,11},{10,... | collective-permute-start | bytes 1769480 | tf_op jit(solution)/shard_map/ppermute | solution.py:203
  82.1 25.4 %collective-permute-start.6 = (bf16[1152,256]{1,0:T(8,128)(2,1)}, bf16[1152,256]{1,0:T(8,128)(2,1)S(1)}, u32[]{:S(2)}, u32[]{:S(2)}) collective-permute-start(bf16[1152,256]{1,0:T(8,128)(2,1)} %add_convert_fusion.3), channel_id=1, source_target_pairs={{0,3},{1,0},{2,1},{3,2},{4,7},{5,4},{6,5},{7,6},{8,11},{9,8},{10,9... | collective-permute-start | bytes 1769480 | tf_op jit(solution)/shard_map/ppermute | solution.py:203
  83.9 23.6 %collective-permute-start.4 = (bf16[1152,256]{1,0:T(8,128)(2,1)}, bf16[1152,256]{1,0:T(8,128)(2,1)S(1)}, u32[]{:S(2)}, u32[]{:S(2)}) collective-permute-start(bf16[1152,256]{1,0:T(8,128)(2,1)} %add_convert_fusion.4), channel_id=1, source_target_pairs={{0,1},{1,2},{2,3},{3,0},{4,5},{5,6},{6,7},{7,4},{8,9},{9,10},{10,1... | collective-permute-start | bytes 1769480 | tf_op jit(solution)/shard_map/ppermute | solution.py:203
  87.2 21.5 %all-to-all-start.1 = ((bf16[16,72,512]{2,1,0:T(8,128)(2,1)}), bf16[16,72,512]{2,1,0:T(8,128)(2,1)S(1)}, u32[]{:S(2)}, u32[]{:S(2)}) async-start(bf16[16,72,512]{2,1,0:T(8,128)(2,1)} %bitcast.12), calls=%async_computation.1 | async-start | bytes 2359296 | tf_op jit(solution)/shard_map/all_to_all | solution.py:208
  93.2 20.0 %copy-start = (f32[256,16]{1,0:T(8,128)S(1)}, f32[256,16]{1,0:T(8,128)}, u32[]{:S(2)}) copy-start(f32[256,16]{1,0:T(8,128)} %get-tuple-element.15.key_ref) | copy-start | bytes 49156
  93.3 20.0 %copy-start.1 = (f32[256,16]{1,0:T(8,128)S(1)}, f32[256,16]{1,0:T(8,128)}, u32[]{:S(2)}) copy-start(f32[256,16]{1,0:T(8,128)} %get-tuple-element.16.gate_ref) | copy-start | bytes 49156
  108.7 15.6 %all-to-all-start.2 = ((bf16[16,72,256]{2,1,0:T(8,128)(2,1)}), bf16[16,72,256]{2,1,0:T(8,128)(2,1)S(1)}, u32[]{:S(2)}, u32[]{:S(2)}) async-start(bf16[16,72,256]{2,1,0:T(8,128)(2,1)} %bitcast.22), calls=%async_computation.2 | async-start | bytes 1179648 | tf_op jit(solution)/shard_map/all_to_all | solution.py:208
  114.3 13.3 %collective-permute-start.11 = (bf16[256,512]{1,0:T(8,128)(2,1)S(1)}, bf16[256,512]{1,0:T(8,128)(2,1)S(1)}, u32[]{:S(2)}, u32[]{:S(2)}) collective-permute-start(bf16[256,512]{1,0:T(8,128)(2,1)S(1)} %shard_map.75), channel_id=1, source_target_pairs={{0,2},{1,3},{2,0},{3,1},{4,6},{5,7},{6,4},{7,5},{8,10},{9,11},{10,... | collective-permute-start | bytes 786440 | tf_op jit(solution)/shard_map/ppermute | solution.py:203
  116.1 14.3 %collective-permute-start.10 = (bf16[256,512]{1,0:T(8,128)(2,1)S(1)}, bf16[256,512]{1,0:T(8,128)(2,1)S(1)}, u32[]{:S(2)}, u32[]{:S(2)}) collective-permute-start(bf16[256,512]{1,0:T(8,128)(2,1)S(1)} %shard_map.75), channel_id=1, source_target_pairs={{0,1},{1,2},{2,3},{3,0},{4,5},{5,6},{6,7},{7,4},{8,9},{9,10},{10,1... | collective-permute-start | bytes 786440 | tf_op jit(solution)/shard_map/ppermute | solution.py:203
  116.8 13.6 %collective-permute-start.9 = (bf16[256,512]{1,0:T(8,128)(2,1)S(1)}, bf16[256,512]{1,0:T(8,128)(2,1)S(1)}, u32[]{:S(2)}, u32[]{:S(2)}) collective-permute-start(bf16[256,512]{1,0:T(8,128)(2,1)S(1)} %shard_map.75), channel_id=1, source_target_pairs={{0,3},{1,0},{2,1},{3,2},{4,7},{5,4},{6,5},{7,6},{8,11},{9,8},{10,9... | collective-permute-start | bytes 786440 | tf_op jit(solution)/shard_map/ppermute | solution.py:203
  124.6 7.7 %collective-permute-start.13 = (bf16[256,256]{1,0:T(8,128)(2,1)S(1)}, bf16[256,256]{1,0:T(8,128)(2,1)S(1)}, u32[]{:S(2)}, u32[]{:S(2)}) collective-permute-start(bf16[256,256]{1,0:T(8,128)(2,1)S(1)} %shard_map.76.refs_5_), channel_id=1, source_target_pairs={{0,2},{1,3},{2,0},{3,1},{4,6},{5,7},{6,4},{7,5},{8,10},{9,11},{10,... | collective-permute-start | bytes 393224 | tf_op jit(solution)/shard_map/ppermute | solution.py:203
  126.7 7.9 %collective-permute-start.14 = (bf16[256,256]{1,0:T(8,128)(2,1)S(1)}, bf16[256,256]{1,0:T(8,128)(2,1)S(1)}, u32[]{:S(2)}, u32[]{:S(2)}) collective-permute-start(bf16[256,256]{1,0:T(8,128)(2,1)S(1)} %shard_map.76.refs_5_), channel_id=1, source_target_pairs={{0,3},{1,0},{2,1},{3,2},{4,7},{5,4},{6,5},{7,6},{8,11},{9,8},{10,9... | collective-permute-start | bytes 393224 | tf_op jit(solution)/shard_map/ppermute | solution.py:203
  127.6 7.7 %collective-permute-start.15 = (bf16[256,256]{1,0:T(8,128)(2,1)S(1)}, bf16[256,256]{1,0:T(8,128)(2,1)S(1)}, u32[]{:S(2)}, u32[]{:S(2)}) collective-permute-start(bf16[256,256]{1,0:T(8,128)(2,1)S(1)} %shard_map.76.refs_5_), channel_id=1, source_target_pairs={{0,1},{1,2},{2,3},{3,0},{4,5},{5,6},{6,7},{7,4},{8,9},{9,10},{10,1... | collective-permute-start | bytes 393224 | tf_op jit(solution)/shard_map/ppermute | solution.py:203
  131.5 5.1 %collective-permute-start.12 = (bf16[256,512]{1,0:T(8,128)(2,1)S(1)}, bf16[256,512]{1,0:T(8,128)(2,1)S(1)}, u32[]{:S(2)}, u32[]{:S(2)}) collective-permute-start(bf16[256,512]{1,0:T(8,128)(2,1)S(1)} %add_convert_fusion.6.refs_0_), channel_id=1, source_target_pairs={{0,64},{64,0},{1,65},{65,1},{2,66},{66,2},{3,67},{67,3},{4,68},{68... | collective-permute-start | bytes 786440 | tf_op jit(solution)/shard_map/ppermute | solution.py:198
  132.2 4.5 %collective-permute-start.19 = (bf16[256,256]{1,0:T(8,128)(2,1)S(1)}, bf16[256,256]{1,0:T(8,128)(2,1)S(1)}, u32[]{:S(2)}, u32[]{:S(2)}) collective-permute-start(bf16[256,256]{1,0:T(8,128)(2,1)S(1)} %shard_map.76.refs_5_), channel_id=1, source_target_pairs={{0,64},{64,0},{1,65},{65,1},{2,66},{66,2},{3,67},{67,3},{4,68},{68... | collective-permute-start | bytes 393224 | tf_op jit(solution)/shard_map/ppermute | solution.py:198
  132.3 4.4 %collective-permute-start.16 = (bf16[256,256]{1,0:T(8,128)(2,1)S(1)}, bf16[256,256]{1,0:T(8,128)(2,1)S(1)}, u32[]{:S(2)}, u32[]{:S(2)}) collective-permute-start(bf16[256,256]{1,0:T(8,128)(2,1)S(1)} %collective-permute-done.13.refs_2_), channel_id=1, source_target_pairs={{0,64},{64,0},{1,65},{65,1},{2,66},{66,2},{3,67},{67,3},{4,68},{68... | collective-permute-start | bytes 393224 | tf_op jit(solution)/shard_map/ppermute | solution.py:198
  134.5 2.1 %collective-permute-start.17 = (bf16[256,256]{1,0:T(8,128)(2,1)S(1)}, bf16[256,256]{1,0:T(8,128)(2,1)S(1)}, u32[]{:S(2)}, u32[]{:S(2)}) collective-permute-start(bf16[256,256]{1,0:T(8,128)(2,1)S(1)} %collective-permute-done.14.refs_3_), channel_id=1, source_target_pairs={{0,64},{64,0},{1,65},{65,1},{2,66},{66,2},{3,67},{67,3},{4,68},{68... | collective-permute-start | bytes 393224 | tf_op jit(solution)/shard_map/ppermute | solution.py:198
  135.3 2.3 %collective-permute-start.18 = (bf16[256,256]{1,0:T(8,128)(2,1)S(1)}, bf16[256,256]{1,0:T(8,128)(2,1)S(1)}, u32[]{:S(2)}, u32[]{:S(2)}) collective-permute-start(bf16[256,256]{1,0:T(8,128)(2,1)S(1)} %collective-permute-done.15.refs_4_), channel_id=1, source_target_pairs={{0,64},{64,0},{1,65},{65,1},{2,66},{66,2},{3,67},{67,3},{4,68},{68... | collective-permute-start | bytes 393224 | tf_op jit(solution)/shard_map/ppermute | solution.py:198
  (4 other events, 41.4 us)
